TPU v7x, 32 devices: a whole 2x2x4 slice. The times are simulated.
32 devices in a mesh: fsdp: 4 (over z), rep: 8 (over y, x, core).
Axes of the slice: x: 2, y: 2, z: 4, core: 2. Of those that a mesh axis runs over, the one named last changes fastest.
Arguments:
- tokens: bfloat16 [8, 2048, 768], P('rep', 'fsdp'), may hold values from -6 to 6
- attention_gain: bfloat16 [768], P('fsdp'), may hold values from 0.25 to 1.75
- projection_in: bfloat16 [768, 2304], P('fsdp'), may hold values from -0.21875 to 0.21875
- attention_out: bfloat16 [768, 768], P('fsdp'), may hold values from -6 to 6
- feedforward_gain: bfloat16 [768], P('fsdp'), may hold values from 0.25 to 1.75
- expansion: bfloat16 [768, 2304], P('fsdp'), may hold values from -0.21875 to 0.21875
- contraction: bfloat16 [1152, 768], P('fsdp'), may hold values from -0.1875 to 0.1875
- cotangent: bfloat16 [8, 2048, 768], P('rep', 'fsdp'), may hold values from -6 to 6
Outputs:
- block_output: bfloat16 [8, 2048, 768], P('rep', 'fsdp')
- token_grad: float32 [8, 2048, 768], P('rep', 'fsdp')
- attention_gain_grad: float32 [768], P('fsdp')
- projection_in_grad: float32 [768, 2304], P('fsdp')
- attention_out_grad: float32 [768, 768], P('fsdp')
- feedforward_gain_grad: float32 [768], P('fsdp')
- expansion_grad: float32 [768, 2304], P('fsdp')
- contraction_grad: float32 [1152, 768], P('fsdp')
All inputs are finite; a program needn't handle non-finite values.
Results may differ from a plain program's by a relative error of at most 0.018.
Values may be sent and summed in bfloat16 or wider, within the bound.
No kernel may reach another device: no remote copies, remote signals or barrier semaphores. Data moves between devices by JAX's collectives and lax.ppermute only.
A program may use at most 128 MiB of HBM per device.

v0:
```python
import math

import jax
import jax.numpy as jnp
from jax import lax
from jax.sharding import PartitionSpec as P

HEADS = 12
HEAD_DIM = 64


EPS = 1e-05
THETA = 160000.0


def layer_norm(values, gain):
    centre = values - jnp.mean(values, axis=-1, keepdims=True)
    spread = jnp.mean(centre * centre, axis=-1, keepdims=True)
    return centre * lax.rsqrt(spread + EPS) * gain


def rotary_tables(count, offset):
    half = HEAD_DIM // 2
    freqs = THETA ** (-(jnp.arange(half, dtype=jnp.float32) * (2.0 / HEAD_DIM)))
    places = (offset + jnp.arange(count, dtype=jnp.int32)).astype(jnp.float32)
    angles = places[:, None] * freqs[None, :]
    return (jnp.cos(angles), jnp.sin(angles))


def rotate(values, cosine, sine):
    count = values.shape[0]
    half = HEAD_DIM // 2
    shaped = values.reshape(count, -1, HEAD_DIM)
    first = shaped[..., :half]
    second = shaped[..., half:]
    cos_three = cosine[:, None, :]
    sin_three = sine[:, None, :]
    turned = jnp.concatenate(
        [first * cos_three - second * sin_three, second * cos_three + first * sin_three], axis=-1
    )
    return turned.reshape(count, -1)


def geglu(inner):
    width = inner.shape[-1] // 2
    return jax.nn.gelu(inner[:, :width], approximate=False) * inner[:, width:]


def heads_first(values):
    return values.reshape(values.shape[0], HEADS, HEAD_DIM).transpose(1, 0, 2)


def rows_first(values):
    return values.transpose(1, 0, 2).reshape(values.shape[1], -1)


def rounded(values):
    return lax.optimization_barrier(values.astype(jnp.bfloat16)).astype(jnp.float32)


def attend_head(parts):
    queries, keys, values = parts
    scale = 1.0 / math.sqrt(HEAD_DIM)
    scores = jnp.einsum("qd,kd->qk", queries, keys, preferred_element_type=jnp.float32) * scale
    highest = jnp.max(scores, axis=-1, keepdims=True)
    raised = jnp.exp(scores - highest)
    total = jnp.sum(raised, axis=-1, keepdims=True)
    chances = raised / total
    mixed = jnp.dot(chances.astype(jnp.bfloat16), values, preferred_element_type=jnp.float32)
    return (mixed, (highest + jnp.log(total))[:, 0])


def attend_back(parts):
    queries, keys, values, upstream, log_total = parts
    scale = 1.0 / math.sqrt(HEAD_DIM)
    scores = jnp.einsum("qd,kd->qk", queries, keys, preferred_element_type=jnp.float32) * scale
    chances = jnp.exp(scores - log_total[:, None])
    prob_back = jnp.einsum("qd,kd->qk", upstream, values, preferred_element_type=jnp.float32)
    inner_sum = jnp.sum(prob_back * chances, axis=-1, keepdims=True)
    score_back = (chances * (prob_back - inner_sum)).astype(jnp.bfloat16)
    query_back = jnp.dot(score_back, keys, preferred_element_type=jnp.float32) * scale
    key_back = (
        jnp.einsum("qk,qd->kd", score_back, queries, preferred_element_type=jnp.float32) * scale
    )
    value_back = jnp.einsum(
        "qk,qd->kd", chances.astype(jnp.bfloat16), upstream, preferred_element_type=jnp.float32
    )
    return (query_back, key_back, value_back)


def local(
    tokens,
    attention_gain,
    projection_in,
    attention_out,
    feedforward_gain,
    expansion,
    contraction,
    cotangent,
):
    gathered = (
        lax.all_gather(attention_gain, "fsdp", axis=0, tiled=True),
        lax.all_gather(projection_in, "fsdp", axis=0, tiled=True),
        lax.all_gather(attention_out, "fsdp", axis=0, tiled=True),
        lax.all_gather(feedforward_gain, "fsdp", axis=0, tiled=True),
        lax.all_gather(expansion, "fsdp", axis=0, tiled=True),
        lax.all_gather(contraction, "fsdp", axis=0, tiled=True),
    )
    gain_one = gathered[0].astype(jnp.float32)
    gain_two = gathered[3].astype(jnp.float32)
    count = tokens.shape[1]
    width = tokens.shape[2]
    cosine, sine = rotary_tables(count, lax.axis_index("fsdp") * count)
    inputs = tokens[0].astype(jnp.float32)
    normed, norm_back = jax.vjp(layer_norm, inputs, gain_one)
    normed_low = normed.astype(jnp.bfloat16)
    projected = jnp.dot(normed_low, gathered[1], preferred_element_type=jnp.float32)
    turned, turn_back = jax.vjp(lambda part: rotate(part, cosine, sine), projected[:, : 2 * width])
    queries = turned[:, :width].astype(jnp.bfloat16)
    own_keys = turned[:, width:].astype(jnp.bfloat16)
    own_values = projected[:, 2 * width :].astype(jnp.bfloat16)
    all_keys, all_values = (
        lax.all_gather(own_keys, "fsdp", axis=0, tiled=True),
        lax.all_gather(own_values, "fsdp", axis=0, tiled=True),
    )
    head_queries = heads_first(queries)
    head_keys = heads_first(all_keys)
    head_values = heads_first(all_values)
    head_mixed, log_totals = lax.map(attend_head, (head_queries, head_keys, head_values))
    merged = rows_first(head_mixed).astype(jnp.bfloat16)
    state = inputs + jnp.dot(merged, gathered[2], preferred_element_type=jnp.float32)
    normed_two, norm_two_back = jax.vjp(layer_norm, state, gain_two)
    normed_two_low = normed_two.astype(jnp.bfloat16)
    inner = jnp.dot(normed_two_low, gathered[4], preferred_element_type=jnp.float32)
    active, glu_back = jax.vjp(geglu, inner)
    active_low = active.astype(jnp.bfloat16)
    result = state + jnp.dot(active_low, gathered[5], preferred_element_type=jnp.float32)
    block_output = result.astype(jnp.bfloat16)[None]
    again = (
        lax.all_gather(attention_gain, "fsdp", axis=0, tiled=True),
        lax.all_gather(projection_in, "fsdp", axis=0, tiled=True),
        lax.all_gather(attention_out, "fsdp", axis=0, tiled=True),
        lax.all_gather(feedforward_gain, "fsdp", axis=0, tiled=True),
        lax.all_gather(expansion, "fsdp", axis=0, tiled=True),
        lax.all_gather(contraction, "fsdp", axis=0, tiled=True),
    )
    upstream = cotangent[0]
    contraction_grad = jnp.einsum(
        "tf,td->fd", active_low, upstream, preferred_element_type=jnp.float32
    )
    active_back = jnp.einsum("td,fd->tf", upstream, again[5], preferred_element_type=jnp.float32)
    (inner_back,) = glu_back(rounded(active_back))
    inner_low = inner_back.astype(jnp.bfloat16)
    expansion_grad = jnp.einsum(
        "td,tf->df", normed_two_low, inner_low, preferred_element_type=jnp.float32
    )
    normed_two_back = jnp.einsum(
        "tf,df->td", inner_low, again[4], preferred_element_type=jnp.float32
    )
    state_part, gain_two_grad = norm_two_back(normed_two_back)
    state_back = upstream.astype(jnp.float32) + state_part
    state_low = state_back.astype(jnp.bfloat16)
    attention_out_grad = jnp.einsum(
        "te,td->ed", merged, state_low, preferred_element_type=jnp.float32
    )
    merged_back = jnp.einsum(
        "td,ed->te", state_low, again[2], preferred_element_type=jnp.float32
    ).astype(jnp.bfloat16)
    head_upstream = heads_first(merged_back)
    query_backs, key_backs, value_backs = lax.map(
        attend_back, (head_queries, head_keys, head_values, head_upstream, log_totals)
    )
    key_sum, value_sum = (
        lax.psum_scatter(
            rows_first(key_backs).astype(jnp.bfloat16), "fsdp", scatter_dimension=0, tiled=True
        ).astype(jnp.float32),
        lax.psum_scatter(
            rows_first(value_backs).astype(jnp.bfloat16), "fsdp", scatter_dimension=0, tiled=True
        ).astype(jnp.float32),
    )
    query_sum = rows_first(query_backs)
    (turn_grad,) = turn_back(jnp.concatenate([query_sum, key_sum], axis=1))
    projected_back = jnp.concatenate([turn_grad, value_sum], axis=1).astype(jnp.bfloat16)
    projection_grad = jnp.einsum(
        "td,te->de", normed_low, projected_back, preferred_element_type=jnp.float32
    )
    normed_back = jnp.einsum(
        "te,de->td", projected_back, again[1], preferred_element_type=jnp.float32
    )
    input_part, gain_one_grad = norm_back(normed_back)
    token_grad = (state_back + input_part)[None]
    owned = (
        lax.psum_scatter(
            gain_one_grad.astype(jnp.bfloat16), "fsdp", scatter_dimension=0, tiled=True
        ).astype(jnp.float32),
        lax.psum_scatter(
            projection_grad.astype(jnp.bfloat16), "fsdp", scatter_dimension=0, tiled=True
        ).astype(jnp.float32),
        lax.psum_scatter(
            attention_out_grad.astype(jnp.bfloat16), "fsdp", scatter_dimension=0, tiled=True
        ).astype(jnp.float32),
        lax.psum_scatter(
            gain_two_grad.astype(jnp.bfloat16), "fsdp", scatter_dimension=0, tiled=True
        ).astype(jnp.float32),
        lax.psum_scatter(
            expansion_grad.astype(jnp.bfloat16), "fsdp", scatter_dimension=0, tiled=True
        ).astype(jnp.float32),
        lax.psum_scatter(
            contraction_grad.astype(jnp.bfloat16), "fsdp", scatter_dimension=0, tiled=True
        ).astype(jnp.float32),
    )
    summed = lax.psum((owned[0], owned[1], owned[2], owned[3], owned[4], owned[5]), "rep")
    return (
        block_output,
        token_grad,
        summed[0],
        summed[1],
        summed[2],
        summed[3],
        summed[4],
        summed[5],
    )


def solution(mesh):
    in_specs = (
        P("rep", "fsdp", None),
        P("fsdp"),
        P("fsdp", None),
        P("fsdp", None),
        P("fsdp"),
        P("fsdp", None),
        P("fsdp", None),
        P("rep", "fsdp", None),
    )
    out_specs = (
        P("rep", "fsdp", None),
        P("rep", "fsdp", None),
        P("fsdp"),
        P("fsdp", None),
        P("fsdp", None),
        P("fsdp"),
        P("fsdp", None),
        P("fsdp", None),
    )
    return jax.shard_map(local, mesh=mesh, in_specs=in_specs, out_specs=out_specs, check_vma=False)
```

profile of v0, /device:TPU:1, one launch (start us, length us, event | category | flops | bytes accessed | tf_op | source)
XLA Modules:
  0.0 987.1 jit_solution(9366258134474320699)
XLA Ops:
  12.4 10.9 %all-reduce.10 = (bf16[768]{0:T(1024)(128)(2,1)S(1)}, bf16[768]{0:T(1024)(128)(2,1)S(1)}) all-reduce(bf16[768]{0:T(1024)(128)(2,1)S(1)} %dynamic-update-slice, bf16[768]{0:T(1024)(128)(2,1)S(1)} %dynamic-update-slice.1), channel_id=1, replica_groups=mesh['fsdp'=4,'rep'=8] {'fsdp'}, use_global_device_ids=true, to_apply=%add.4 | all-reduce | flops 1536 | bytes 6144
  25.3 56.4 %all-gather.7.cloned.1.call-done = bf16[768,2304]{1,0:T(8,128)(2,1)} async-done(((bf16[192,2304]{1,0:T(8,128)(2,1)}), bf16[768,2304]{1,0:T(8,128)(2,1)}) %all-gather.7.cloned.1.call-update) | async-done | bytes 3538960 | tf_op jit(solution)/shard_map/all_gather | solution.py:103
  81.7 4.1 fusion.73
  90.0 2.5 copy.30
  94.3 2.4 slice.64
  99.7 22.5 %all-gather.17.cloned.1.call-done = bf16[1152,768]{1,0:T(8,128)(2,1)} async-done(((bf16[288,768]{1,0:T(8,128)(2,1)}), bf16[1152,768]{1,0:T(8,128)(2,1)}) %all-gather.17.cloned.1.call-update) | async-done | bytes 1769488 | tf_op jit(solution)/shard_map/all_gather | solution.py:107
  122.2 3.7 convolution_convert_fusion.3
  127.5 59.3 %all-gather.9.cloned.1.call-done = bf16[2048,768]{0,1:T(8,128)(2,1)} async-done(((bf16[512,768]{0,1:T(8,128)(2,1)}), bf16[2048,768]{0,1:T(8,128)(2,1)}) %all-gather.9.cloned.1.call-update) | async-done | bytes 3145744 | tf_op jit(solution)/shard_map/all_gather | solution.py:123
  186.8 6.6 copy.33
  193.4 57.6 %all-gather.11.cloned.1.call-done = bf16[2048,768]{1,0:T(8,128)(2,1)} async-done(((bf16[512,768]{1,0:T(8,128)(2,1)}), bf16[2048,768]{1,0:T(8,128)(2,1)}) %all-gather.11.cloned.1.call-update) | async-done | bytes 3145744 | tf_op jit(solution)/shard_map/all_gather | solution.py:124
  250.9 3.2 copy.31
  254.1 4.6 copy.34
  258.7 120.7 %while.28 = (s32[]{:T(128)}, bf16[12,512,64]{1,2,0:T(8,128)(2,1)}, f32[12,512]{1,0:T(8,128)}, bf16[12,512,64]{2,1,0:T(8,128)(2,1)}, bf16[12,2048,64]{2,1,0:T(8,128)(2,1)}, /*index=5*/bf16[12,2048,64]{2,1,0:T(8,128)(2,1)}) while((s32[]{:T(128)}, bf16[12,512,64]{1,2,0:T(8,128)(2,1)}, f32[12,512]{1,0:T(8,128)}, ...), condition=%wide.region_5.6_spmd.clone, body=%wide.region_2.5_spmd.sunk.clone | while | flops 277872128 | bytes 30693476 | solution.py:129
  264.8 4.1 fusion.128
  274.8 4.0 fusion.128
  284.9 4.0 fusion.128
  295.0 4.0 fusion.128
  305.0 4.1 fusion.128
  315.1 4.1 fusion.128
  325.2 4.0 fusion.128
  335.2 4.0 fusion.128
  345.3 4.0 fusion.128
  355.3 4.0 fusion.128
  365.3 4.0 fusion.128
  375.3 4.0 fusion.128
  379.4 2.4 fusion.81
  383.5 4.2 fusion.76
  387.7 5.4 convert_multiply_fusion.1
  393.2 2.3 multiply_add_fusion
  396.4 2.3 multiply_reduce_fusion.2
  404.0 2.3 copy.35
  406.2 139.5 %while.29 = (s32[]{:T(128)}, f32[12,512,64]{1,2,0:T(8,128)}, bf16[12,2048,64]{1,2,0:T(8,128)(2,1)}, bf16[12,2048,64]{1,2,0:T(8,128)(2,1)}, bf16[12,512,64]{2,1,0...) while((s32[]{:T(128)}, f32[12,512,64]{1,2,0:T(8,128)}, ...), condition=%wide.region_12.13_spmd.clone, body=%wide.region_10.12_spmd.sunk.clone | while | flops 679640576 | bytes 34618464 | solution.py:170
  413.3 2.5 fusion.137
  425.0 2.5 fusion.137
  436.6 2.5 fusion.137
  446.1 2.2 fusion.138
  448.3 2.5 fusion.137
  457.7 2.2 fusion.138
  459.9 2.5 fusion.137
  469.3 2.2 fusion.138
  471.5 2.5 fusion.137
  481.0 2.2 fusion.138
  483.1 2.5 fusion.137
  492.6 2.2 fusion.138
  494.7 2.5 fusion.137
  506.3 2.5 fusion.137
  517.9 2.5 fusion.137
  529.6 2.5 fusion.137
  541.2 2.5 fusion.137
  546.5 3.2 convolution_convert_fusion.4
  549.8 3.7 convolution_convert_fusion.2
  553.6 6.8 convolution_convert_fusion
  560.8 43.9 %reduce-scatter.7.cloned.1.call-done = bf16[512,768]{0,1:T(8,128)(2,1)} async-done(((bf16[2048,768]{0,1:T(8,128)(2,1)}), bf16[512,768]{0,1:T(8,128)(2,1)}) %reduce-scatter.7.cloned.1.call-update) | async-done | bytes 786448 | tf_op jit(solution)/shard_map/reduce_scatter | solution.py:174
  608.3 58.9 %reduce-scatter.9.cloned.1.call-done = bf16[512,768]{0,1:T(8,128)(2,1)} async-done(((bf16[2048,768]{0,1:T(8,128)(2,1)}), bf16[512,768]{0,1:T(8,128)(2,1)}) %reduce-scatter.9.cloned.1.call-update) | async-done | bytes 786448 | tf_op jit(solution)/shard_map/reduce_scatter | solution.py:177
  667.2 5.8 convolution_convert_fusion.1
  673.7 4.4 fusion.61
  678.0 20.8 %reduce-scatter.13.cloned.1.call-done = bf16[192,768]{1,0:T(8,128)(2,1)} async-done(((bf16[768,768]{1,0:T(8,128)(2,1)}), bf16[192,768]{1,0:T(8,128)(2,1)}) %reduce-scatter.13.cloned.1.call-update) | async-done | bytes 294928 | tf_op jit(solution)/shard_map/reduce_scatter | solution.py:199
  698.8 39.9 %reduce-scatter.17.cloned.1.call-done = bf16[288,768]{1,0:T(8,128)(2,1)} async-done(((bf16[1152,768]{1,0:T(8,128)(2,1)}), bf16[288,768]{1,0:T(8,128)(2,1)}) %reduce-scatter.17.cloned.1.call-update) | async-done | bytes 442384 | tf_op jit(solution)/shard_map/reduce_scatter | solution.py:208
  738.7 5.0 fusion.58
  745.6 9.0 all-reduce.9
  754.7 3.3 add_bitcast_fusion
  758.0 48.8 %reduce-scatter.15.cloned.1.call-done = bf16[192,2304]{1,0:T(8,128)(2,1)} async-done(((bf16[768,2304]{1,0:T(8,128)(2,1)}), bf16[192,2304]{1,0:T(8,128)(2,1)}) %reduce-scatter.15.cloned.1.call-update) | async-done | bytes 884752 | tf_op jit(solution)/shard_map/reduce_scatter | solution.py:205
  806.8 69.0 %reduce-scatter.11.cloned.1.call-done = bf16[192,2304]{1,0:T(8,128)(2,1)} async-done(((bf16[768,2304]{1,0:T(8,128)(2,1)}), bf16[192,2304]{1,0:T(8,128)(2,1)}) %reduce-scatter.11.cloned.1.call-update) | async-done | bytes 884752 | tf_op jit(solution)/shard_map/reduce_scatter | solution.py:196
  875.8 104.5 %all-reduce.12 = (f32[192]{0:T(256)}, f32[192,2304]{1,0:T(8,128)}, f32[192,768]{1,0:T(8,128)}, f32[192]{0:T(256)}, f32[192,2304]{1,0:T(8,128)}, /*index=5*/f32[288,768]{1,0:T(8,128)}) all-reduce(f32[192]{0:T(256)S(1)} %get-tuple-element.195, ...), channel_id=1, replica_groups=mesh['fsdp'=4,'rep'=8] {'rep'}, use_global_device_ids=true, to_apply=%region_19.20 | all-reduce | flops 1253760 | bytes 7523328 | tf_op jit(solution)/shard_map/psum | solution.py:212
  (258 shorter events, 202.6 us)
Async XLA Ops:
  7.2 17.5 %copy-start.1 = (bf16[1,512,768]{2,1,0:T(8,128)(2,1)S(1)}, bf16[1,512,768]{2,1,0:T(8,128)(2,1)}, u32[]{:S(2)}) copy-start(bf16[1,512,768]{2,1,0:T(8,128)(2,1)} %param.12) | copy-start | bytes 2359300
  7.2 74.5 %all-gather.7.cloned.1.call-start = ((), (), s32[]{:S(2)}) async-start(), calls=%async_computation.6 | async-start | bytes 4423680 | tf_op jit(solution)/shard_map/all_gather | solution.py:103
  7.9 114.3 %all-gather.17.cloned.1.call-start = ((), (), s32[]{:S(2)}) async-start(), calls=%async_computation.11 | async-start | bytes 2211840 | tf_op jit(solution)/shard_map/all_gather | solution.py:107
  8.7 178.1 %all-gather.9.cloned.1.call-start = ((), (), s32[]{:S(2)}) async-start(), calls=%async_computation.7 | async-start | bytes 3932160 | tf_op jit(solution)/shard_map/all_gather | solution.py:123
  25.0 60.8 %copy-start.18 = (f32[512]{0:T(512)}, f32[512]{0:T(512)S(1)}, u32[]{:S(2)}) copy-start(f32[512]{0:T(512)S(1)} %fusion.57) | copy-start | bytes 6148
  25.3 67.2 %copy-start.13 = (f32[512,32]{0,1:T(8,128)}, f32[512,32]{0,1:T(8,128)S(1)}, u32[]{:S(2)}) copy-start(f32[512,32]{0,1:T(8,128)S(1)} %get-tuple-element.185) | copy-start | bytes 196612
  25.3 67.2 %copy-start.15 = (f32[512,32]{0,1:T(8,128)}, f32[512,32]{0,1:T(8,128)S(1)}, u32[]{:S(2)}) copy-start(f32[512,32]{0,1:T(8,128)S(1)} %get-tuple-element.186) | copy-start | bytes 196612
  85.8 2.1 copy-start.6
  94.3 28.0 %copy-start.7 = (bf16[1,512,768]{2,1,0:T(8,128)(2,1)S(1)}, bf16[1,512,768]{2,1,0:T(8,128)(2,1)}, u32[]{:S(2)}) copy-start(bf16[1,512,768]{2,1,0:T(8,128)(2,1)} %param.19) | copy-start | bytes 2359300
  94.3 156.7 %all-gather.11.cloned.1.call-start = ((), (), s32[]{:S(2)}) async-start(), calls=%async_computation.8 | async-start | bytes 3932160 | tf_op jit(solution)/shard_map/all_gather | solution.py:124
  96.8 282.6 %all-gather.13.cloned.1.call-start = ((), (), s32[]{:S(2)}) async-start(), calls=%async_computation.9 | async-start | bytes 1474560 | tf_op jit(solution)/shard_map/all_gather | solution.py:104
  97.4 286.1 %all-gather.15.cloned.1.call-start = ((), (), s32[]{:S(2)}) async-start(), calls=%async_computation.10 | async-start | bytes 4423680 | tf_op jit(solution)/shard_map/all_gather | solution.py:106
  97.9 506.7 %reduce-scatter.7.cloned.1.call-start = ((), (), s32[]{:S(2)}) async-start(), calls=%async_computation.12 | async-start | bytes 3932160 | tf_op jit(solution)/shard_map/reduce_scatter | solution.py:174
  258.7 120.7 %copy-start.2 = (bf16[1,512,768]{2,1,0:T(8,128)(2,1)S(1)}, bf16[1,512,768]{2,1,0:T(8,128)(2,1)}, u32[]{:S(2)}) copy-start(bf16[1,512,768]{2,1,0:T(8,128)(2,1)} %param.12) | copy-start | bytes 2359300
  260.7 1.9 copy-start
  270.7 1.9 copy-start
  280.8 1.9 copy-start
  290.9 1.9 copy-start
  300.9 1.9 copy-start
  311.0 1.9 copy-start
  321.1 1.9 copy-start
  331.1 1.9 copy-start
  341.2 1.9 copy-start
  351.2 1.9 copy-start
  361.2 1.9 copy-start
  371.2 1.9 copy-start
  381.8 13.7 %copy-start.3 = (f32[512,768]{1,0:T(8,128)}, f32[512,768]{1,0:T(8,128)S(1)}, u32[]{:S(2)}) copy-start(f32[512,768]{1,0:T(8,128)S(1)} %get-tuple-element.190) | copy-start | bytes 4718596
  382.1 0.8 copy-start.20
  383.5 4.2 copy-start.5
  393.1 2.4 copy-start.9
  393.1 2.4 copy-start.22
  393.1 2.4 copy-start.24
  393.2 3.3 copy-start.26
  395.5 3.2 copy-start.10
  396.4 2.3 copy-start.21
  398.7 2.1 copy-start.8
  400.8 1.4 copy-start.27
  401.1 0.9 copy-start.12
  545.7 121.5 %reduce-scatter.9.cloned.1.call-start = ((), (), s32[]{:S(2)}) async-start(), calls=%async_computation.13 | async-start | bytes 3932160 | tf_op jit(solution)/shard_map/reduce_scatter | solution.py:177
  546.5 152.3 %reduce-scatter.13.cloned.1.call-start = ((), (), s32[]{:S(2)}) async-start(), calls=%async_computation.15 | async-start | bytes 1474560 | tf_op jit(solution)/shard_map/reduce_scatter | solution.py:199
  549.7 188.9 %reduce-scatter.17.cloned.1.call-start = ((), (), s32[]{:S(2)}) async-start(), calls=%async_computation.17 | async-start | bytes 2211840 | tf_op jit(solution)/shard_map/reduce_scatter | solution.py:208
  549.8 3.8 copy-start.23
  549.8 3.8 copy-start.25
  553.5 253.3 %reduce-scatter.15.cloned.1.call-start = ((), (), s32[]{:S(2)}) async-start(), calls=%async_computation.16 | async-start | bytes 4423680 | tf_op jit(solution)/shard_map/reduce_scatter | solution.py:205
  560.4 45.7 %copy-start.14 = (f32[512,32]{0,1:T(8,128)S(1)}, f32[512,32]{0,1:T(8,128)}, u32[]{:S(2)}) copy-start(f32[512,32]{0,1:T(8,128)} %copy-done.13) | copy-start | bytes 196612
  560.4 45.7 %copy-start.16 = (f32[512,32]{0,1:T(8,128)S(1)}, f32[512,32]{0,1:T(8,128)}, u32[]{:S(2)}) copy-start(f32[512,32]{0,1:T(8,128)} %copy-done.15) | copy-start | bytes 196612
  560.4 315.3 %reduce-scatter.11.cloned.1.call-start = ((), (), s32[]{:S(2)}) async-start(), calls=%async_computation.14 | async-start | bytes 4423680 | tf_op jit(solution)/shard_map/reduce_scatter | solution.py:196
  604.6 1.6 copy-start.11
  678.0 65.6 %copy-start.19 = (f32[512]{0:T(512)S(1)}, f32[512]{0:T(512)}, u32[]{:S(2)}) copy-start(f32[512]{0:T(512)} %copy-done.18) | copy-start | bytes 6148
  743.7 1.1 copy-start.4
  754.7 121.1 %copy-start.17 = (bf16[192,768]{1,0:T(8,128)(2,1)S(1)}, bf16[192,768]{1,0:T(8,128)(2,1)}, u32[]{:S(2)}) copy-start(bf16[192,768]{1,0:T(8,128)(2,1)} %reduce-scatter.13.cloned.1.call-done) | copy-start | bytes 884740
Sparse Core Ops, SparseCore 0:
  9.6 72.0 all-gather.6
  83.3 38.9 all-gather.16
  124.4 62.3 all-gather.8
  188.8 62.1 all-gather.10
  252.4 28.5 all-gather.12
  282.4 69.6 all-gather.14
  545.8 58.7 reduce-scatter.6
  606.9 60.2 reduce-scatter.8
  669.6 29.1 reduce-scatter.12
  701.5 37.0 reduce-scatter.16
  741.1 65.6 reduce-scatter.14
  809.1 66.6 reduce-scatter.10
where the time goes:
time: 992 us; the launch traced here: 987 us
  waiting for transfers between devices  480 us (48%)
  matrix products  244 us (25%)
  blocking collectives  124 us (12%)
  local copies, waits for them, and re-layouts  83.4 us (8%)
  other arithmetic  37.9 us (4%)
  between operations  15.9 us (2%)
    psum x1, blocking collectives, local(): lax.psum((owned[0], owned[1], owned[2], owned[3], owned[4], owned[5]), 'r...  104 us
    reduce_scatter x1, waiting for transfers between devices, local(): lax.psum_scatter(projection_grad.astype(jnp.bfloat16), 'fsdp', scatter_di...  69 us
    all_gather x1, waiting for transfers between devices, local(): lax.all_gather(own_keys, 'fsdp', axis=0, tiled=True)  59.3 us
    reduce_scatter x1, waiting for transfers between devices, local(): lax.psum_scatter(rows_first(value_backs).astype(jnp.bfloat16), 'fsdp', sc...  58.9 us
    all_gather x1, waiting for transfers between devices, local(): lax.all_gather(own_values, 'fsdp', axis=0, tiled=True)  57.6 us
    all_gather x1, waiting for transfers between devices, local(): lax.all_gather(projection_in, 'fsdp', axis=0, tiled=True)  56.4 us
    reduce_scatter x1, waiting for transfers between devices, local(): lax.psum_scatter(expansion_grad.astype(jnp.bfloat16), 'fsdp', scatter_dim...  48.8 us
    dot_general x12, matrix products, attend_head(): jnp.dot(chances.astype(jnp.bfloat16), values, preferred_element_type=jnp....  48.4 us
  transfers between devices with their start and end apart: 12, of which 10 were waited for; matrix products, arithmetic and copies ran while one was open for 18% of the time, Pallas kernels for 0%

commit v1 on v0

v1 whole, which is shorter than its diff:
```python
import functools
import math

import jax
import jax.numpy as jnp
from jax import lax
from jax.experimental import pallas as pl
from jax.experimental.pallas import tpu as pltpu
from jax.sharding import PartitionSpec as P

HEADS = 12
HEAD_DIM = 64
HALF = HEAD_DIM // 2
SCALE = 1.0 / math.sqrt(HEAD_DIM)
EPS = 1e-05
THETA = 160000.0
F32 = jnp.float32
BF16 = jnp.bfloat16
NN = (((1,), (0,)), ((), ()))
NT = (((1,), (1,)), ((), ()))
TN = (((0,), (0,)), ((), ()))
TT = (((0,), (1,)), ((), ()))


def mul(a, b, dims=NN):
    return lax.dot_general(a, b, dims, preferred_element_type=F32)


def layer_norm(values, gain):
    centre = values - jnp.mean(values, axis=-1, keepdims=True)
    spread = jnp.mean(centre * centre, axis=-1, keepdims=True)
    return centre * lax.rsqrt(spread + EPS) * gain


def layer_norm_back(values, gain, grad):
    centre = values - jnp.mean(values, axis=-1, keepdims=True)
    inverse = lax.rsqrt(jnp.mean(centre * centre, axis=-1, keepdims=True) + EPS)
    unit = centre * inverse
    scaled = grad * gain
    first = jnp.mean(scaled, axis=-1, keepdims=True)
    second = jnp.mean(scaled * unit, axis=-1, keepdims=True)
    return inverse * (scaled - first - unit * second)


def geglu(inner):
    width = inner.shape[-1] // 2
    return jax.nn.gelu(inner[:, :width], approximate=False) * inner[:, width:]


def rounded(values):
    return lax.optimization_barrier(values.astype(BF16)).astype(F32)


def attend_kernel(heads, q_ref, k_ref, v_ref, out_ref, log_ref):
    for head in range(heads):
        rows = pl.ds(head * HEAD_DIM, HEAD_DIM)
        scores = mul(k_ref[head], q_ref[rows, :])
        highest = jnp.max(scores, axis=0, keepdims=True)
        raised = jnp.exp(scores - highest)
        total = jnp.sum(raised, axis=0, keepdims=True)
        mixed = mul(v_ref[rows, :], raised.astype(BF16))
        out_ref[rows, :] = (mixed / total).astype(BF16)
        log_ref[pl.ds(head, 1), :] = highest + jnp.log(total)


def attend(queries, keys, values, step=256):
    width, count = queries.shape
    heads = keys.shape[0]
    return pl.pallas_call(
        functools.partial(attend_kernel, heads),
        grid=(count // step,),
        in_specs=[
            pl.BlockSpec((width, step), lambda i: (0, i)),
            pl.BlockSpec((heads, count, HEAD_DIM), lambda i: (0, 0, 0)),
            pl.BlockSpec((width, count), lambda i: (0, 0)),
        ],
        out_specs=[
            pl.BlockSpec((width, step), lambda i: (0, i)),
            pl.BlockSpec((heads, step), lambda i: (0, i)),
        ],
        out_shape=[
            jax.ShapeDtypeStruct((width, count), BF16),
            jax.ShapeDtypeStruct((heads, count), F32),
        ],
        compiler_params=pltpu.CompilerParams(vmem_limit_bytes=48 * 2**20),
        cost_estimate=pl.CostEstimate(
            flops=4 * heads * count * count * HEAD_DIM,
            bytes_accessed=8 * width * count,
            transcendentals=heads * count * count,
        ),
        name="attend",
    )(queries, keys, values)


def turn_back(values, cosine, sine):
    first, second = values[:HALF], values[HALF:]
    return jnp.concatenate([first * cosine + second * sine, second * cosine - first * sine], axis=0)


def attend_back_kernel(
    head, q_ref, kt_ref, k_ref, v_ref, up_ref, out_ref, log_ref, cos_ref, sin_ref, grad_ref, dk_ref, dv_ref
):
    index = pl.program_id(0)
    step = q_ref.shape[1]

    @pl.when(index == 0)
    def _():
        dk_ref[...] = jnp.zeros_like(dk_ref)
        dv_ref[...] = jnp.zeros_like(dv_ref)

    upstream = up_ref[...]
    inner_sum = jnp.sum(upstream.astype(F32) * out_ref[...].astype(F32), axis=0, keepdims=True)
    chances = jnp.exp(mul(k_ref[0], q_ref[...]) - log_ref[pl.ds(head, 1), :])
    prob_back = mul(v_ref[0], upstream)
    score_back = (chances * (prob_back - inner_sum)).astype(BF16)
    dv_ref[...] += mul(chances.astype(BF16), upstream, NT)
    dk_ref[...] += mul(score_back, q_ref[...], NT)
    columns = pl.ds(pl.multiple_of(index * step, step), step)
    query_back = mul(kt_ref[...], score_back) * SCALE
    grad_ref[pl.ds(0, HEAD_DIM), columns] = turn_back(
        query_back, cos_ref[:, columns], sin_ref[:, columns]
    ).astype(BF16)

    @pl.when(index == pl.num_programs(0) - 1)
    def _():
        key_back = turn_back(dk_ref[...].T, cos_ref[...], sin_ref[...])
        grad_ref[pl.ds(HEAD_DIM, HEAD_DIM), :] = key_back.astype(BF16)
        grad_ref[pl.ds(2 * HEAD_DIM, HEAD_DIM), :] = dv_ref[...].T.astype(BF16)


def attend_back(head, queries, keys_turned, keys, values, upstream, merged, logs, cosine, sine, step=256):
    count = queries.shape[1]
    heads = keys.shape[0]
    some = pl.BlockSpec((HEAD_DIM, step), lambda i: (head, i))
    rows = pl.BlockSpec((1, count, HEAD_DIM), lambda i: (head, 0, 0))
    whole = pl.BlockSpec((HALF, count), lambda i: (0, 0))
    return pl.pallas_call(
        functools.partial(attend_back_kernel, head),
        grid=(count // step,),
        in_specs=[
            some,
            pl.BlockSpec((HEAD_DIM, count), lambda i: (head, 0)),
            rows,
            rows,
            some,
            some,
            pl.BlockSpec((heads, step), lambda i: (0, i)),
            whole,
            whole,
        ],
        out_specs=pl.BlockSpec((3 * HEAD_DIM, count), lambda i: (0, 0)),
        out_shape=jax.ShapeDtypeStruct((3 * HEAD_DIM, count), BF16),
        scratch_shapes=[pltpu.VMEM((count, HEAD_DIM), F32), pltpu.VMEM((count, HEAD_DIM), F32)],
        compiler_params=pltpu.CompilerParams(vmem_limit_bytes=48 * 2**20),
        cost_estimate=pl.CostEstimate(
            flops=10 * count * count * HEAD_DIM,
            bytes_accessed=16 * HEAD_DIM * count,
            transcendentals=count * count,
        ),
        name="attend_back",
    )(queries, keys_turned, keys, values, upstream, merged, logs, cosine, sine)


def swap(values, axis, size, offset):
    return lax.ppermute(values, axis, [(i, i ^ offset) for i in range(size)])


def exchange(pieces, size):
    return [pieces[0]] + [swap(pieces[d], "fsdp", size, d) for d in range(1, size)]


def pick(blocks, index):
    return lax.dynamic_index_in_dim(blocks, index, 0, keepdims=False)


def reorder(blocks, z, size):
    return jnp.stack([pick(blocks, z ^ j) for j in range(size)])


def orders(ranks):
    far = []
    bit = 2
    while bit < ranks:
        far.append(bit)
        bit *= 2
    return far, far[::-1]


def place(r, bits):
    total = 0
    for k, bit in enumerate(bits):
        total = total + jnp.where(r & bit != 0, 1 << k, 0)
    return total


def grow(values, r, ranks, bits):
    for bit in bits:
        other = swap(values, "rep", ranks, bit)
        upper = r & bit != 0
        values = jnp.concatenate(
            [jnp.where(upper, other, values), jnp.where(upper, values, other)], axis=1
        )
    return values


def shrink(values, r, ranks, bits):
    for bit in bits:
        half = values.shape[1] // 2
        mine = jnp.where(r & bit != 0, half, 0)
        sent = lax.dynamic_slice_in_dim(values, half - mine, half, 1)
        kept = lax.dynamic_slice_in_dim(values, mine, half, 1)
        other = swap(sent, "rep", ranks, bit)
        values = (kept.astype(F32) + other.astype(F32)).astype(BF16)
    return values


def halves(values):
    middle = values.shape[-1] // 2
    return values[..., :middle], values[..., middle:]


def gather_rows(shard, z, r, size, ranks):
    rows = shard.shape[0] // ranks
    one, two = orders(ranks)
    left, right = halves(shard)
    piece = jnp.concatenate(
        [
            lax.dynamic_slice_in_dim(left, place(r, one + [1]) * rows, rows, 0),
            lax.dynamic_slice_in_dim(right, place(r, two + [1]) * rows, rows, 0),
        ],
        axis=1,
    )
    blocks = reorder(jnp.stack(exchange([piece] * size, size)), z, size)
    left, right = halves(blocks)
    both = jnp.concatenate([grow(left, r, ranks, one), grow(right, r, ranks, two)], axis=2)
    return grow(both, r, ranks, [1])


def reduce_rows(blocks, z, r, size, ranks):
    one, two = orders(ranks)
    left, right = halves(shrink(blocks, r, ranks, [1]))
    both = jnp.concatenate(
        [shrink(left, r, ranks, one[::-1]), shrink(right, r, ranks, two[::-1])], axis=2
    )
    arrived = exchange([pick(both, z ^ d) for d in range(size)], size)
    total = sum(part.astype(F32) for part in arrived).astype(BF16)[None]
    left, right = halves(total)
    both = jnp.concatenate([grow(left, r, ranks, one), grow(right, r, ranks, two)], axis=2)
    return grow(both, r, ranks, [1])[0]


def gather_rows_short(shard, z, r, size, ranks):
    rows = shard.shape[0] // ranks
    bits = orders(ranks)[0] + [1]
    piece = lax.dynamic_slice_in_dim(shard, place(r, bits) * rows, rows, 0)
    blocks = reorder(jnp.stack(exchange([piece] * size, size)), z, size)
    return grow(blocks, r, ranks, bits)


def reduce_rows_short(blocks, z, r, size, ranks):
    bits = orders(ranks)[0] + [1]
    mine = shrink(blocks, r, ranks, bits[::-1])
    arrived = exchange([pick(mine, z ^ d) for d in range(size)], size)
    return grow(reorder(jnp.stack(arrived), z, size), r, ranks, bits)


def local(size, ranks, tokens, gain_a, projection_in, attention_out, gain_b, expansion, contraction, cotangent):
    z = lax.axis_index("fsdp")
    r = lax.axis_index("rep")
    own = tokens[0]
    count, width = own.shape
    part = width // size
    hidden = contraction.shape[0]
    heads = HEADS // size

    gains = jnp.stack([gain_a, gain_b])
    gains = reorder(jnp.stack(exchange([gains] * size, size)), z, size)
    gain_one = gains[:, 0].reshape(width).astype(F32)
    gain_two = gains[:, 1].reshape(width).astype(F32)

    columns = [projection_in[:, t * width : (t + 1) * width] for t in range(3)]
    into = gather_rows_short(jnp.concatenate(columns, axis=0), z, r, size, ranks)
    into = into.reshape(size, 3, part, width).transpose(1, 3, 0, 2).reshape(3, width, width)
    blocks = exchange([own] * size, size)

    columns = [expansion[:, t * width : (t + 1) * width] for t in range(3)]
    stacked = jnp.concatenate([attention_out] + columns + [contraction], axis=0)
    pad = -stacked.shape[0] % (8 * ranks)
    stacked = jnp.concatenate([stacked, jnp.zeros((pad, width), BF16)], axis=0)
    rest = gather_rows(stacked, z, r, size, ranks)
    out_weight = reorder(rest[:, :part], z, size).reshape(width, width)
    expand = [rest[:, (1 + t) * part : (2 + t) * part].reshape(width, width) for t in range(3)]
    contract = rest[:, 4 * part : 4 * part + hidden].reshape(size * hidden, width)

    freqs = THETA ** (-(jnp.arange(HALF, dtype=F32) * (2.0 / HEAD_DIM)))
    places = jnp.concatenate([(z ^ d) * count + jnp.arange(count, dtype=jnp.int32) for d in range(size)])
    angles = freqs[:, None] * places.astype(F32)[None, :]
    cosine, sine = jnp.cos(angles), jnp.sin(angles)

    normed = jnp.concatenate([layer_norm(b.astype(F32), gain_one).astype(BF16) for b in blocks], axis=0)
    own_into = [lax.dynamic_slice_in_dim(into[t], z * part, part, 0) for t in range(3)]

    def rotate(values):
        shaped = values.reshape(heads, 2, HALF, size * count)
        first, second = shaped[:, 0], shaped[:, 1]
        turned = jnp.stack([first * cosine - second * sine, second * cosine + first * sine], axis=1)
        return turned.reshape(part, size * count)

    queries = (rotate(mul(own_into[0], normed, NT)).astype(BF16) * SCALE).astype(BF16)
    keys_turned = rotate(mul(own_into[1], normed, NT)).astype(BF16)
    keys = keys_turned.reshape(heads, HEAD_DIM, size * count).transpose(0, 2, 1)
    values_turned = mul(own_into[2], normed, NT).astype(BF16)
    values = values_turned.reshape(heads, HEAD_DIM, size * count).transpose(0, 2, 1)
    own_merged, logs = attend(queries, keys, values_turned)

    arrived = exchange([own_merged[:, d * count : (d + 1) * count] for d in range(size)], size)
    merged = jnp.concatenate(arrived, axis=0)
    inputs = own.astype(F32)
    state = inputs + mul(merged, out_weight, TN)
    normed_two = layer_norm(state, gain_two).astype(BF16)
    inner = jnp.concatenate([mul(normed_two, w) for w in expand], axis=1)
    active, glu_back = jax.vjp(geglu, inner)
    active = active.astype(BF16)
    block_output = (state + mul(active, contract)).astype(BF16)[None]

    upstream = cotangent[0]
    (inner_back,) = glu_back(rounded(mul(upstream, contract, NT)))
    inner_back = inner_back.astype(BF16)
    normed_two_back = sum(
        mul(inner_back[:, t * width : (t + 1) * width], expand[t], NT) for t in range(3)
    )
    state_back = upstream.astype(F32) + layer_norm_back(state, gain_two, normed_two_back)
    state_low = state_back.astype(BF16)
    merged_back = mul(out_weight, state_low, NT).astype(BF16)
    arrived = exchange([merged_back[d * part : (d + 1) * part] for d in range(size)], size)
    own_upstream = jnp.concatenate(arrived, axis=1)

    contraction_grad = mul(active, upstream, TN).astype(BF16).reshape(size, hidden, width)
    expansion_grad = [
        mul(normed_two, inner_back[:, t * width : (t + 1) * width], TN).astype(BF16).reshape(size, part, width)
        for t in range(3)
    ]
    out_grad = reorder(mul(merged, state_low).astype(BF16).reshape(size, part, width), z, size)
    grads = jnp.concatenate(
        [out_grad] + expansion_grad + [contraction_grad, jnp.zeros((size, pad, width), BF16)], axis=1
    )
    grads = reduce_rows(grads, z, r, size, ranks).astype(F32)
    attention_out_sum = grads[:part]
    expansion_sum = jnp.concatenate([grads[(1 + t) * part : (2 + t) * part] for t in range(3)], axis=1)
    contraction_sum = grads[4 * part : 4 * part + hidden]

    turned_backs = []
    received = []
    weights = []
    by_head = into.reshape(3, size, heads, HEAD_DIM, width)
    for head in range(heads):
        grad = attend_back(
            head, queries, keys_turned, keys, values, own_upstream, own_merged, logs, cosine, sine
        )
        turned_backs.append(grad)
        received += exchange([grad[:, d * count : (d + 1) * count] for d in range(size)], size)
        chosen = by_head[:, :, head].transpose(1, 0, 2, 3)
        weights.append(reorder(chosen, z, size).reshape(size * 3 * HEAD_DIM, width))
    projected_back = jnp.concatenate(received, axis=0)
    normed_back = mul(projected_back, jnp.concatenate(weights, axis=0), TN)
    token_grad = (state_back + layer_norm_back(inputs, gain_one, normed_back))[None]

    all_backs = jnp.stack(turned_backs).reshape(heads, 3, HEAD_DIM, size * count)
    all_backs = all_backs.transpose(1, 0, 2, 3).reshape(3 * part, size * count)
    into_grad = mul(normed, all_backs, TT).astype(BF16).reshape(size, part, 3 * part)
    into_sum = reduce_rows_short(into_grad, z, r, size, ranks)
    into_sum = into_sum.reshape(size, part, 3, part).transpose(1, 2, 0, 3).reshape(part, 3 * width).astype(F32)

    gain_one_sum = jnp.sum(into_sum * projection_in.astype(F32), axis=1) / gain_a.astype(F32)
    gain_two_sum = jnp.sum(expansion_sum * expansion.astype(F32), axis=1) / gain_b.astype(F32)
    return (
        block_output,
        token_grad,
        gain_one_sum,
        into_sum,
        attention_out_sum,
        gain_two_sum,
        expansion_sum,
        contraction_sum,
    )


def solution(mesh):
    tokens, rows, line = P("rep", "fsdp", None), P("fsdp", None), P("fsdp")
    in_specs = (tokens, line, rows, rows, line, rows, rows, tokens)
    out_specs = (tokens, tokens, line, rows, rows, line, rows, rows)
    body = functools.partial(local, mesh.shape["fsdp"], mesh.shape["rep"])
    return jax.shard_map(body, mesh=mesh, in_specs=in_specs, out_specs=out_specs, check_vma=False)
```

time: 992 us -> 447 us (0.45)
  waiting for transfers between devices: 480 us -> 131 us
  matrix products: 244 us -> 34.9 us
  blocking collectives: 124 us -> 0 us
  starting transfers between devices: 0.92 us -> 96.9 us
  Pallas kernels: 0 us -> 68.8 us
  local copies, waits for them, and re-layouts: 83.4 us -> 57.6 us
  between operations: 15.9 us -> 2.55 us
  other arithmetic: 37.9 us -> 49.2 us
    reduce_scatter x6 -> x0, waiting for transfers between devices: 281 us -> none  [the longest x1 69 us: local(): lax.psum_scatter(projection_grad.astype(jnp.bfloat16), 'fsdp', scatter_di...]
    dot_general x96 -> x20, matrix products: 244 us -> 34.9 us  [mul(): return lax.dot_general(a, b, dims, preferred_element_type=F32)]
    all_gather x6 -> x0, waiting for transfers between devices: 196 us -> none  [the longest x1 59.3 us: local(): lax.all_gather(own_keys, 'fsdp', axis=0, tiled=True)]
    ppermute x0 -> x57, waiting for transfers between devices: none -> 131 us  [swap(): return lax.ppermute(values, axis, [(i, i ^ offset) for i in range(size)])]
    psum x1 -> x0, blocking collectives: 104 us -> none  [local(): lax.psum((owned[0], owned[1], owned[2], owned[3], owned[4], owned[5]), 'r...]
    ppermute x0 -> x57, starting transfers between devices: none -> 96.9 us  [swap(): return lax.ppermute(values, axis, [(i, i ^ offset) for i in range(size)])]
    pallas_call x0 -> x4, Pallas kernels: none -> 68.8 us  [the longest x3 39.5 us: attend_back(): pl.pallas_call(functools.partial(attend_back_kernel, head), grid=(count /...]
    while x27 -> x0, local copies, waits for them, and re-layouts: 35.8 us -> none
  transfers between devices with their start and end apart: 12 -> 57, of which waited for: 10 -> 22; matrix products, arithmetic and copies ran while one was open for 18% -> 22% of each run, Pallas kernels for 0% -> 16%
where the time goes in v1:
time: 447 us; the launch traced here: 441 us
  waiting for transfers between devices  131 us (29%)
  starting transfers between devices  96.9 us (22%)
  Pallas kernels  68.8 us (15%)
  local copies, waits for them, and re-layouts  57.6 us (13%)
  other arithmetic  49.2 us (11%)
  matrix products  34.9 us (8%)
    ppermute x57, waiting for transfers between devices, swap(): return lax.ppermute(values, axis, [(i, i ^ offset) for i in range(size)])  131 us
    ppermute x57, starting transfers between devices, swap(): return lax.ppermute(values, axis, [(i, i ^ offset) for i in range(size)])  96.9 us
    pallas_call x3, Pallas kernels, attend_back(): pl.pallas_call(functools.partial(attend_back_kernel, head), grid=(count /...  39.5 us
    dot_general x20, matrix products, mul(): return lax.dot_general(a, b, dims, preferred_element_type=F32)  34.9 us
    pallas_call x1, Pallas kernels, attend(): pl.pallas_call(functools.partial(attend_kernel, heads), grid=(count // st...  29.3 us
    unnamed x111, local copies, waits for them, and re-layouts  16.2 us
  transfers between devices with their start and end apart: 57, of which 22 were waited for; matrix products, arithmetic and copies ran while one was open for 22% of the time, Pallas kernels for 16%

profile of v1, /device:TPU:1, one launch (start us, length us, event | category | flops | bytes accessed | tf_op | source)
XLA Modules:
  0.0 440.6 jit_solution(8975694850170273600)
XLA Ops:
  7.6 4.2 collective-permute-start.17
  17.3 3.8 collective-permute-done.8
  21.2 3.0 collective-permute-start.2
  24.1 7.7 %collective-permute-done.7 = bf16[2,192]{1,0:T(2,128)(2,1)S(1)} collective-permute-done((bf16[2,192]{1,0:T(2,128)(2,1)S(1)}, bf16[2,192]{1,0:T(2,128)(2,1)S(1)}, u32[]{:S(2)}, u32[]{:S(2)}) %collective-permute-start.7) | collective-permute-done | bytes 800 | tf_op jit(solution)/shard_map/ppermute | solution.py:165
  35.3 2.6 collective-permute-done.1
  38.8 3.3 collective-permute-start.10
  48.3 4.0 collective-permute-done.3
  53.5 6.5 %collective-permute-done.18 = bf16[4,136,384]{2,1,0:T(8,128)(2,1)} collective-permute-done((bf16[4,136,384]{2,1,0:T(8,128)(2,1)}, bf16[4,136,384]{2,1,0:T(8,128)(2,1)}, u32[]{:S(2)}, u32[]{:S(2)}) %collective-permute-start.18) | collective-permute-done | bytes 417824 | tf_op jit(solution)/shard_map/ppermute | solution.py:165
  64.0 13.0 %collective-permute-done.9 = bf16[512,768]{1,0:T(8,128)(2,1)S(1)} collective-permute-done((bf16[512,768]{1,0:T(8,128)(2,1)S(1)}, bf16[512,768]{1,0:T(8,128)(2,1)S(1)}, u32[]{:S(2)}, u32[]{:S(2)}) %collective-permute-start.9) | collective-permute-done | bytes 786464 | tf_op jit(solution)/shard_map/ppermute | solution.py:165
  80.1 12.4 %collective-permute-done.11 = bf16[512,768]{1,0:T(8,128)(2,1)S(1)} collective-permute-done((bf16[512,768]{1,0:T(8,128)(2,1)S(1)}, bf16[512,768]{1,0:T(8,128)(2,1)S(1)}, u32[]{:S(2)}, u32[]{:S(2)}) %collective-permute-start.11) | collective-permute-done | bytes 786464 | tf_op jit(solution)/shard_map/ppermute | solution.py:165
  94.7 6.8 %collective-permute-start.5 = (bf16[4,288,768]{2,1,0:T(8,128)(2,1)S(1)}, bf16[4,288,768]{2,1,0:T(8,128)(2,1)S(1)}, u32[]{:S(2)}, u32[]{:S(2)}) collective-permute-start(bf16[4,288,768]{2,1,0:T(8,128)(2,1)S(1)} %pad_maximum_fusion.5), channel_id=1, source_target_pairs={{0,1},{1,0},{2,3},{3,2},{4,5},{5,4},{6,7},{7,6},{8,9},{9,8},{10,11... | collective-permute-start | bytes 5308424 | tf_op jit(solution)/shard_map/ppermute | solution.py:165
  101.8 2.4 fusion.24
  105.0 2.3 maximum_maximum_fusion
  107.3 2.7 collective-permute-start.22
  114.9 8.1 %copy.47 = bf16[3,768,4,192]{3,2,1,0:T(4,128)(2,1)} copy(bf16[3,768,4,192]{1,3,0,2:T(8,128)(2,1)} %bitcast.169) | data formatting | bytes 7077888 | tf_op jit(solution)/shard_map/transpose | solution.py:283
  123.1 1.5 copy.44
  124.6 4.3 fusion.65
  130.8 6.2 %convolution_convert_fusion.2.v_ref = bf16[192,2048]{1,0:T(8,128)(2,1)S(1)} fusion(bf16[768,768]{0,1:T(8,128)(2,1)} %bitcast.193, s32[]{:T(128)S(6)} %select_n.349, bf16[512,768]{1,0:T(8,128)(2,1)S(1)} %copy-done.38, bf16[512,768]{1,0:T(8,128)(2,1)S(1)} %copy-done.35, bf16[512,768]{1,0:T(8,128)(2,1)S(1)} %copy-done.32, bf16[512,768]{1,0:T(8,128)(2,1)S(1)} %copy-done.29), kind=kOutput, calls=%fused_computation.19 | convolution fusion | flops 616955904 | bytes 4325380 | tf_op jit(solution)/shard_map/dot_general | solution.py:26
  137.0 29.3 %attend.1 = (bf16[192,2048]{1,0:T(8,128)(2,1)S(1)}, f32[3,2048]{1,0:T(4,128)S(1)}) custom-call(bf16[192,2048]{1,0:T(8,128)(2,1)S(1)} %bitcast.163, bf16[3,2048,64]{2,1,0:T(8,128)(2,1)S(1)} %bitcast.159, bf16[192,2048]{1,0:T(8,128)(2,1)S(1)} %convolution_convert_fusion.2.v_ref), custom_call_target="tpu_custom_call" | custom-call | flops 3221225472 | bytes 3145728 | tf_op jit(solution)/shard_map/attend/pallas_call | solution.py:69
  168.5 10.3 %collective-permute-start.13 = (bf16[192,512]{1,0:T(8,128)(2,1)S(1)}, bf16[192,512]{1,0:T(8,128)(2,1)}, u32[]{:S(2)}, u32[]{:S(2)}) collective-permute-start(bf16[192,512]{1,0:T(8,128)(2,1)S(1)} %get-tuple-element.118), channel_id=1, source_target_pairs={{0,16},{8,24},{16,0},{24,8},{1,17},{9,25},{17,1},{25,9},{2,18},{10... | collective-permute-start | bytes 589832 | tf_op jit(solution)/shard_map/ppermute | solution.py:165
  178.7 1.5 copy.46
  180.3 8.9 %reshape_reshape.3 = bf16[3,4,3,64,768]{4,3,2,1,0:T(8,128)(2,1)} reshape(bf16[3,768,4,192]{3,2,1,0:T(4,128)(2,1)} %copy.47) | data formatting | bytes 7077888 | tf_op jit(solution)/shard_map/reshape;reshape | solution.py:355
  189.2 2.2 fusion.90
  196.0 2.8 broadcast_select_fusion
  202.5 2.0 fusion.103
  207.5 5.4 %convert_multiply_fusion.1 = (f32[512,1152]{1,0:T(8,128)S(1)}, f32[512,1152]{1,0:T(8,128)S(1)}) fusion(bf16[512,1152]{1,0:T(8,128)(2,1)S(1)} %fusion.6, f32[512,768]{1,0:T(8,128)S(1)} %fusion.105, f32[512,768]{1,0:T(8,128)S(1)} %fusion.104), kind=kLoop, calls=%fused_computation.17 | loop fusion | flops 39518208 | bytes 9043968 | tf_op jit(solution)/shard_map/transpose(jvp())/mul | solution.py:47
  218.5 2.1 fusion.43
  224.4 2.1 collective-permute-start.25
  228.0 1.9 convolution_convert_fusion.6
  230.5 2.0 constant_dynamic-slice_fusion.4
  232.6 2.0 copy-done.8
  234.6 1.9 collective-permute-start.44
  236.5 7.9 %collective-permute-done.24 = bf16[192,512]{1,0:T(8,128)(2,1)S(1)} collective-permute-done((bf16[192,512]{1,0:T(8,128)(2,1)S(1)}, bf16[192,512]{1,0:T(8,128)(2,1)S(1)}, u32[]{:S(2)}, u32[]{:S(2)}) %collective-permute-start.24) | collective-permute-done | bytes 196640 | tf_op jit(solution)/shard_map/ppermute | solution.py:165
  244.5 13.3 %attend_back.5 = bf16[192,2048]{1,0:T(8,128)(2,1)S(1)} custom-call(bf16[192,2048]{1,0:T(8,128)(2,1)S(1)} %bitcast.164, bf16[192,2048]{1,0:T(8,128)(2,1)S(1)} %bitcast.156, bf16[3,2048,64]{2,1,0:T(8,128)(2,1)S(1)} %bitcast.160, bf16[3,2048,64]{2,1,0:T(8,128)(2,1)} %bitcast.184, bf16[192,2048]{1,0:T(8,128)(2,1)S(1)} %pad_maximum_fusion.18.up_ref, ...), custom_call_target="tpu_custom_call" | custom-call | flops 2684354560 | bytes 2097152 | tf_op jit(solution)/shard_map/attend_back/pallas_call | solution.py:137
  257.8 13.1 %attend_back.4 = bf16[192,2048]{1,0:T(8,128)(2,1)S(1)} custom-call(bf16[192,2048]{1,0:T(8,128)(2,1)S(1)} %bitcast.165, bf16[192,2048]{1,0:T(8,128)(2,1)S(1)} %bitcast.157, bf16[3,2048,64]{2,1,0:T(8,128)(2,1)S(1)} %bitcast.161, bf16[3,2048,64]{2,1,0:T(8,128)(2,1)} %bitcast.185, bf16[192,2048]{1,0:T(8,128)(2,1)S(1)} %pad_maximum_fusion.18.up_ref, ...), custom_call_target="tpu_custom_call" | custom-call | flops 2684354560 | bytes 2097152 | tf_op jit(solution)/shard_map/attend_back/pallas_call | solution.py:137
  270.9 13.1 %attend_back.3 = bf16[192,2048]{1,0:T(8,128)(2,1)S(1)} custom-call(bf16[192,2048]{1,0:T(8,128)(2,1)S(1)} %bitcast.166, bf16[192,2048]{1,0:T(8,128)(2,1)S(1)} %bitcast.158, bf16[3,2048,64]{2,1,0:T(8,128)(2,1)S(1)} %bitcast.162, bf16[3,2048,64]{2,1,0:T(8,128)(2,1)} %bitcast.186, bf16[192,2048]{1,0:T(8,128)(2,1)S(1)} %pad_maximum_fusion.18.up_ref, ...), custom_call_target="tpu_custom_call" | custom-call | flops 2684354560 | bytes 2097152 | tf_op jit(solution)/shard_map/attend_back/pallas_call | solution.py:137
  284.2 2.4 collective-permute-start.27
  288.0 5.1 %collective-permute-done.26 = bf16[192,512]{1,0:T(8,128)(2,1)S(1)} collective-permute-done((bf16[192,512]{1,0:T(8,128)(2,1)S(1)}, bf16[192,512]{1,0:T(8,128)(2,1)S(1)}, u32[]{:S(2)}, u32[]{:S(2)}) %collective-permute-start.26) | collective-permute-done | bytes 196640 | tf_op jit(solution)/shard_map/ppermute | solution.py:165
  293.2 5.6 %collective-permute-done.28 = bf16[192,512]{1,0:T(8,128)(2,1)S(1)} collective-permute-done((bf16[192,512]{1,0:T(8,128)(2,1)S(1)}, bf16[192,512]{1,0:T(8,128)(2,1)S(1)}, u32[]{:S(2)}, u32[]{:S(2)}) %collective-permute-start.28) | collective-permute-done | bytes 196640 | tf_op jit(solution)/shard_map/ppermute | solution.py:165
  298.9 4.7 %collective-permute-start.29 = (bf16[192,512]{1,0:T(8,128)(2,1)S(1)}, bf16[192,512]{1,0:T(8,128)(2,1)S(1)}, u32[]{:S(2)}, u32[]{:S(2)}) collective-permute-start(bf16[192,512]{1,0:T(8,128)(2,1)S(1)} %get-tuple-element.106), channel_id=1, source_target_pairs={{0,8},{8,0},{16,24},{24,16},{1,9},{9,1},{17,25},{25,17},{2,10},{10... | collective-permute-start | bytes 589832 | tf_op jit(solution)/shard_map/ppermute | solution.py:165
  303.6 2.0 convolution_convert_fusion.7
  306.4 2.3 collective-permute-start.30
  308.8 2.3 collective-permute-start.35
  313.0 8.2 %collective-permute-done.30 = bf16[192,512]{1,0:T(8,128)(2,1)S(1)} collective-permute-done((bf16[192,512]{1,0:T(8,128)(2,1)S(1)}, bf16[192,512]{1,0:T(8,128)(2,1)S(1)}, u32[]{:S(2)}, u32[]{:S(2)}) %collective-permute-start.30) | collective-permute-done | bytes 196640 | tf_op jit(solution)/shard_map/ppermute | solution.py:165
  323.4 3.8 collective-permute-start.32
  331.9 1.8 collective-permute-done.33
  334.3 6.9 %collective-permute-done.34 = bf16[192,512]{1,0:T(8,128)(2,1)S(1)} collective-permute-done((bf16[192,512]{1,0:T(8,128)(2,1)S(1)}, bf16[192,512]{1,0:T(8,128)(2,1)S(1)}, u32[]{:S(2)}, u32[]{:S(2)}) %collective-permute-start.34) | collective-permute-done | bytes 196640 | tf_op jit(solution)/shard_map/ppermute | solution.py:165
  342.0 4.2 fusion.87
  347.6 2.8 add_convert_fusion
  352.3 4.1 collective-permute-start.40
  356.4 2.7 collective-permute-start.39
  359.8 1.7 fusion.29
  362.2 3.2 collective-permute-done.45
  366.0 10.2 %collective-permute-done.47 = bf16[4,272,384]{2,1,0:T(8,128)(2,1)S(1)} collective-permute-done((bf16[4,272,384]{2,1,0:T(8,128)(2,1)S(1)}, bf16[4,272,384]{2,1,0:T(8,128)(2,1)S(1)}, u32[]{:S(2)}, u32[]{:S(2)}) %collective-permute-start.47) | collective-permute-done | bytes 835616 | tf_op jit(solution)/shard_map/ppermute | solution.py:165
  376.9 8.2 %collective-permute-done.46 = bf16[4,136,384]{2,1,0:T(8,128)(2,1)S(1)} collective-permute-done((bf16[4,136,384]{2,1,0:T(8,128)(2,1)S(1)}, bf16[4,136,384]{2,1,0:T(8,128)(2,1)S(1)}, u32[]{:S(2)}, u32[]{:S(2)}) %collective-permute-start.46) | collective-permute-done | bytes 417824 | tf_op jit(solution)/shard_map/ppermute | solution.py:165
  385.5 2.6 collective-permute-start.51
  389.9 2.2 collective-permute-done.51
  392.2 12.1 %collective-permute-done.50 = bf16[136,768]{1,0:T(8,128)(2,1)S(1)} collective-permute-done((bf16[136,768]{1,0:T(8,128)(2,1)S(1)}, bf16[136,768]{1,0:T(8,128)(2,1)S(1)}, u32[]{:S(2)}, u32[]{:S(2)}) %collective-permute-start.50) | collective-permute-done | bytes 208928 | tf_op jit(solution)/shard_map/ppermute | solution.py:165
  406.0 2.0 collective-permute-done.52
  409.7 5.5 %collective-permute-start.43 = (bf16[4,96,576]{2,1,0:T(8,128)(2,1)S(1)}, bf16[4,96,576]{2,1,0:T(8,128)(2,1)S(1)}, u32[]{:S(2)}, u32[]{:S(2)}) collective-permute-start(bf16[4,96,576]{2,1,0:T(8,128)(2,1)S(1)} %pad_maximum_fusion.19), channel_id=1, source_target_pairs={{0,1},{1,0},{2,3},{3,2},{4,5},{5,4},{6,7},{7,6},{8,9},{9,8},{10,11... | collective-permute-start | bytes 1327112 | tf_op jit(solution)/shard_map/ppermute | solution.py:165
  416.0 6.1 %collective-permute-done.53 = bf16[1,272,384]{2,1,0:T(8,128)(2,1)S(1)} collective-permute-done((bf16[1,272,384]{2,1,0:T(8,128)(2,1)S(1)}, bf16[1,272,384]{2,1,0:T(8,128)(2,1)S(1)}, u32[]{:S(2)}, u32[]{:S(2)}) %collective-permute-start.53) | collective-permute-done | bytes 208928 | tf_op jit(solution)/shard_map/ppermute | solution.py:165
  425.5 2.0 copy.52
  427.5 2.7 copy.53
  430.2 2.9 reshape.343
  (334 shorter events, 101.3 us)
Async XLA Ops:
  7.6 35.4 %collective-permute-start.17 = (bf16[136,768]{1,0:T(8,128)(2,1)}, bf16[136,768]{1,0:T(8,128)(2,1)}, u32[]{:S(2)}, u32[]{:S(2)}) collective-permute-start(bf16[136,768]{1,0:T(8,128)(2,1)} %get-tuple-element.141), channel_id=1, source_target_pairs={{0,24},{8,16},{16,8},{24,0},{1,25},{9,17},{17,9},{25,1},{2,26},{10... | collective-permute-start | bytes 626696 | tf_op jit(solution)/shard_map/ppermute | solution.py:165
  11.8 32.4 %collective-permute-start.16 = (bf16[136,768]{1,0:T(8,128)(2,1)}, bf16[136,768]{1,0:T(8,128)(2,1)}, u32[]{:S(2)}, u32[]{:S(2)}) collective-permute-start(bf16[136,768]{1,0:T(8,128)(2,1)} %get-tuple-element.141), channel_id=1, source_target_pairs={{0,16},{8,24},{16,0},{24,8},{1,17},{9,25},{17,1},{25,9},{2,18},{10... | collective-permute-start | bytes 626696 | tf_op jit(solution)/shard_map/ppermute | solution.py:165
  11.8 9.3 %collective-permute-start.8 = (bf16[2,192]{1,0:T(2,128)(2,1)S(1)}, bf16[2,192]{1,0:T(2,128)(2,1)S(1)}, u32[]{:S(2)}, u32[]{:S(2)}) collective-permute-start(bf16[2,192]{1,0:T(2,128)(2,1)S(1)} %pad_maximum_fusion.33), channel_id=1, source_target_pairs={{0,24},{8,16},{16,8},{24,0},{1,25},{9,17},{17,9},{25,1},{2,26},{10... | collective-permute-start | bytes 2312 | tf_op jit(solution)/shard_map/ppermute | solution.py:165
  13.2 18.6 %collective-permute-start.7 = (bf16[2,192]{1,0:T(2,128)(2,1)S(1)}, bf16[2,192]{1,0:T(2,128)(2,1)S(1)}, u32[]{:S(2)}, u32[]{:S(2)}) collective-permute-start(bf16[2,192]{1,0:T(2,128)(2,1)S(1)} %pad_maximum_fusion.33), channel_id=1, source_target_pairs={{0,16},{8,24},{16,0},{24,8},{1,17},{9,25},{17,1},{25,9},{2,18},{10... | collective-permute-start | bytes 2312 | tf_op jit(solution)/shard_map/ppermute | solution.py:165
  14.3 18.6 %collective-permute-start.6 = (bf16[2,192]{1,0:T(2,128)(2,1)S(1)}, bf16[2,192]{1,0:T(2,128)(2,1)S(1)}, u32[]{:S(2)}, u32[]{:S(2)}) collective-permute-start(bf16[2,192]{1,0:T(2,128)(2,1)S(1)} %pad_maximum_fusion.33), channel_id=1, source_target_pairs={{0,8},{8,0},{16,24},{24,16},{1,9},{9,1},{17,25},{25,17},{2,10},{10... | collective-permute-start | bytes 2312 | tf_op jit(solution)/shard_map/ppermute | solution.py:165
  21.2 13.1 %collective-permute-start.2 = (bf16[72,768]{1,0:T(8,128)(2,1)S(1)}, bf16[72,768]{1,0:T(8,128)(2,1)S(1)}, u32[]{:S(2)}, u32[]{:S(2)}) collective-permute-start(bf16[72,768]{1,0:T(8,128)(2,1)S(1)} %fusion.77), channel_id=1, source_target_pairs={{0,24},{8,16},{16,8},{24,0},{1,25},{9,17},{17,9},{25,1},{2,26},{10... | collective-permute-start | bytes 331784 | tf_op jit(solution)/shard_map/ppermute | solution.py:165
  31.9 6.1 %collective-permute-start.1 = (bf16[72,768]{1,0:T(8,128)(2,1)S(1)}, bf16[72,768]{1,0:T(8,128)(2,1)S(1)}, u32[]{:S(2)}, u32[]{:S(2)}) collective-permute-start(bf16[72,768]{1,0:T(8,128)(2,1)S(1)} %fusion.77), channel_id=1, source_target_pairs={{0,16},{8,24},{16,0},{24,8},{1,17},{9,25},{17,1},{25,9},{2,18},{10... | collective-permute-start | bytes 331784 | tf_op jit(solution)/shard_map/ppermute | solution.py:165
  32.9 5.9 %collective-permute-start = (bf16[72,768]{1,0:T(8,128)(2,1)S(1)}, bf16[72,768]{1,0:T(8,128)(2,1)S(1)}, u32[]{:S(2)}, u32[]{:S(2)}) collective-permute-start(bf16[72,768]{1,0:T(8,128)(2,1)S(1)} %fusion.77), channel_id=1, source_target_pairs={{0,8},{8,0},{16,24},{24,16},{1,9},{9,1},{17,25},{25,17},{2,10},{10... | collective-permute-start | bytes 331784 | tf_op jit(solution)/shard_map/ppermute | solution.py:165
  34.2 10.0 %collective-permute-start.15 = (bf16[136,768]{1,0:T(8,128)(2,1)}, bf16[136,768]{1,0:T(8,128)(2,1)S(1)}, u32[]{:S(2)}, u32[]{:S(2)}) collective-permute-start(bf16[136,768]{1,0:T(8,128)(2,1)} %get-tuple-element.141), channel_id=1, source_target_pairs={{0,8},{8,0},{16,24},{24,16},{1,9},{9,1},{17,25},{25,17},{2,10},{10... | collective-permute-start | bytes 626696 | tf_op jit(solution)/shard_map/ppermute | solution.py:165
  38.0 39.0 %collective-permute-start.9 = (bf16[512,768]{1,0:T(8,128)(2,1)S(1)}, bf16[512,768]{1,0:T(8,128)(2,1)S(1)}, u32[]{:S(2)}, u32[]{:S(2)}) collective-permute-start(bf16[512,768]{1,0:T(8,128)(2,1)S(1)} %bitcast.170), channel_id=1, source_target_pairs={{0,8},{8,0},{16,24},{24,16},{1,9},{9,1},{17,25},{25,17},{2,10},{10... | collective-permute-start | bytes 2359304 | tf_op jit(solution)/shard_map/ppermute | solution.py:165
  38.8 39.6 %collective-permute-start.10 = (bf16[512,768]{1,0:T(8,128)(2,1)S(1)}, bf16[512,768]{1,0:T(8,128)(2,1)}, u32[]{:S(2)}, u32[]{:S(2)}) collective-permute-start(bf16[512,768]{1,0:T(8,128)(2,1)S(1)} %bitcast.171), channel_id=1, source_target_pairs={{0,16},{8,24},{16,0},{24,8},{1,17},{9,25},{17,1},{25,9},{2,18},{10... | collective-permute-start | bytes 2359304 | tf_op jit(solution)/shard_map/ppermute | solution.py:165
  43.0 9.3 %collective-permute-start.3 = (bf16[4,72,768]{2,1,0:T(8,128)(2,1)}, bf16[4,72,768]{2,1,0:T(8,128)(2,1)}, u32[]{:S(2)}, u32[]{:S(2)}) collective-permute-start(bf16[4,72,768]{2,1,0:T(8,128)(2,1)} %pad_maximum_fusion.22), channel_id=1, source_target_pairs={{0,2},{1,3},{2,0},{3,1},{4,6},{5,7},{6,4},{7,5},{8,10},{9,11},{10,... | collective-permute-start | bytes 1327112 | tf_op jit(solution)/shard_map/ppermute | solution.py:165
  46.6 13.4 %collective-permute-start.18 = (bf16[4,136,384]{2,1,0:T(8,128)(2,1)}, bf16[4,136,384]{2,1,0:T(8,128)(2,1)}, u32[]{:S(2)}, u32[]{:S(2)}) collective-permute-start(bf16[4,136,384]{2,1,0:T(8,128)(2,1)} %get-tuple-element.94), channel_id=1, source_target_pairs={{0,2},{1,3},{2,0},{3,1},{4,6},{5,7},{6,4},{7,5},{8,10},{9,11},{10,... | collective-permute-start | bytes 1253384 | tf_op jit(solution)/shard_map/ppermute | solution.py:165
  46.9 14.3 %collective-permute-start.20 = (bf16[4,136,384]{2,1,0:T(8,128)(2,1)}, bf16[4,136,384]{2,1,0:T(8,128)(2,1)}, u32[]{:S(2)}, u32[]{:S(2)}) collective-permute-start(bf16[4,136,384]{2,1,0:T(8,128)(2,1)} %get-tuple-element.95), channel_id=1, source_target_pairs={{0,4},{1,5},{2,6},{3,7},{4,0},{5,1},{6,2},{7,3},{8,12},{9,13},{10,... | collective-permute-start | bytes 1253384 | tf_op jit(solution)/shard_map/ppermute | solution.py:165
  52.3 40.2 %collective-permute-start.11 = (bf16[512,768]{1,0:T(8,128)(2,1)S(1)}, bf16[512,768]{1,0:T(8,128)(2,1)S(1)}, u32[]{:S(2)}, u32[]{:S(2)}) collective-permute-start(bf16[512,768]{1,0:T(8,128)(2,1)S(1)} %bitcast.172), channel_id=1, source_target_pairs={{0,24},{8,16},{16,8},{24,0},{1,25},{9,17},{17,9},{25,1},{2,26},{10... | collective-permute-start | bytes 2359304 | tf_op jit(solution)/shard_map/ppermute | solution.py:165
  60.0 34.2 %collective-permute-start.4 = (bf16[4,144,768]{2,1,0:T(8,128)(2,1)S(1)}, bf16[4,144,768]{2,1,0:T(8,128)(2,1)S(1)}, u32[]{:S(2)}, u32[]{:S(2)}) collective-permute-start(bf16[4,144,768]{2,1,0:T(8,128)(2,1)S(1)} %pad_maximum_fusion.12), channel_id=1, source_target_pairs={{0,4},{1,5},{2,6},{3,7},{4,0},{5,1},{6,2},{7,3},{8,12},{9,13},{10,... | collective-permute-start | bytes 2654216 | tf_op jit(solution)/shard_map/ppermute | solution.py:165
  62.6 41.7 %collective-permute-start.21 = (bf16[4,272,384]{2,1,0:T(8,128)(2,1)S(1)}, bf16[4,272,384]{2,1,0:T(8,128)(2,1)S(1)}, u32[]{:S(2)}, u32[]{:S(2)}) collective-permute-start(bf16[4,272,384]{2,1,0:T(8,128)(2,1)S(1)} %pad_maximum_fusion.16), channel_id=1, source_target_pairs={{0,2},{1,3},{2,0},{3,1},{4,6},{5,7},{6,4},{7,5},{8,10},{9,11},{10,... | collective-permute-start | bytes 2506760 | tf_op jit(solution)/shard_map/ppermute | solution.py:165
  77.0 27.7 %collective-permute-start.19 = (bf16[4,272,384]{2,1,0:T(8,128)(2,1)S(1)}, bf16[4,272,384]{2,1,0:T(8,128)(2,1)S(1)}, u32[]{:S(2)}, u32[]{:S(2)}) collective-permute-start(bf16[4,272,384]{2,1,0:T(8,128)(2,1)S(1)} %pad_maximum_fusion.15), channel_id=1, source_target_pairs={{0,4},{1,5},{2,6},{3,7},{4,0},{5,1},{6,2},{7,3},{8,12},{9,13},{10,... | collective-permute-start | bytes 2506760 | tf_op jit(solution)/shard_map/ppermute | solution.py:165
  94.7 15.3 %collective-permute-start.5 = (bf16[4,288,768]{2,1,0:T(8,128)(2,1)S(1)}, bf16[4,288,768]{2,1,0:T(8,128)(2,1)S(1)}, u32[]{:S(2)}, u32[]{:S(2)}) collective-permute-start(bf16[4,288,768]{2,1,0:T(8,128)(2,1)S(1)} %pad_maximum_fusion.5), channel_id=1, source_target_pairs={{0,1},{1,0},{2,3},{3,2},{4,5},{5,4},{6,7},{7,6},{8,9},{9,8},{10,11... | collective-permute-start | bytes 5308424 | tf_op jit(solution)/shard_map/ppermute | solution.py:165
  107.3 87.9 %collective-permute-start.22 = (bf16[4,544,768]{2,1,0:T(8,128)(2,1)}, bf16[4,544,768]{2,1,0:T(8,128)(2,1)}, u32[]{:S(2)}, u32[]{:S(2)}) collective-permute-start(bf16[4,544,768]{2,1,0:T(8,128)(2,1)} %maximum_maximum_fusion), channel_id=1, source_target_pairs={{0,1},{1,0},{2,3},{3,2},{4,5},{5,4},{6,7},{7,6},{8,9},{9,8},{10,11... | collective-permute-start | bytes 10027016 | tf_op jit(solution)/shard_map/ppermute | solution.py:165
  167.9 33.5 %collective-permute-start.14 = (bf16[192,512]{1,0:T(8,128)(2,1)}, bf16[192,512]{1,0:T(8,128)(2,1)}, u32[]{:S(2)}, u32[]{:S(2)}) collective-permute-start(bf16[192,512]{1,0:T(8,128)(2,1)} %get-tuple-element.117), channel_id=1, source_target_pairs={{0,24},{8,16},{16,8},{24,0},{1,25},{9,17},{17,9},{25,1},{2,26},{10... | collective-permute-start | bytes 589832 | tf_op jit(solution)/shard_map/ppermute | solution.py:165
  168.5 33.0 %collective-permute-start.13 = (bf16[192,512]{1,0:T(8,128)(2,1)S(1)}, bf16[192,512]{1,0:T(8,128)(2,1)}, u32[]{:S(2)}, u32[]{:S(2)}) collective-permute-start(bf16[192,512]{1,0:T(8,128)(2,1)S(1)} %get-tuple-element.118), channel_id=1, source_target_pairs={{0,16},{8,24},{16,0},{24,8},{1,17},{9,25},{17,1},{25,9},{2,18},{10... | collective-permute-start | bytes 589832 | tf_op jit(solution)/shard_map/ppermute | solution.py:165
  178.7 22.8 %collective-permute-start.12 = (bf16[192,512]{1,0:T(8,128)(2,1)S(1)}, bf16[192,512]{1,0:T(8,128)(2,1)}, u32[]{:S(2)}, u32[]{:S(2)}) collective-permute-start(bf16[192,512]{1,0:T(8,128)(2,1)S(1)} %get-tuple-element.119), channel_id=1, source_target_pairs={{0,8},{8,0},{16,24},{24,16},{1,9},{9,1},{17,25},{25,17},{2,10},{10... | collective-permute-start | bytes 589832 | tf_op jit(solution)/shard_map/ppermute | solution.py:165
  224.4 12.1 %collective-permute-start.25 = (bf16[192,512]{1,0:T(8,128)(2,1)S(1)}, bf16[192,512]{1,0:T(8,128)(2,1)S(1)}, u32[]{:S(2)}, u32[]{:S(2)}) collective-permute-start(bf16[192,512]{1,0:T(8,128)(2,1)S(1)} %get-tuple-element.113), channel_id=1, source_target_pairs={{0,24},{8,16},{16,8},{24,0},{1,25},{9,17},{17,9},{25,1},{2,26},{10... | collective-permute-start | bytes 589832 | tf_op jit(solution)/shard_map/ppermute | solution.py:165
  226.5 17.9 %collective-permute-start.24 = (bf16[192,512]{1,0:T(8,128)(2,1)S(1)}, bf16[192,512]{1,0:T(8,128)(2,1)S(1)}, u32[]{:S(2)}, u32[]{:S(2)}) collective-permute-start(bf16[192,512]{1,0:T(8,128)(2,1)S(1)} %get-tuple-element.114), channel_id=1, source_target_pairs={{0,16},{8,24},{16,0},{24,8},{1,17},{9,25},{17,1},{25,9},{2,18},{10... | collective-permute-start | bytes 589832 | tf_op jit(solution)/shard_map/ppermute | solution.py:165
  227.1 17.3 %collective-permute-start.23 = (bf16[192,512]{1,0:T(8,128)(2,1)S(1)}, bf16[192,512]{1,0:T(8,128)(2,1)S(1)}, u32[]{:S(2)}, u32[]{:S(2)}) collective-permute-start(bf16[192,512]{1,0:T(8,128)(2,1)S(1)} %get-tuple-element.115), channel_id=1, source_target_pairs={{0,8},{8,0},{16,24},{24,16},{1,9},{9,1},{17,25},{25,17},{2,10},{10... | collective-permute-start | bytes 589832 | tf_op jit(solution)/shard_map/ppermute | solution.py:165
  234.6 113.0 %collective-permute-start.44 = (bf16[4,544,768]{2,1,0:T(8,128)(2,1)}, bf16[4,544,768]{2,1,0:T(8,128)(2,1)}, u32[]{:S(2)}, u32[]{:S(2)}) collective-permute-start(bf16[4,544,768]{2,1,0:T(8,128)(2,1)} %constant_dynamic-slice_fusion.4), channel_id=1, source_target_pairs={{0,1},{1,0},{2,3},{3,2},{4,5},{5,4},{6,7},{7,6},{8,9},{9,8},{10,11... | collective-permute-start | bytes 10027016 | tf_op jit(solution)/shard_map/ppermute | solution.py:165
  284.1 9.0 %collective-permute-start.26 = (bf16[192,512]{1,0:T(8,128)(2,1)S(1)}, bf16[192,512]{1,0:T(8,128)(2,1)S(1)}, u32[]{:S(2)}, u32[]{:S(2)}) collective-permute-start(bf16[192,512]{1,0:T(8,128)(2,1)S(1)} %get-tuple-element.110), channel_id=1, source_target_pairs={{0,8},{8,0},{16,24},{24,16},{1,9},{9,1},{17,25},{25,17},{2,10},{10... | collective-permute-start | bytes 589832 | tf_op jit(solution)/shard_map/ppermute | solution.py:165
  284.2 9.0 %collective-permute-start.27 = (bf16[192,512]{1,0:T(8,128)(2,1)S(1)}, bf16[192,512]{1,0:T(8,128)(2,1)S(1)}, u32[]{:S(2)}, u32[]{:S(2)}) collective-permute-start(bf16[192,512]{1,0:T(8,128)(2,1)S(1)} %get-tuple-element.109), channel_id=1, source_target_pairs={{0,16},{8,24},{16,0},{24,8},{1,17},{9,25},{17,1},{25,9},{2,18},{10... | collective-permute-start | bytes 589832 | tf_op jit(solution)/shard_map/ppermute | solution.py:165
  286.5 12.2 %collective-permute-start.28 = (bf16[192,512]{1,0:T(8,128)(2,1)S(1)}, bf16[192,512]{1,0:T(8,128)(2,1)S(1)}, u32[]{:S(2)}, u32[]{:S(2)}) collective-permute-start(bf16[192,512]{1,0:T(8,128)(2,1)S(1)} %get-tuple-element.108), channel_id=1, source_target_pairs={{0,24},{8,16},{16,8},{24,0},{1,25},{9,17},{17,9},{25,1},{2,26},{10... | collective-permute-start | bytes 589832 | tf_op jit(solution)/shard_map/ppermute | solution.py:165
  287.7 15.8 %copy-start.39 = (bf16[512,768]{1,0:T(8,128)(2,1)S(1)}, bf16[512,768]{1,0:T(8,128)(2,1)}, u32[]{:S(2)}) copy-start(bf16[512,768]{1,0:T(8,128)(2,1)} %copy-done.37) | copy-start | bytes 2359300
  288.0 15.6 %copy-start.30 = (bf16[512,768]{1,0:T(8,128)(2,1)S(1)}, bf16[512,768]{1,0:T(8,128)(2,1)}, u32[]{:S(2)}) copy-start(bf16[512,768]{1,0:T(8,128)(2,1)} %copy-done.27) | copy-start | bytes 2359300
  288.0 15.6 %copy-start.33 = (bf16[512,768]{1,0:T(8,128)(2,1)S(1)}, bf16[512,768]{1,0:T(8,128)(2,1)}, u32[]{:S(2)}) copy-start(bf16[512,768]{1,0:T(8,128)(2,1)} %copy-done.31) | copy-start | bytes 2359300
  298.9 13.5 %collective-permute-start.29 = (bf16[192,512]{1,0:T(8,128)(2,1)S(1)}, bf16[192,512]{1,0:T(8,128)(2,1)S(1)}, u32[]{:S(2)}, u32[]{:S(2)}) collective-permute-start(bf16[192,512]{1,0:T(8,128)(2,1)S(1)} %get-tuple-element.106), channel_id=1, source_target_pairs={{0,8},{8,0},{16,24},{24,16},{1,9},{9,1},{17,25},{25,17},{2,10},{10... | collective-permute-start | bytes 589832 | tf_op jit(solution)/shard_map/ppermute | solution.py:165
  306.4 14.8 %collective-permute-start.30 = (bf16[192,512]{1,0:T(8,128)(2,1)S(1)}, bf16[192,512]{1,0:T(8,128)(2,1)S(1)}, u32[]{:S(2)}, u32[]{:S(2)}) collective-permute-start(bf16[192,512]{1,0:T(8,128)(2,1)S(1)} %get-tuple-element.105), channel_id=1, source_target_pairs={{0,16},{8,24},{16,0},{24,8},{1,17},{9,25},{17,1},{25,9},{2,18},{10... | collective-permute-start | bytes 589832 | tf_op jit(solution)/shard_map/ppermute | solution.py:165
  308.8 20.9 %collective-permute-start.35 = (bf16[4,96,576]{2,1,0:T(8,128)(2,1)S(1)}, bf16[4,96,576]{2,1,0:T(8,128)(2,1)S(1)}, u32[]{:S(2)}, u32[]{:S(2)}) collective-permute-start(bf16[4,96,576]{2,1,0:T(8,128)(2,1)S(1)} %constant_dynamic-slice_fusion.16), channel_id=1, source_target_pairs={{0,1},{1,0},{2,3},{3,2},{4,5},{5,4},{6,7},{7,6},{8,9},{9,8},{10,11... | collective-permute-start | bytes 1327112 | tf_op jit(solution)/shard_map/ppermute | solution.py:165
  311.2 10.7 %collective-permute-start.31 = (bf16[192,512]{1,0:T(8,128)(2,1)S(1)}, bf16[192,512]{1,0:T(8,128)(2,1)S(1)}, u32[]{:S(2)}, u32[]{:S(2)}) collective-permute-start(bf16[192,512]{1,0:T(8,128)(2,1)S(1)} %get-tuple-element.104), channel_id=1, source_target_pairs={{0,24},{8,16},{16,8},{24,0},{1,25},{9,17},{17,9},{25,1},{2,26},{10... | collective-permute-start | bytes 589832 | tf_op jit(solution)/shard_map/ppermute | solution.py:165
  322.6 19.4 %copy-start.25 = (bf16[4,3,64,768]{3,2,1,0:T(8,128)(2,1)S(1)}, bf16[4,3,64,768]{3,2,1,0:T(8,128)(2,1)}, u32[]{:S(2)}) copy-start(bf16[4,3,64,768]{3,2,1,0:T(8,128)(2,1)} %pad_maximum_fusion.9) | copy-start | bytes 3538948
  323.4 18.6 %copy-start.7 = (bf16[1,512,768]{2,1,0:T(8,128)(2,1)S(1)}, bf16[1,512,768]{2,1,0:T(8,128)(2,1)}, u32[]{:S(2)}) copy-start(bf16[1,512,768]{2,1,0:T(8,128)(2,1)} %param.8) | copy-start | bytes 2359300
  323.4 18.6 %copy-start.23 = (bf16[4,3,64,768]{3,2,1,0:T(8,128)(2,1)S(1)}, bf16[4,3,64,768]{3,2,1,0:T(8,128)(2,1)}, u32[]{:S(2)}) copy-start(bf16[4,3,64,768]{3,2,1,0:T(8,128)(2,1)} %pad_maximum_fusion.11) | copy-start | bytes 3538948
  323.4 18.6 %copy-start.24 = (bf16[4,3,64,768]{3,2,1,0:T(8,128)(2,1)S(1)}, bf16[4,3,64,768]{3,2,1,0:T(8,128)(2,1)}, u32[]{:S(2)}) copy-start(bf16[4,3,64,768]{3,2,1,0:T(8,128)(2,1)} %pad_maximum_fusion.10) | copy-start | bytes 3538948
  323.4 7.8 %collective-permute-start.32 = (bf16[192,512]{1,0:T(8,128)(2,1)S(1)}, bf16[192,512]{1,0:T(8,128)(2,1)S(1)}, u32[]{:S(2)}, u32[]{:S(2)}) collective-permute-start(bf16[192,512]{1,0:T(8,128)(2,1)S(1)} %get-tuple-element.102), channel_id=1, source_target_pairs={{0,8},{8,0},{16,24},{24,16},{1,9},{9,1},{17,25},{25,17},{2,10},{10... | collective-permute-start | bytes 589832 | tf_op jit(solution)/shard_map/ppermute | solution.py:165
  327.2 6.5 %collective-permute-start.33 = (bf16[192,512]{1,0:T(8,128)(2,1)S(1)}, bf16[192,512]{1,0:T(8,128)(2,1)S(1)}, u32[]{:S(2)}, u32[]{:S(2)}) collective-permute-start(bf16[192,512]{1,0:T(8,128)(2,1)S(1)} %get-tuple-element.101), channel_id=1, source_target_pairs={{0,16},{8,24},{16,0},{24,8},{1,17},{9,25},{17,1},{25,9},{2,18},{10... | collective-permute-start | bytes 589832 | tf_op jit(solution)/shard_map/ppermute | solution.py:165
  328.6 12.7 %collective-permute-start.34 = (bf16[192,512]{1,0:T(8,128)(2,1)S(1)}, bf16[192,512]{1,0:T(8,128)(2,1)S(1)}, u32[]{:S(2)}, u32[]{:S(2)}) collective-permute-start(bf16[192,512]{1,0:T(8,128)(2,1)S(1)} %get-tuple-element.100), channel_id=1, source_target_pairs={{0,24},{8,16},{16,8},{24,0},{1,25},{9,17},{17,9},{25,1},{2,26},{10... | collective-permute-start | bytes 589832 | tf_op jit(solution)/shard_map/ppermute | solution.py:165
  329.9 16.4 %collective-permute-start.36 = (bf16[4,48,576]{2,1,0:T(8,128)(2,1)S(1)}, bf16[4,48,576]{2,1,0:T(8,128)(2,1)S(1)}, u32[]{:S(2)}, u32[]{:S(2)}) collective-permute-start(bf16[4,48,576]{2,1,0:T(8,128)(2,1)S(1)} %constant_dynamic-slice_fusion.15), channel_id=1, source_target_pairs={{0,4},{1,5},{2,6},{3,7},{4,0},{5,1},{6,2},{7,3},{8,12},{9,13},{10,... | collective-permute-start | bytes 663560 | tf_op jit(solution)/shard_map/ppermute | solution.py:165
  346.3 5.9 %collective-permute-start.37 = (bf16[4,24,576]{2,1,0:T(8,128)(2,1)S(1)}, bf16[4,24,576]{2,1,0:T(8,128)(2,1)S(1)}, u32[]{:S(2)}, u32[]{:S(2)}) collective-permute-start(bf16[4,24,576]{2,1,0:T(8,128)(2,1)S(1)} %constant_dynamic-slice_fusion.14), channel_id=1, source_target_pairs={{0,2},{1,3},{2,0},{3,1},{4,6},{5,7},{6,4},{7,5},{8,10},{9,11},{10,... | collective-permute-start | bytes 331784 | tf_op jit(solution)/shard_map/ppermute | solution.py:165
  350.9 14.5 %collective-permute-start.45 = (bf16[4,272,384]{2,1,0:T(8,128)(2,1)S(1)}, bf16[4,272,384]{2,1,0:T(8,128)(2,1)S(1)}, u32[]{:S(2)}, u32[]{:S(2)}) collective-permute-start(bf16[4,272,384]{2,1,0:T(8,128)(2,1)S(1)} %constant_dynamic-slice_fusion.3), channel_id=1, source_target_pairs={{0,4},{1,5},{2,6},{3,7},{4,0},{5,1},{6,2},{7,3},{8,12},{9,13},{10,... | collective-permute-start | bytes 2506760 | tf_op jit(solution)/shard_map/ppermute | solution.py:165
  352.3 9.1 %collective-permute-start.40 = (bf16[24,576]{1,0:T(8,128)(2,1)S(1)}, bf16[24,576]{1,0:T(8,128)(2,1)S(1)}, u32[]{:S(2)}, u32[]{:S(2)}) collective-permute-start(bf16[24,576]{1,0:T(8,128)(2,1)S(1)} %get-tuple-element.147), channel_id=1, source_target_pairs={{0,24},{8,16},{16,8},{24,0},{1,25},{9,17},{17,9},{25,1},{2,26},{10... | collective-permute-start | bytes 82952 | tf_op jit(solution)/shard_map/ppermute | solution.py:165
  356.4 5.0 %collective-permute-start.39 = (bf16[24,576]{1,0:T(8,128)(2,1)S(1)}, bf16[24,576]{1,0:T(8,128)(2,1)S(1)}, u32[]{:S(2)}, u32[]{:S(2)}) collective-permute-start(bf16[24,576]{1,0:T(8,128)(2,1)S(1)} %get-tuple-element.148), channel_id=1, source_target_pairs={{0,16},{8,24},{16,0},{24,8},{1,17},{9,25},{17,1},{25,9},{2,18},{10... | collective-permute-start | bytes 82952 | tf_op jit(solution)/shard_map/ppermute | solution.py:165
  359.1 3.0 collective-permute-start.38
  359.4 16.8 %collective-permute-start.47 = (bf16[4,272,384]{2,1,0:T(8,128)(2,1)S(1)}, bf16[4,272,384]{2,1,0:T(8,128)(2,1)S(1)}, u32[]{:S(2)}, u32[]{:S(2)}) collective-permute-start(bf16[4,272,384]{2,1,0:T(8,128)(2,1)S(1)} %constant_dynamic-slice_fusion.1), channel_id=1, source_target_pairs={{0,2},{1,3},{2,0},{3,1},{4,6},{5,7},{6,4},{7,5},{8,10},{9,11},{10,... | collective-permute-start | bytes 2506760 | tf_op jit(solution)/shard_map/ppermute | solution.py:165
  365.7 19.5 %collective-permute-start.46 = (bf16[4,136,384]{2,1,0:T(8,128)(2,1)S(1)}, bf16[4,136,384]{2,1,0:T(8,128)(2,1)S(1)}, u32[]{:S(2)}, u32[]{:S(2)}) collective-permute-start(bf16[4,136,384]{2,1,0:T(8,128)(2,1)S(1)} %constant_dynamic-slice_fusion.2), channel_id=1, source_target_pairs={{0,2},{1,3},{2,0},{3,1},{4,6},{5,7},{6,4},{7,5},{8,10},{9,11},{10,... | collective-permute-start | bytes 1253384 | tf_op jit(solution)/shard_map/ppermute | solution.py:165
  376.5 8.8 %collective-permute-start.48 = (bf16[4,136,384]{2,1,0:T(8,128)(2,1)S(1)}, bf16[4,136,384]{2,1,0:T(8,128)(2,1)S(1)}, u32[]{:S(2)}, u32[]{:S(2)}) collective-permute-start(bf16[4,136,384]{2,1,0:T(8,128)(2,1)S(1)} %constant_dynamic-slice_fusion), channel_id=1, source_target_pairs={{0,4},{1,5},{2,6},{3,7},{4,0},{5,1},{6,2},{7,3},{8,12},{9,13},{10,... | collective-permute-start | bytes 1253384 | tf_op jit(solution)/shard_map/ppermute | solution.py:165
  376.8 12.3 %collective-permute-start.41 = (bf16[4,24,576]{2,1,0:T(8,128)(2,1)S(1)}, bf16[4,24,576]{2,1,0:T(8,128)(2,1)S(1)}, u32[]{:S(2)}, u32[]{:S(2)}) collective-permute-start(bf16[4,24,576]{2,1,0:T(8,128)(2,1)S(1)} %pad_maximum_fusion.30), channel_id=1, source_target_pairs={{0,2},{1,3},{2,0},{3,1},{4,6},{5,7},{6,4},{7,5},{8,10},{9,11},{10,... | collective-permute-start | bytes 331784 | tf_op jit(solution)/shard_map/ppermute | solution.py:165
  385.5 6.7 %collective-permute-start.51 = (bf16[136,768]{1,0:T(8,128)(2,1)S(1)}, bf16[136,768]{1,0:T(8,128)(2,1)S(1)}, u32[]{:S(2)}, u32[]{:S(2)}) collective-permute-start(bf16[136,768]{1,0:T(8,128)(2,1)S(1)} %get-tuple-element.91), channel_id=1, source_target_pairs={{0,24},{8,16},{16,8},{24,0},{1,25},{9,17},{17,9},{25,1},{2,26},{10... | collective-permute-start | bytes 626696 | tf_op jit(solution)/shard_map/ppermute | solution.py:165
  388.0 16.2 %collective-permute-start.50 = (bf16[136,768]{1,0:T(8,128)(2,1)S(1)}, bf16[136,768]{1,0:T(8,128)(2,1)S(1)}, u32[]{:S(2)}, u32[]{:S(2)}) collective-permute-start(bf16[136,768]{1,0:T(8,128)(2,1)S(1)} %get-tuple-element.90), channel_id=1, source_target_pairs={{0,16},{8,24},{16,0},{24,8},{1,17},{9,25},{17,1},{25,9},{2,18},{10... | collective-permute-start | bytes 626696 | tf_op jit(solution)/shard_map/ppermute | solution.py:165
  388.4 15.9 %collective-permute-start.49 = (bf16[136,768]{1,0:T(8,128)(2,1)S(1)}, bf16[136,768]{1,0:T(8,128)(2,1)S(1)}, u32[]{:S(2)}, u32[]{:S(2)}) collective-permute-start(bf16[136,768]{1,0:T(8,128)(2,1)S(1)} %get-tuple-element.89), channel_id=1, source_target_pairs={{0,8},{8,0},{16,24},{24,16},{1,9},{9,1},{17,25},{25,17},{2,10},{10... | collective-permute-start | bytes 626696 | tf_op jit(solution)/shard_map/ppermute | solution.py:165
  389.2 16.8 %collective-permute-start.42 = (bf16[4,48,576]{2,1,0:T(8,128)(2,1)S(1)}, bf16[4,48,576]{2,1,0:T(8,128)(2,1)S(1)}, u32[]{:S(2)}, u32[]{:S(2)}) collective-permute-start(bf16[4,48,576]{2,1,0:T(8,128)(2,1)S(1)} %pad_maximum_fusion.23), channel_id=1, source_target_pairs={{0,4},{1,5},{2,6},{3,7},{4,0},{5,1},{6,2},{7,3},{8,12},{9,13},{10,... | collective-permute-start | bytes 663560 | tf_op jit(solution)/shard_map/ppermute | solution.py:165
  404.4 3.6 collective-permute-start.52
  404.7 3.5 collective-permute-start.54
  408.4 7.5 %collective-permute-start.55 = (bf16[1,272,384]{2,1,0:T(8,128)(2,1)S(1)}, bf16[1,272,384]{2,1,0:T(8,128)(2,1)S(1)}, u32[]{:S(2)}, u32[]{:S(2)}) collective-permute-start(bf16[1,272,384]{2,1,0:T(8,128)(2,1)S(1)} %pad_maximum_fusion.26), channel_id=1, source_target_pairs={{0,2},{1,3},{2,0},{3,1},{4,6},{5,7},{6,4},{7,5},{8,10},{9,11},{10,... | collective-permute-start | bytes 626696 | tf_op jit(solution)/shard_map/ppermute | solution.py:165
  409.7 14.2 %collective-permute-start.43 = (bf16[4,96,576]{2,1,0:T(8,128)(2,1)S(1)}, bf16[4,96,576]{2,1,0:T(8,128)(2,1)S(1)}, u32[]{:S(2)}, u32[]{:S(2)}) collective-permute-start(bf16[4,96,576]{2,1,0:T(8,128)(2,1)S(1)} %pad_maximum_fusion.19), channel_id=1, source_target_pairs={{0,1},{1,0},{2,3},{3,2},{4,5},{5,4},{6,7},{7,6},{8,9},{9,8},{10,11... | collective-permute-start | bytes 1327112 | tf_op jit(solution)/shard_map/ppermute | solution.py:165
  415.2 6.8 %collective-permute-start.53 = (bf16[1,272,384]{2,1,0:T(8,128)(2,1)S(1)}, bf16[1,272,384]{2,1,0:T(8,128)(2,1)S(1)}, u32[]{:S(2)}, u32[]{:S(2)}) collective-permute-start(bf16[1,272,384]{2,1,0:T(8,128)(2,1)S(1)} %pad_maximum_fusion.25), channel_id=1, source_target_pairs={{0,4},{1,5},{2,6},{3,7},{4,0},{5,1},{6,2},{7,3},{8,12},{9,13},{10,... | collective-permute-start | bytes 626696 | tf_op jit(solution)/shard_map/ppermute | solution.py:165
  423.1 11.0 %collective-permute-start.56 = (bf16[1,544,768]{2,1,0:T(8,128)(2,1)}, bf16[1,544,768]{2,1,0:T(8,128)(2,1)}, u32[]{:S(2)}, u32[]{:S(2)}) collective-permute-start(bf16[1,544,768]{2,1,0:T(8,128)(2,1)} %maximum_maximum_fusion.1), channel_id=1, source_target_pairs={{0,1},{1,0},{2,3},{3,2},{4,5},{5,4},{6,7},{7,6},{8,9},{9,8},{10,11... | collective-permute-start | bytes 2506760 | tf_op jit(solution)/shard_map/ppermute | solution.py:165
  (40 other events, 196.8 us)

commit v2 on v1

v2 whole, which is shorter than its diff:
```python
import functools
import math

import jax
import jax.numpy as jnp
from jax import lax
from jax.experimental import pallas as pl
from jax.experimental.pallas import tpu as pltpu
from jax.sharding import PartitionSpec as P

HEADS = 12
HEAD_DIM = 64
HALF = HEAD_DIM // 2
SCALE = 1.0 / math.sqrt(HEAD_DIM)
EPS = 1e-05
THETA = 160000.0
F32 = jnp.float32
BF16 = jnp.bfloat16
NN = (((1,), (0,)), ((), ()))
NT = (((1,), (1,)), ((), ()))
TN = (((0,), (0,)), ((), ()))
TT = (((0,), (1,)), ((), ()))


def mul(a, b, dims=NN):
    return lax.dot_general(a, b, dims, preferred_element_type=F32)


def layer_norm(values, gain):
    centre = values - jnp.mean(values, axis=-1, keepdims=True)
    spread = jnp.mean(centre * centre, axis=-1, keepdims=True)
    return centre * lax.rsqrt(spread + EPS) * gain


def layer_norm_back(values, gain, grad):
    centre = values - jnp.mean(values, axis=-1, keepdims=True)
    inverse = lax.rsqrt(jnp.mean(centre * centre, axis=-1, keepdims=True) + EPS)
    unit = centre * inverse
    scaled = grad * gain
    first = jnp.mean(scaled, axis=-1, keepdims=True)
    second = jnp.mean(scaled * unit, axis=-1, keepdims=True)
    return inverse * (scaled - first - unit * second)


def geglu(inner):
    width = inner.shape[-1] // 2
    return jax.nn.gelu(inner[:, :width], approximate=False) * inner[:, width:]


def rounded(values):
    return lax.optimization_barrier(values.astype(BF16)).astype(F32)


def attend_kernel(q_ref, k_ref, v_ref, out_ref, log_ref):
    scores = mul(k_ref[0], q_ref[...])
    highest = jnp.max(scores, axis=0, keepdims=True)
    raised = jnp.exp(scores - highest)
    total = jnp.sum(raised, axis=0, keepdims=True)
    mixed = mul(v_ref[...], raised.astype(BF16))
    out_ref[...] = (mixed / total).astype(BF16)
    log_ref[...] = highest + jnp.log(total)


def attend(head, queries, keys, values, step=256):
    count = queries.shape[1]
    return pl.pallas_call(
        attend_kernel,
        grid=(count // step,),
        in_specs=[
            pl.BlockSpec((HEAD_DIM, step), lambda i: (head, i)),
            pl.BlockSpec((1, count, HEAD_DIM), lambda i: (head, 0, 0)),
            pl.BlockSpec((HEAD_DIM, count), lambda i: (head, 0)),
        ],
        out_specs=[
            pl.BlockSpec((HEAD_DIM, step), lambda i: (0, i)),
            pl.BlockSpec((1, step), lambda i: (0, i)),
        ],
        out_shape=[
            jax.ShapeDtypeStruct((HEAD_DIM, count), BF16),
            jax.ShapeDtypeStruct((1, count), F32),
        ],
        compiler_params=pltpu.CompilerParams(vmem_limit_bytes=48 * 2**20),
        cost_estimate=pl.CostEstimate(
            flops=40 * count * count * HEAD_DIM,
            bytes_accessed=8 * HEAD_DIM * count,
            transcendentals=count * count,
        ),
        name="attend",
    )(queries, keys, values)


def turn_back(values, cosine, sine):
    first, second = values[:HALF], values[HALF:]
    return jnp.concatenate([first * cosine + second * sine, second * cosine - first * sine], axis=0)


def attend_back_kernel(
    q_ref, kt_ref, k_ref, v_ref, up_ref, out_ref, log_ref, cos_ref, sin_ref, grad_ref, dk_ref, dv_ref
):
    index = pl.program_id(0)
    step = q_ref.shape[1]

    @pl.when(index == 0)
    def _():
        dk_ref[...] = jnp.zeros_like(dk_ref)
        dv_ref[...] = jnp.zeros_like(dv_ref)

    upstream = up_ref[...]
    inner_sum = jnp.sum(upstream.astype(F32) * out_ref[...].astype(F32), axis=0, keepdims=True)
    chances = jnp.exp(mul(k_ref[0], q_ref[...]) - log_ref[...])
    prob_back = mul(v_ref[0], upstream)
    score_back = (chances * (prob_back - inner_sum)).astype(BF16)
    dv_ref[...] += mul(chances.astype(BF16), upstream, NT)
    dk_ref[...] += mul(score_back, q_ref[...], NT)
    columns = pl.ds(pl.multiple_of(index * step, step), step)
    query_back = mul(kt_ref[...], score_back) * SCALE
    grad_ref[pl.ds(0, HEAD_DIM), columns] = turn_back(
        query_back, cos_ref[:, columns], sin_ref[:, columns]
    ).astype(BF16)

    @pl.when(index == pl.num_programs(0) - 1)
    def _():
        key_back = turn_back(dk_ref[...].T, cos_ref[...], sin_ref[...])
        grad_ref[pl.ds(HEAD_DIM, HEAD_DIM), :] = key_back.astype(BF16)
        grad_ref[pl.ds(2 * HEAD_DIM, HEAD_DIM), :] = dv_ref[...].T.astype(BF16)


def attend_back(head, queries, keys_turned, keys, values, upstream, merged, logs, cosine, sine, step=256):
    count = queries.shape[1]
    some = pl.BlockSpec((HEAD_DIM, step), lambda i: (head, i))
    rows = pl.BlockSpec((1, count, HEAD_DIM), lambda i: (head, 0, 0))
    whole = pl.BlockSpec((HALF, count), lambda i: (0, 0))
    return pl.pallas_call(
        attend_back_kernel,
        grid=(count // step,),
        in_specs=[
            some,
            pl.BlockSpec((HEAD_DIM, count), lambda i: (head, 0)),
            rows,
            rows,
            some,
            some,
            pl.BlockSpec((1, step), lambda i: (0, i)),
            whole,
            whole,
        ],
        out_specs=pl.BlockSpec((3 * HEAD_DIM, count), lambda i: (0, 0)),
        out_shape=jax.ShapeDtypeStruct((3 * HEAD_DIM, count), BF16),
        scratch_shapes=[pltpu.VMEM((count, HEAD_DIM), F32), pltpu.VMEM((count, HEAD_DIM), F32)],
        compiler_params=pltpu.CompilerParams(vmem_limit_bytes=48 * 2**20),
        cost_estimate=pl.CostEstimate(
            flops=56 * count * count * HEAD_DIM,
            bytes_accessed=16 * HEAD_DIM * count,
            transcendentals=count * count,
        ),
        name="attend_back",
    )(queries, keys_turned, keys, values, upstream, merged, logs, cosine, sine)


def after(values, *others):
    return lax.optimization_barrier((values, others))[0]


def swap(values, axis, size, offset):
    return lax.ppermute(values, axis, [(i, i ^ offset) for i in range(size)])


def exchange(pieces, size):
    return [pieces[0]] + [swap(pieces[d], "fsdp", size, d) for d in range(1, size)]


def column(values, size, ranks, pairs):
    full = [
        (z * ranks + r, to * ranks + (r & ~1) + core)
        for z in range(size)
        for r in range(ranks)
        for to, core in pairs(z, r & 1)
    ]
    return lax.ppermute(values, ("fsdp", "rep"), full)


def collect(own, home, size, ranks):
    first = column(
        own, size, ranks, lambda z, c: [(z ^ 1, c) if c == z >> 1 else (z ^ 2, 1 - c)]
    )
    second = column(first, size, ranks, lambda z, c: [] if c == z >> 1 else [(z ^ 1, c)])
    low = jnp.where(home, own, first)
    high = jnp.where(home, first, second)
    pair = jnp.concatenate([low, high], axis=0)
    other = swap(pair, "rep", ranks, 1)
    return pair, other, second


def trade_out(pieces, size, ranks):
    def round_of(k):
        return lambda z, c: [((2 * c + (z & 1)) ^ k, z >> 1)]

    return [column(pieces[k], size, ranks, round_of(k)) for k in range(size)]


def trade_back(pieces, size, ranks):
    def round_of(k):
        return lambda z, c: [(2 * c + ((z ^ k) & 1), (z ^ k) >> 1)]

    return [column(pieces[k], size, ranks, round_of(k)) for k in range(size)]


def pick(blocks, index):
    return lax.dynamic_index_in_dim(blocks, index, 0, keepdims=False)


def reorder(blocks, z, size):
    return jnp.stack([pick(blocks, z ^ j) for j in range(size)])


def orders(ranks):
    far = []
    bit = 2
    while bit < ranks:
        far.append(bit)
        bit *= 2
    return far, far[::-1]


def place(r, bits):
    total = 0
    for k, bit in enumerate(bits):
        total = total + jnp.where(r & bit != 0, 1 << k, 0)
    return total


def grow(values, r, ranks, bits):
    for bit in bits:
        other = swap(values, "rep", ranks, bit)
        upper = r & bit != 0
        values = jnp.concatenate(
            [jnp.where(upper, other, values), jnp.where(upper, values, other)], axis=1
        )
    return values


def shrink(values, r, ranks, bits):
    for bit in bits:
        half = values.shape[1] // 2
        mine = jnp.where(r & bit != 0, half, 0)
        sent = lax.dynamic_slice_in_dim(values, half - mine, half, 1)
        kept = lax.dynamic_slice_in_dim(values, mine, half, 1)
        other = swap(sent, "rep", ranks, bit)
        values = (kept.astype(F32) + other.astype(F32)).astype(BF16)
    return values


def halves(values):
    middle = values.shape[-1] // 2
    return values[..., :middle], values[..., middle:]


def split_rows(shard, r, ranks):
    rows = shard.shape[0] // ranks
    one, two = orders(ranks)
    left, right = halves(shard)
    return jnp.concatenate(
        [
            lax.dynamic_slice_in_dim(left, place(r, one + [1]) * rows, rows, 0),
            lax.dynamic_slice_in_dim(right, place(r, two + [1]) * rows, rows, 0),
        ],
        axis=1,
    )


def grow_both(values, r, ranks):
    one, two = orders(ranks)
    left, right = halves(values)
    return jnp.concatenate([grow(left, r, ranks, one), grow(right, r, ranks, two)], axis=2)


def shrink_both(values, r, ranks):
    one, two = orders(ranks)
    left, right = halves(values)
    return jnp.concatenate(
        [shrink(left, r, ranks, one[::-1]), shrink(right, r, ranks, two[::-1])], axis=2
    )


def local(size, ranks, tokens, gain_a, projection_in, attention_out, gain_b, expansion, contraction, cotangent):
    z = lax.axis_index("fsdp")
    r = lax.axis_index("rep")
    core = r & 1
    group = 2 * core + (z & 1)
    home = core == z >> 1
    own = tokens[0]
    count, width = own.shape
    part = width // size
    hidden = contraction.shape[0]
    heads = HEADS // size

    columns = [projection_in[:, t * width : (t + 1) * width] for t in range(3)]
    piece = split_rows(jnp.concatenate(columns, axis=0), r, ranks)
    pieces = exchange([piece] * size, size)
    gains = jnp.stack([gain_a, gain_b])
    gains = exchange([gains] * size, size)
    pair, other, second = collect(after(own, *pieces), home, size, ranks)
    into = grow(grow_both(reorder(jnp.stack(pieces), z, size), r, ranks), r, ranks, [1])
    into = into.reshape(size, 3, part, width)
    into = [into[:, t].reshape(width, width) for t in range(3)]
    gains = reorder(jnp.stack(gains), z, size)
    gain_one = gains[:, 0].reshape(width).astype(F32)
    gain_two = gains[:, 1].reshape(width).astype(F32)

    freqs = THETA ** (-(jnp.arange(HALF, dtype=F32) * (2.0 / HEAD_DIM)))
    places = jnp.concatenate([(group ^ d) * count + jnp.arange(count, dtype=jnp.int32) for d in range(size)])
    angles = freqs[:, None] * places.astype(F32)[None, :]
    cosine, sine = jnp.cos(angles), jnp.sin(angles)

    normed = jnp.concatenate(
        [layer_norm(b.astype(F32), gain_one).astype(BF16) for b in (pair, other)], axis=0
    )
    own_into = [lax.dynamic_slice_in_dim(into[t], group * part, part, 1) for t in range(3)]

    def rotate(values):
        shaped = values.reshape(heads, 2, HALF, size * count)
        first, second = shaped[:, 0], shaped[:, 1]
        turned = jnp.stack([first * cosine - second * sine, second * cosine + first * sine], axis=1)
        return turned.reshape(part, size * count)

    queries = (rotate(mul(own_into[0], normed, TT)).astype(BF16) * SCALE).astype(BF16)
    keys_turned = rotate(mul(own_into[1], normed, TT)).astype(BF16)
    keys = keys_turned.reshape(heads, HEAD_DIM, size * count).transpose(0, 2, 1)
    values_turned = mul(own_into[2], normed, TT).astype(BF16)
    values = values_turned.reshape(heads, HEAD_DIM, size * count).transpose(0, 2, 1)

    columns = [expansion[:, t * width : (t + 1) * width] for t in range(3)]
    stacked = jnp.concatenate([attention_out] + columns + [contraction], axis=0)
    pad = -stacked.shape[0] % (8 * ranks)
    stacked = jnp.concatenate([stacked, jnp.zeros((pad, width), BF16)], axis=0)
    piece = split_rows(after(stacked, second), r, ranks)
    pieces = exchange([piece] * size, size)
    merged = []
    logs = []
    rest = reorder(jnp.stack(pieces), z, size)
    for head in range(heads):
        tied = keys if head == 0 else after(keys, rest)
        if head == 1:
            rest = grow_both(rest, r, ranks)
        out, log = attend(head, queries, tied, values_turned)
        merged.append(out)
        logs.append(log)
    rest = grow(rest, r, ranks, [1])
    own_merged = jnp.concatenate(merged, axis=0)

    arrived = trade_out([own_merged[:, d * count : (d + 1) * count] for d in range(size)], size, ranks)
    merged = jnp.concatenate(arrived, axis=0)
    out_weight = reorder(rest[:, :part], z, size).reshape(width, width)
    expand = [rest[:, (1 + t) * part : (2 + t) * part].reshape(width, width) for t in range(3)]
    contract = rest[:, 4 * part : 4 * part + hidden].reshape(size * hidden, width)
    inputs = own.astype(F32)
    state = inputs + mul(merged, out_weight, TN)
    normed_two = layer_norm(state, gain_two).astype(BF16)
    inner = jnp.concatenate([mul(normed_two, w) for w in expand], axis=1)
    active, glu_back = jax.vjp(geglu, inner)
    active = active.astype(BF16)
    block_output = (state + mul(active, contract)).astype(BF16)[None]

    upstream = cotangent[0]
    (inner_back,) = glu_back(rounded(mul(upstream, contract, NT)))
    inner_back = inner_back.astype(BF16)
    normed_two_back = sum(
        mul(inner_back[:, t * width : (t + 1) * width], expand[t], NT) for t in range(3)
    )
    state_back = upstream.astype(F32) + layer_norm_back(state, gain_two, normed_two_back)
    state_low = state_back.astype(BF16)
    merged_back = mul(out_weight, state_low, NT).astype(BF16)
    arrived = trade_back([merged_back[d * part : (d + 1) * part] for d in range(size)], size, ranks)
    own_upstream = jnp.concatenate(arrived, axis=1)

    contraction_grad = mul(active, upstream, TN).astype(BF16).reshape(size, hidden, width)
    expansion_grad = [
        mul(normed_two, inner_back[:, t * width : (t + 1) * width], TN).astype(BF16).reshape(size, part, width)
        for t in range(3)
    ]
    out_grad = reorder(mul(merged, state_low).astype(BF16).reshape(size, part, width), z, size)
    grads = jnp.concatenate(
        [out_grad] + expansion_grad + [contraction_grad, jnp.zeros((size, pad, width), BF16)], axis=1
    )
    grads = shrink(grads, r, ranks, [1])

    turned_backs = []
    received = []
    tied = after(own_upstream, grads)
    for head in range(heads):
        if head == 2:
            grads = shrink_both(grads, r, ranks)
            tied = after(own_upstream, grads, *received[0])
        grad = attend_back(
            head, queries, keys_turned, keys, values, tied, own_merged, logs[head], cosine, sine
        )
        turned_backs.append(grad)
        received.append(trade_out([grad[:, d * count : (d + 1) * count] for d in range(size)], size, ranks))

    grads = exchange([pick(grads, z ^ d) for d in range(size)], size)
    grads = sum(part.astype(F32) for part in grads).astype(BF16)[None]
    grads = grow(grow_both(grads, r, ranks), r, ranks, [1])[0].astype(F32)
    attention_out_sum = grads[:part]
    expansion_sum = jnp.concatenate([grads[(1 + t) * part : (2 + t) * part] for t in range(3)], axis=1)
    contraction_sum = grads[4 * part : 4 * part + hidden]

    projected_back = jnp.stack([jnp.stack(pieces) for pieces in received], axis=1)
    projected_back = reorder(projected_back, z, size).reshape(size, heads, 3, HEAD_DIM, count)
    projected_back = projected_back.transpose(2, 0, 1, 3, 4).reshape(3, width, count)
    normed_back = sum(mul(projected_back[t], into[t], TT) for t in range(3))
    token_grad = (state_back + layer_norm_back(inputs, gain_one, normed_back))[None]

    all_backs = jnp.stack(turned_backs).reshape(heads, 3, HEAD_DIM, size * count)
    all_backs = all_backs.transpose(1, 0, 2, 3).reshape(3 * part, size * count)
    into_grad = mul(normed, all_backs, TT).astype(BF16).reshape(size, part, 3 * part)
    into_grad = shrink(into_grad, r, ranks, orders(ranks)[1])
    arrived = exchange([pick(into_grad, z ^ d) for d in range(size)], size)
    even = (arrived[0].astype(F32) + arrived[2].astype(F32)).astype(BF16)
    odd = (arrived[1].astype(F32) + arrived[3].astype(F32)).astype(BF16)
    low = z & 1 == 0
    into_sum = jnp.stack([jnp.where(low, even, odd), jnp.where(low, odd, even)])
    into_sum = grow(into_sum, r, ranks, orders(ranks)[0])
    partner = swap(into_sum, "rep", ranks, 1)
    low = core == 0
    into_sum = jnp.concatenate([jnp.where(low, into_sum, partner), jnp.where(low, partner, into_sum)], axis=0)
    into_sum = into_sum.reshape(size, part, 3, part).transpose(1, 2, 0, 3).reshape(part, 3 * width).astype(F32)

    gain_one_sum = jnp.sum(into_sum * projection_in.astype(F32), axis=1) / gain_a.astype(F32)
    gain_two_sum = jnp.sum(expansion_sum * expansion.astype(F32), axis=1) / gain_b.astype(F32)
    return (
        block_output,
        token_grad,
        gain_one_sum,
        into_sum,
        attention_out_sum,
        gain_two_sum,
        expansion_sum,
        contraction_sum,
    )


def solution(mesh):
    tokens, rows, line = P("rep", "fsdp", None), P("fsdp", None), P("fsdp")
    in_specs = (tokens, line, rows, rows, line, rows, rows, tokens)
    out_specs = (tokens, tokens, line, rows, rows, line, rows, rows)
    body = functools.partial(local, mesh.shape["fsdp"], mesh.shape["rep"])
    return jax.shard_map(body, mesh=mesh, in_specs=in_specs, out_specs=out_specs, check_vma=False)
```

time: 447 us -> 409 us (0.915)
  local copies, waits for them, and re-layouts: 57.6 us -> 40.9 us
  waiting for transfers between devices: 131 us -> 116 us
  matrix products: 34.9 us -> 28 us
  starting transfers between devices: 96.9 us -> 91.7 us
    ppermute x57 -> x41, waiting for transfers between devices: 131 us -> 67.8 us  [swap(): return lax.ppermute(values, axis, [(i, i ^ offset) for i in range(size)])]
    ppermute x57 -> x41, starting transfers between devices: 96.9 us -> 47.6 us  [swap(): return lax.ppermute(values, axis, [(i, i ^ offset) for i in range(size)])]
    ppermute x0 -> x22, waiting for transfers between devices: none -> 48.7 us  [column(): return lax.ppermute(values, ('fsdp', 'rep'), full)]
    ppermute x0 -> x22, starting transfers between devices: none -> 44.1 us  [column(): return lax.ppermute(values, ('fsdp', 'rep'), full)]
    another operation x1 -> x0, local copies, waits for them, and re-layouts: 8.9 us -> none  [local(): by_head = into.reshape(3, size, heads, HEAD_DIM, width)]
    transpose x1 -> x0, local copies, waits for them, and re-layouts: 8.13 us -> none  [local(): into.reshape(size, 3, part, width).transpose(1, 3, 0, 2)]
    dot_general x20 -> x22, matrix products: 34.9 us -> 28 us  [mul(): return lax.dot_general(a, b, dims, preferred_element_type=F32)]
    unnamed x111 -> x145, local copies, waits for them, and re-layouts: 16.2 us -> 17 us
  transfers between devices with their start and end apart: 57 -> 63, of which waited for: 22 -> 24; matrix products, arithmetic and copies ran while one was open for 22% -> 18% of each run, Pallas kernels for 16% -> 14%
where the time goes in v2:
time: 409 us; the launch traced here: 402 us
  waiting for transfers between devices  116 us (28%)
  starting transfers between devices  91.7 us (22%)
  Pallas kernels  69.4 us (17%)
  other arithmetic  53 us (13%)
  local copies, waits for them, and re-layouts  40.9 us (10%)
  matrix products  28 us (7%)
    ppermute x41, waiting for transfers between devices, swap(): return lax.ppermute(values, axis, [(i, i ^ offset) for i in range(size)])  67.8 us
    ppermute x22, waiting for transfers between devices, column(): return lax.ppermute(values, ('fsdp', 'rep'), full)  48.7 us
    ppermute x41, starting transfers between devices, swap(): return lax.ppermute(values, axis, [(i, i ^ offset) for i in range(size)])  47.6 us
    ppermute x22, starting transfers between devices, column(): return lax.ppermute(values, ('fsdp', 'rep'), full)  44.1 us
    pallas_call x3, Pallas kernels, attend_back(): pl.pallas_call(attend_back_kernel, grid=(count // step,), in_specs=[some,...  39.4 us
    pallas_call x3, Pallas kernels, attend(): pl.pallas_call(attend_kernel, grid=(count // step,), in_specs=[pl.BlockSp...  30 us
    dot_general x22, matrix products, mul(): return lax.dot_general(a, b, dims, preferred_element_type=F32)  28 us
    unnamed x145, local copies, waits for them, and re-layouts  17 us
  transfers between devices with their start and end apart: 63, of which 24 were waited for; matrix products, arithmetic and copies ran while one was open for 18% of the time, Pallas kernels for 14%

profile of v2, /device:TPU:1, one launch (start us, length us, event | category | flops | bytes accessed | tf_op | source)
XLA Modules:
  0.0 402.4 jit_solution(18151223224669766158)
XLA Ops:
  2.8 4.2 %collective-permute-start.2 = (bf16[72,768]{1,0:T(8,128)(2,1)}, bf16[72,768]{1,0:T(8,128)(2,1)S(1)}, u32[]{:S(2)}, u32[]{:S(2)}) collective-permute-start(bf16[72,768]{1,0:T(8,128)(2,1)} %get-tuple-element.172), channel_id=1, source_target_pairs={{0,24},{8,16},{16,8},{24,0},{1,25},{9,17},{17,9},{25,1},{2,26},{10... | collective-permute-start | bytes 331784 | tf_op jit(solution)/shard_map/ppermute | solution.py:165
  7.3 3.3 collective-permute-start.12
  13.6 2.5 collective-permute-done.1
  21.3 2.0 collective-permute-start.8
  30.1 12.2 %collective-permute-done.8 = bf16[512,768]{1,0:T(8,128)(2,1)} collective-permute-done((bf16[512,768]{1,0:T(8,128)(2,1)S(1)}, bf16[512,768]{1,0:T(8,128)(2,1)}, u32[]{:S(2)}, u32[]{:S(2)}) %collective-permute-start.8) | collective-permute-done | bytes 786464 | tf_op jit(solution)/shard_map/ppermute | solution.py:179
  42.3 1.9 collective-permute-start.9
  47.2 8.1 %collective-permute-done.9 = bf16[512,768]{1,0:T(8,128)(2,1)} collective-permute-done((bf16[512,768]{1,0:T(8,128)(2,1)}, bf16[512,768]{1,0:T(8,128)(2,1)}, u32[]{:S(2)}, u32[]{:S(2)}) %collective-permute-start.9) | collective-permute-done | bytes 786464 | tf_op jit(solution)/shard_map/ppermute | solution.py:179
  56.8 2.3 collective-permute-start.14
  61.1 1.7 collective-permute-start.13
  63.3 10.6 %collective-permute-done.15 = bf16[136,768]{1,0:T(8,128)(2,1)S(1)} collective-permute-done((bf16[136,768]{1,0:T(8,128)(2,1)S(1)}, bf16[136,768]{1,0:T(8,128)(2,1)S(1)}, u32[]{:S(2)}, u32[]{:S(2)}) %collective-permute-start.15) | collective-permute-done | bytes 208928 | tf_op jit(solution)/shard_map/ppermute | solution.py:165
  75.5 7.5 %collective-permute-done.17 = bf16[4,136,384]{2,1,0:T(8,128)(2,1)S(1)} collective-permute-done((bf16[4,136,384]{2,1,0:T(8,128)(2,1)S(1)}, bf16[4,136,384]{2,1,0:T(8,128)(2,1)S(1)}, u32[]{:S(2)}, u32[]{:S(2)}) %collective-permute-start.17) | collective-permute-done | bytes 417824 | tf_op jit(solution)/shard_map/ppermute | solution.py:165
  87.4 12.4 %collective-permute-done.20 = bf16[4,272,384]{2,1,0:T(8,128)(2,1)S(1)} collective-permute-done((bf16[4,272,384]{2,1,0:T(8,128)(2,1)S(1)}, bf16[4,272,384]{2,1,0:T(8,128)(2,1)S(1)}, u32[]{:S(2)}, u32[]{:S(2)}) %collective-permute-start.20) | collective-permute-done | bytes 835616 | tf_op jit(solution)/shard_map/ppermute | solution.py:165
  101.2 2.0 maximum_maximum_fusion
  103.4 4.9 %collective-permute-start.25 = (bf16[4,544,768]{2,1,0:T(8,128)(2,1)}, bf16[4,544,768]{2,1,0:T(8,128)(2,1)}, u32[]{:S(2)}, u32[]{:S(2)}) collective-permute-start(bf16[4,544,768]{2,1,0:T(8,128)(2,1)} %maximum_maximum_fusion), channel_id=1, source_target_pairs={{0,1},{1,0},{2,3},{3,2},{4,5},{5,4},{6,7},{7,6},{8,9},{9,8},{10,11... | collective-permute-start | bytes 10027016 | tf_op jit(solution)/shard_map/ppermute | solution.py:165
  109.2 1.8 fusion.9
  113.0 1.5 copy.44
  114.5 3.6 fusion.49
  121.2 10.0 %attend.3 = (bf16[64,2048]{1,0:T(8,128)(2,1)S(1)}, f32[1,2048]{1,0:T(1,128)S(1)}) custom-call(bf16[192,2048]{1,0:T(8,128)(2,1)S(1)} %bitcast.176, bf16[3,2048,64]{2,1,0:T(8,128)(2,1)S(1)} %bitcast.170, bf16[192,2048]{1,0:T(8,128)(2,1)S(1)} %convolution_convert_fusion.2.v_ref), custom_call_target="tpu_custom_call" | custom-call | flops 10737418240 | bytes 1048576 | tf_op jit(solution)/shard_map/attend/pallas_call | solution.py:66
  131.2 10.0 %attend.4 = (bf16[64,2048]{1,0:T(8,128)(2,1)S(1)}, f32[1,2048]{1,0:T(1,128)S(1)}) custom-call(bf16[192,2048]{1,0:T(8,128)(2,1)S(1)} %bitcast.177, bf16[3,2048,64]{2,1,0:T(8,128)(2,1)S(1)} %bitcast.171, bf16[192,2048]{1,0:T(8,128)(2,1)S(1)} %convolution_convert_fusion.2.v_ref), custom_call_target="tpu_custom_call" | custom-call | flops 10737418240 | bytes 1048576 | tf_op jit(solution)/shard_map/attend/pallas_call | solution.py:66
  141.3 10.0 %attend.5 = (bf16[64,2048]{1,0:T(8,128)(2,1)S(1)}, f32[1,2048]{1,0:T(1,128)S(1)}) custom-call(bf16[192,2048]{1,0:T(8,128)(2,1)S(1)} %bitcast.178, bf16[3,2048,64]{2,1,0:T(8,128)(2,1)S(1)} %bitcast.172, bf16[192,2048]{1,0:T(8,128)(2,1)S(1)} %convolution_convert_fusion.2.v_ref), custom_call_target="tpu_custom_call" | custom-call | flops 10737418240 | bytes 1048576 | tf_op jit(solution)/shard_map/attend/pallas_call | solution.py:66
  152.0 1.9 collective-permute-start.21
  154.0 2.4 collective-permute-start.22
  156.5 1.8 collective-permute-start.24
  158.2 10.1 %collective-permute-done.21 = bf16[192,512]{1,0:T(8,128)(2,1)} collective-permute-done((bf16[192,512]{1,0:T(8,128)(2,1)}, bf16[192,512]{1,0:T(8,128)(2,1)}, u32[]{:S(2)}, u32[]{:S(2)}) %collective-permute-start.21) | collective-permute-done | bytes 196640 | tf_op jit(solution)/shard_map/ppermute | solution.py:179
  171.2 3.7 broadcast_select_fusion
  183.2 5.2 %convert_multiply_fusion.1 = (f32[512,1152]{1,0:T(8,128)S(1)}, f32[512,1152]{1,0:T(8,128)S(1)}) fusion(bf16[512,1152]{1,0:T(8,128)(2,1)S(1)} %fusion.10, f32[512,768]{1,0:T(8,128)S(1)} %fusion.88, f32[512,768]{1,0:T(8,128)S(1)} %fusion.87), kind=kLoop, calls=%fused_computation.25 | loop fusion | flops 39518208 | bytes 9043968 | tf_op jit(solution)/shard_map/transpose(jvp())/mul | solution.py:47
  188.4 1.5 multiply_add_fusion
  198.9 2.1 constant_dynamic-slice_fusion.10
  201.0 1.7 copy-done.12
  205.4 2.5 copy.46
  207.9 2.7 convolution_convert_fusion.8
  210.7 6.3 %collective-permute-start.26 = (bf16[192,512]{1,0:T(8,128)(2,1)S(1)}, bf16[192,512]{1,0:T(8,128)(2,1)S(1)}, u32[]{:S(2)}, u32[]{:S(2)}) collective-permute-start(bf16[192,512]{1,0:T(8,128)(2,1)S(1)} %get-tuple-element.129), channel_id=1, source_target_pairs={{0,0},{1,16},{2,2},{3,18},{4,4},{5,20},{6,6},{7,22},{8,8},{9,24},{... | collective-permute-start | bytes 589832 | tf_op jit(solution)/shard_map/ppermute | solution.py:179
  217.0 2.3 collective-permute-start.27
  219.4 2.1 fusion.27
  222.8 2.9 collective-permute-done.27
  225.7 1.9 collective-permute-done.28
  227.6 2.1 collective-permute-done.29
  229.8 2.7 add_convert_fusion
  234.2 13.3 %attend_back.3 = bf16[192,2048]{1,0:T(8,128)(2,1)S(1)} custom-call(bf16[192,2048]{1,0:T(8,128)(2,1)S(1)} %bitcast.179, bf16[192,2048]{1,0:T(8,128)(2,1)S(1)} %bitcast.167, bf16[3,2048,64]{2,1,0:T(8,128)(2,1)S(1)} %bitcast.173, bf16[3,2048,64]{2,1,0:T(8,128)(2,1)} %bitcast.203, bf16[192,2048]{1,0:T(8,128)(2,1)S(1)} %constant_dynamic-update-slice_fusion.10.up_ref, ...), custom_call_target="tpu_custom_call" | custom-call | flops 15032385536 | bytes 2097152 | tf_op jit(solution)/shard_map/attend_back/pallas_call | solution.py:133
  247.5 7.1 %collective-permute-start.31 = (bf16[192,512]{1,0:T(8,128)(2,1)S(1)}, bf16[192,512]{1,0:T(8,128)(2,1)S(1)}, u32[]{:S(2)}, u32[]{:S(2)}) collective-permute-start(bf16[192,512]{1,0:T(8,128)(2,1)S(1)} %get-tuple-element.125), channel_id=1, source_target_pairs={{0,0},{1,16},{2,2},{3,18},{4,4},{5,20},{6,6},{7,22},{8,8},{9,24},{... | collective-permute-start | bytes 589832 | tf_op jit(solution)/shard_map/ppermute | solution.py:179
  254.6 1.8 collective-permute-start.32
  256.4 2.4 collective-permute-start.34
  258.8 13.1 %attend_back.4 = bf16[192,2048]{1,0:T(8,128)(2,1)S(1)} custom-call(bf16[192,2048]{1,0:T(8,128)(2,1)S(1)} %bitcast.180, bf16[192,2048]{1,0:T(8,128)(2,1)S(1)} %bitcast.168, bf16[3,2048,64]{2,1,0:T(8,128)(2,1)S(1)} %bitcast.174, bf16[3,2048,64]{2,1,0:T(8,128)(2,1)} %bitcast.204, bf16[192,2048]{1,0:T(8,128)(2,1)S(1)} %constant_dynamic-update-slice_fusion.10.up_ref, ...), custom_call_target="tpu_custom_call" | custom-call | flops 15032385536 | bytes 2097152 | tf_op jit(solution)/shard_map/attend_back/pallas_call | solution.py:133
  274.8 1.8 collective-permute-start.37
  276.6 1.8 collective-permute-start.36
  278.4 1.9 collective-permute-start.35
  280.7 13.1 %attend_back.5 = bf16[192,2048]{1,0:T(8,128)(2,1)S(1)} custom-call(bf16[192,2048]{1,0:T(8,128)(2,1)S(1)} %bitcast.181, bf16[192,2048]{1,0:T(8,128)(2,1)S(1)} %bitcast.169, bf16[3,2048,64]{2,1,0:T(8,128)(2,1)S(1)} %bitcast.175, bf16[3,2048,64]{2,1,0:T(8,128)(2,1)} %bitcast.205, bf16[192,2048]{1,0:T(8,128)(2,1)S(1)} %constant_dynamic-update-slice_fusion.10.up_ref, ...), custom_call_target="tpu_custom_call" | custom-call | flops 15032385536 | bytes 2097152 | tf_op jit(solution)/shard_map/attend_back/pallas_call | solution.py:133
  295.7 2.0 convolution_convert_fusion.7
  302.1 3.5 collective-permute-start.43
  307.7 10.5 %collective-permute-done.45 = bf16[192,512]{1,0:T(8,128)(2,1)S(1)} collective-permute-done((bf16[192,512]{1,0:T(8,128)(2,1)S(1)}, bf16[192,512]{1,0:T(8,128)(2,1)S(1)}, u32[]{:S(2)}, u32[]{:S(2)}) %collective-permute-start.45) | collective-permute-done | bytes 196640 | tf_op jit(solution)/shard_map/ppermute | solution.py:179
  326.1 1.6 fusion.25
  331.2 4.8 %collective-permute-done.48 = bf16[4,48,576]{2,1,0:T(8,128)(2,1)S(1)} collective-permute-done((bf16[4,48,576]{2,1,0:T(8,128)(2,1)S(1)}, bf16[4,48,576]{2,1,0:T(8,128)(2,1)S(1)}, u32[]{:S(2)}, u32[]{:S(2)}) %collective-permute-start.48) | collective-permute-done | bytes 221216 | tf_op jit(solution)/shard_map/ppermute | solution.py:165
  336.2 2.2 collective-permute-start.50
  343.0 3.8 collective-permute-done.42
  352.0 1.7 collective-permute-done.57
  353.7 13.1 %collective-permute-done.56 = bf16[136,768]{1,0:T(8,128)(2,1)S(1)} collective-permute-done((bf16[136,768]{1,0:T(8,128)(2,1)S(1)}, bf16[136,768]{1,0:T(8,128)(2,1)S(1)}, u32[]{:S(2)}, u32[]{:S(2)}) %collective-permute-start.56) | collective-permute-done | bytes 208928 | tf_op jit(solution)/shard_map/ppermute | solution.py:165
  367.3 1.5 collective-permute-start.60
  368.9 1.6 collective-permute-done.58
  372.5 4.0 collective-permute-start.54
  376.5 1.5 collective-permute-start.59
  378.1 5.2 %collective-permute-done.59 = bf16[1,272,384]{2,1,0:T(8,128)(2,1)S(1)} collective-permute-done((bf16[1,272,384]{2,1,0:T(8,128)(2,1)S(1)}, bf16[1,272,384]{2,1,0:T(8,128)(2,1)S(1)}, u32[]{:S(2)}, u32[]{:S(2)}) %collective-permute-start.59) | collective-permute-done | bytes 208928 | tf_op jit(solution)/shard_map/ppermute | solution.py:165
  386.8 2.3 copy.52
  389.1 2.7 copy.53
  391.8 2.9 reshape.290
  (387 shorter events, 109.9 us)
Async XLA Ops:
  2.8 10.0 %collective-permute-start.2 = (bf16[72,768]{1,0:T(8,128)(2,1)}, bf16[72,768]{1,0:T(8,128)(2,1)S(1)}, u32[]{:S(2)}, u32[]{:S(2)}) collective-permute-start(bf16[72,768]{1,0:T(8,128)(2,1)} %get-tuple-element.172), channel_id=1, source_target_pairs={{0,24},{8,16},{16,8},{24,0},{1,25},{9,17},{17,9},{25,1},{2,26},{10... | collective-permute-start | bytes 331784 | tf_op jit(solution)/shard_map/ppermute | solution.py:165
  6.9 9.2 %collective-permute-start.1 = (bf16[72,768]{1,0:T(8,128)(2,1)}, bf16[72,768]{1,0:T(8,128)(2,1)S(1)}, u32[]{:S(2)}, u32[]{:S(2)}) collective-permute-start(bf16[72,768]{1,0:T(8,128)(2,1)} %get-tuple-element.172), channel_id=1, source_target_pairs={{0,16},{8,24},{16,0},{24,8},{1,17},{9,25},{17,1},{25,9},{2,18},{10... | collective-permute-start | bytes 331784 | tf_op jit(solution)/shard_map/ppermute | solution.py:165
  6.9 9.2 %collective-permute-start = (bf16[72,768]{1,0:T(8,128)(2,1)}, bf16[72,768]{1,0:T(8,128)(2,1)S(1)}, u32[]{:S(2)}, u32[]{:S(2)}) collective-permute-start(bf16[72,768]{1,0:T(8,128)(2,1)} %get-tuple-element.172), channel_id=1, source_target_pairs={{0,8},{8,0},{16,24},{24,16},{1,9},{9,1},{17,25},{25,17},{2,10},{10... | collective-permute-start | bytes 331784 | tf_op jit(solution)/shard_map/ppermute | solution.py:165
  7.3 14.1 %collective-permute-start.12 = (bf16[2,192]{1,0:T(2,128)(2,1)S(1)}, bf16[2,192]{1,0:T(2,128)(2,1)S(1)}, u32[]{:S(2)}, u32[]{:S(2)}) collective-permute-start(bf16[2,192]{1,0:T(2,128)(2,1)S(1)} %pad_maximum_fusion.31), channel_id=1, source_target_pairs={{0,24},{8,16},{16,8},{24,0},{1,25},{9,17},{17,9},{25,1},{2,26},{10... | collective-permute-start | bytes 2312 | tf_op jit(solution)/shard_map/ppermute | solution.py:165
  10.6 12.7 %collective-permute-start.11 = (bf16[2,192]{1,0:T(2,128)(2,1)S(1)}, bf16[2,192]{1,0:T(2,128)(2,1)S(1)}, u32[]{:S(2)}, u32[]{:S(2)}) collective-permute-start(bf16[2,192]{1,0:T(2,128)(2,1)S(1)} %pad_maximum_fusion.31), channel_id=1, source_target_pairs={{0,16},{8,24},{16,0},{24,8},{1,17},{9,25},{17,1},{25,9},{2,18},{10... | collective-permute-start | bytes 2312 | tf_op jit(solution)/shard_map/ppermute | solution.py:165
  12.8 10.5 %collective-permute-start.10 = (bf16[2,192]{1,0:T(2,128)(2,1)S(1)}, bf16[2,192]{1,0:T(2,128)(2,1)}, u32[]{:S(2)}, u32[]{:S(2)}) collective-permute-start(bf16[2,192]{1,0:T(2,128)(2,1)S(1)} %pad_maximum_fusion.31), channel_id=1, source_target_pairs={{0,8},{8,0},{16,24},{24,16},{1,9},{9,1},{17,25},{25,17},{2,10},{10... | collective-permute-start | bytes 2312 | tf_op jit(solution)/shard_map/ppermute | solution.py:165
  18.8 5.9 %collective-permute-start.3 = (bf16[4,72,384]{2,1,0:T(8,128)(2,1)}, bf16[4,72,384]{2,1,0:T(8,128)(2,1)}, u32[]{:S(2)}, u32[]{:S(2)}) collective-permute-start(bf16[4,72,384]{2,1,0:T(8,128)(2,1)} %get-tuple-element.144), channel_id=1, source_target_pairs={{0,2},{1,3},{2,0},{3,1},{4,6},{5,7},{6,4},{7,5},{8,10},{9,11},{10,... | collective-permute-start | bytes 663560 | tf_op jit(solution)/shard_map/ppermute | solution.py:165
  20.1 5.6 %collective-permute-start.5 = (bf16[4,72,384]{2,1,0:T(8,128)(2,1)}, bf16[4,72,384]{2,1,0:T(8,128)(2,1)}, u32[]{:S(2)}, u32[]{:S(2)}) collective-permute-start(bf16[4,72,384]{2,1,0:T(8,128)(2,1)} %get-tuple-element.145), channel_id=1, source_target_pairs={{0,4},{1,5},{2,6},{3,7},{4,0},{5,1},{6,2},{7,3},{8,12},{9,13},{10,... | collective-permute-start | bytes 663560 | tf_op jit(solution)/shard_map/ppermute | solution.py:165
  21.3 20.9 %collective-permute-start.8 = (bf16[512,768]{1,0:T(8,128)(2,1)S(1)}, bf16[512,768]{1,0:T(8,128)(2,1)}, u32[]{:S(2)}, u32[]{:S(2)}) collective-permute-start(bf16[512,768]{1,0:T(8,128)(2,1)S(1)} %bitcast.183), channel_id=1, source_target_pairs={{0,8},{1,16},{2,10},{3,18},{4,12},{5,20},{6,14},{7,22},{8,0},{9,24... | collective-permute-start | bytes 2359304 | tf_op jit(solution)/shard_map/ppermute | solution.py:179
  27.7 16.6 %collective-permute-start.6 = (bf16[4,144,384]{2,1,0:T(8,128)(2,1)}, bf16[4,144,384]{2,1,0:T(8,128)(2,1)}, u32[]{:S(2)}, u32[]{:S(2)}) collective-permute-start(bf16[4,144,384]{2,1,0:T(8,128)(2,1)} %pad_maximum_fusion.22), channel_id=1, source_target_pairs={{0,2},{1,3},{2,0},{3,1},{4,6},{5,7},{6,4},{7,5},{8,10},{9,11},{10,... | collective-permute-start | bytes 1327112 | tf_op jit(solution)/shard_map/ppermute | solution.py:165
  28.8 16.9 %collective-permute-start.4 = (bf16[4,144,384]{2,1,0:T(8,128)(2,1)}, bf16[4,144,384]{2,1,0:T(8,128)(2,1)}, u32[]{:S(2)}, u32[]{:S(2)}) collective-permute-start(bf16[4,144,384]{2,1,0:T(8,128)(2,1)} %pad_maximum_fusion.21), channel_id=1, source_target_pairs={{0,4},{1,5},{2,6},{3,7},{4,0},{5,1},{6,2},{7,3},{8,12},{9,13},{10,... | collective-permute-start | bytes 1327112 | tf_op jit(solution)/shard_map/ppermute | solution.py:165
  42.3 13.0 %collective-permute-start.9 = (bf16[512,768]{1,0:T(8,128)(2,1)}, bf16[512,768]{1,0:T(8,128)(2,1)}, u32[]{:S(2)}, u32[]{:S(2)}) collective-permute-start(bf16[512,768]{1,0:T(8,128)(2,1)} %collective-permute-done.8), channel_id=1, source_target_pairs={{1,9},{3,11},{5,13},{7,15},{9,1},{11,3},{13,5},{15,7},{16,24},{18,... | collective-permute-start | bytes 2359304 | tf_op jit(solution)/shard_map/ppermute | solution.py:179
  47.1 37.8 %collective-permute-start.7 = (bf16[4,288,768]{2,1,0:T(8,128)(2,1)S(1)}, bf16[4,288,768]{2,1,0:T(8,128)(2,1)S(1)}, u32[]{:S(2)}, u32[]{:S(2)}) collective-permute-start(bf16[4,288,768]{2,1,0:T(8,128)(2,1)S(1)} %maximum_maximum_fusion.1), channel_id=1, source_target_pairs={{0,1},{1,0},{2,3},{3,2},{4,5},{5,4},{6,7},{7,6},{8,9},{9,8},{10,11... | collective-permute-start | bytes 5308424 | tf_op jit(solution)/shard_map/ppermute | solution.py:165
  55.6 7.7 %collective-permute-start.16 = (bf16[136,768]{1,0:T(8,128)(2,1)S(1)}, bf16[136,768]{1,0:T(8,128)(2,1)S(1)}, u32[]{:S(2)}, u32[]{:S(2)}) collective-permute-start(bf16[136,768]{1,0:T(8,128)(2,1)S(1)} %get-tuple-element.170), channel_id=1, source_target_pairs={{0,24},{8,16},{16,8},{24,0},{1,25},{9,17},{17,9},{25,1},{2,26},{10... | collective-permute-start | bytes 626696 | tf_op jit(solution)/shard_map/ppermute | solution.py:165
  55.6 18.3 %collective-permute-start.15 = (bf16[136,768]{1,0:T(8,128)(2,1)S(1)}, bf16[136,768]{1,0:T(8,128)(2,1)S(1)}, u32[]{:S(2)}, u32[]{:S(2)}) collective-permute-start(bf16[136,768]{1,0:T(8,128)(2,1)S(1)} %get-tuple-element.170), channel_id=1, source_target_pairs={{0,16},{8,24},{16,0},{24,8},{1,17},{9,25},{17,1},{25,9},{2,18},{10... | collective-permute-start | bytes 626696 | tf_op jit(solution)/shard_map/ppermute | solution.py:165
  56.8 17.1 %collective-permute-start.14 = (bf16[136,768]{1,0:T(8,128)(2,1)S(1)}, bf16[136,768]{1,0:T(8,128)(2,1)S(1)}, u32[]{:S(2)}, u32[]{:S(2)}) collective-permute-start(bf16[136,768]{1,0:T(8,128)(2,1)S(1)} %get-tuple-element.170), channel_id=1, source_target_pairs={{0,8},{8,0},{16,24},{24,16},{1,9},{9,1},{17,25},{25,17},{2,10},{10... | collective-permute-start | bytes 626696 | tf_op jit(solution)/shard_map/ppermute | solution.py:165
  61.1 47.2 %collective-permute-start.13 = (bf16[1024,768]{1,0:T(8,128)(2,1)S(1)}, bf16[1024,768]{1,0:T(8,128)(2,1)S(1)}, u32[]{:S(2)}, u32[]{:S(2)}) collective-permute-start(bf16[1024,768]{1,0:T(8,128)(2,1)S(1)} %pad_maximum_fusion.8), channel_id=1, source_target_pairs={{0,1},{1,0},{2,3},{3,2},{4,5},{5,4},{6,7},{7,6},{8,9},{9,8},{10,11... | collective-permute-start | bytes 4718600 | tf_op jit(solution)/shard_map/ppermute | solution.py:165
  74.3 8.7 %collective-permute-start.17 = (bf16[4,136,384]{2,1,0:T(8,128)(2,1)S(1)}, bf16[4,136,384]{2,1,0:T(8,128)(2,1)S(1)}, u32[]{:S(2)}, u32[]{:S(2)}) collective-permute-start(bf16[4,136,384]{2,1,0:T(8,128)(2,1)S(1)} %get-tuple-element.108), channel_id=1, source_target_pairs={{0,2},{1,3},{2,0},{3,1},{4,6},{5,7},{6,4},{7,5},{8,10},{9,11},{10,... | collective-permute-start | bytes 1253384 | tf_op jit(solution)/shard_map/ppermute | solution.py:165
  74.6 8.4 %collective-permute-start.19 = (bf16[4,136,384]{2,1,0:T(8,128)(2,1)S(1)}, bf16[4,136,384]{2,1,0:T(8,128)(2,1)S(1)}, u32[]{:S(2)}, u32[]{:S(2)}) collective-permute-start(bf16[4,136,384]{2,1,0:T(8,128)(2,1)S(1)} %get-tuple-element.109), channel_id=1, source_target_pairs={{0,4},{1,5},{2,6},{3,7},{4,0},{5,1},{6,2},{7,3},{8,12},{9,13},{10,... | collective-permute-start | bytes 1253384 | tf_op jit(solution)/shard_map/ppermute | solution.py:165
  83.3 16.5 %collective-permute-start.20 = (bf16[4,272,384]{2,1,0:T(8,128)(2,1)S(1)}, bf16[4,272,384]{2,1,0:T(8,128)(2,1)S(1)}, u32[]{:S(2)}, u32[]{:S(2)}) collective-permute-start(bf16[4,272,384]{2,1,0:T(8,128)(2,1)S(1)} %pad_maximum_fusion.16), channel_id=1, source_target_pairs={{0,2},{1,3},{2,0},{3,1},{4,6},{5,7},{6,4},{7,5},{8,10},{9,11},{10,... | collective-permute-start | bytes 2506760 | tf_op jit(solution)/shard_map/ppermute | solution.py:165
  84.6 16.2 %collective-permute-start.18 = (bf16[4,272,384]{2,1,0:T(8,128)(2,1)S(1)}, bf16[4,272,384]{2,1,0:T(8,128)(2,1)S(1)}, u32[]{:S(2)}, u32[]{:S(2)}) collective-permute-start(bf16[4,272,384]{2,1,0:T(8,128)(2,1)S(1)} %pad_maximum_fusion.15), channel_id=1, source_target_pairs={{0,4},{1,5},{2,6},{3,7},{4,0},{5,1},{6,2},{7,3},{8,12},{9,13},{10,... | collective-permute-start | bytes 2506760 | tf_op jit(solution)/shard_map/ppermute | solution.py:165
  103.4 67.8 %collective-permute-start.25 = (bf16[4,544,768]{2,1,0:T(8,128)(2,1)}, bf16[4,544,768]{2,1,0:T(8,128)(2,1)}, u32[]{:S(2)}, u32[]{:S(2)}) collective-permute-start(bf16[4,544,768]{2,1,0:T(8,128)(2,1)} %maximum_maximum_fusion), channel_id=1, source_target_pairs={{0,1},{1,0},{2,3},{3,2},{4,5},{5,4},{6,7},{7,6},{8,9},{9,8},{10,11... | collective-permute-start | bytes 10027016 | tf_op jit(solution)/shard_map/ppermute | solution.py:165
  121.1 137.7 %copy-start.2 = (bf16[3,2,32,2048]{3,2,1,0:T(8,128)(2,1)}, bf16[3,2,32,2048]{3,2,1,0:T(8,128)(2,1)S(1)}, u32[]{:S(2)}) copy-start(bf16[3,2,32,2048]{3,2,1,0:T(8,128)(2,1)S(1)} %maximum_multiply_fusion) | copy-start | bytes 2359300
  152.0 16.3 %collective-permute-start.21 = (bf16[192,512]{1,0:T(8,128)(2,1)}, bf16[192,512]{1,0:T(8,128)(2,1)}, u32[]{:S(2)}, u32[]{:S(2)}) collective-permute-start(bf16[192,512]{1,0:T(8,128)(2,1)} %get-tuple-element.133), channel_id=1, source_target_pairs={{0,0},{1,16},{2,2},{3,18},{4,4},{5,20},{6,6},{7,22},{8,8},{9,24},{... | collective-permute-start | bytes 589832 | tf_op jit(solution)/shard_map/ppermute | solution.py:179
  154.0 15.3 %collective-permute-start.22 = (bf16[192,512]{1,0:T(8,128)(2,1)S(1)}, bf16[192,512]{1,0:T(8,128)(2,1)}, u32[]{:S(2)}, u32[]{:S(2)}) collective-permute-start(bf16[192,512]{1,0:T(8,128)(2,1)S(1)} %get-tuple-element.132), channel_id=1, source_target_pairs={{0,8},{1,24},{2,10},{3,26},{4,12},{5,28},{6,14},{7,30},{8,0},{9,16... | collective-permute-start | bytes 589832 | tf_op jit(solution)/shard_map/ppermute | solution.py:179
  156.4 14.7 %collective-permute-start.23 = (bf16[192,512]{1,0:T(8,128)(2,1)S(1)}, bf16[192,512]{1,0:T(8,128)(2,1)S(1)}, u32[]{:S(2)}, u32[]{:S(2)}) collective-permute-start(bf16[192,512]{1,0:T(8,128)(2,1)S(1)} %get-tuple-element.131), channel_id=1, source_target_pairs={{0,16},{1,0},{2,18},{3,2},{4,20},{5,4},{6,22},{7,6},{8,24},{9,8},{... | collective-permute-start | bytes 589832 | tf_op jit(solution)/shard_map/ppermute | solution.py:179
  156.5 14.7 %collective-permute-start.24 = (bf16[192,512]{1,0:T(8,128)(2,1)S(1)}, bf16[192,512]{1,0:T(8,128)(2,1)S(1)}, u32[]{:S(2)}, u32[]{:S(2)}) collective-permute-start(bf16[192,512]{1,0:T(8,128)(2,1)S(1)} %get-tuple-element.130), channel_id=1, source_target_pairs={{0,24},{1,8},{2,26},{3,10},{4,28},{5,12},{6,30},{7,14},{8,16},{9,0... | collective-permute-start | bytes 589832 | tf_op jit(solution)/shard_map/ppermute | solution.py:179
  202.6 27.1 %collective-permute-start.30 = (bf16[4,544,768]{2,1,0:T(8,128)(2,1)}, bf16[4,544,768]{2,1,0:T(8,128)(2,1)}, u32[]{:S(2)}, u32[]{:S(2)}) collective-permute-start(bf16[4,544,768]{2,1,0:T(8,128)(2,1)} %constant_dynamic-slice_fusion.10), channel_id=1, source_target_pairs={{0,1},{1,0},{2,3},{3,2},{4,5},{5,4},{6,7},{7,6},{8,9},{9,8},{10,11... | collective-permute-start | bytes 10027016 | tf_op jit(solution)/shard_map/ppermute | solution.py:165
  210.7 12.1 %collective-permute-start.26 = (bf16[192,512]{1,0:T(8,128)(2,1)S(1)}, bf16[192,512]{1,0:T(8,128)(2,1)S(1)}, u32[]{:S(2)}, u32[]{:S(2)}) collective-permute-start(bf16[192,512]{1,0:T(8,128)(2,1)S(1)} %get-tuple-element.129), channel_id=1, source_target_pairs={{0,0},{1,16},{2,2},{3,18},{4,4},{5,20},{6,6},{7,22},{8,8},{9,24},{... | collective-permute-start | bytes 589832 | tf_op jit(solution)/shard_map/ppermute | solution.py:179
  217.0 8.7 %collective-permute-start.27 = (bf16[192,512]{1,0:T(8,128)(2,1)S(1)}, bf16[192,512]{1,0:T(8,128)(2,1)S(1)}, u32[]{:S(2)}, u32[]{:S(2)}) collective-permute-start(bf16[192,512]{1,0:T(8,128)(2,1)S(1)} %get-tuple-element.128), channel_id=1, source_target_pairs={{0,8},{1,24},{2,10},{3,26},{4,12},{5,28},{6,14},{7,30},{8,0},{9,16... | collective-permute-start | bytes 589832 | tf_op jit(solution)/shard_map/ppermute | solution.py:179
  221.4 6.2 %collective-permute-start.28 = (bf16[192,512]{1,0:T(8,128)(2,1)S(1)}, bf16[192,512]{1,0:T(8,128)(2,1)S(1)}, u32[]{:S(2)}, u32[]{:S(2)}) collective-permute-start(bf16[192,512]{1,0:T(8,128)(2,1)S(1)} %get-tuple-element.127), channel_id=1, source_target_pairs={{0,1},{1,17},{2,3},{3,19},{4,5},{5,21},{6,7},{7,23},{8,9},{9,25},{... | collective-permute-start | bytes 589832 | tf_op jit(solution)/shard_map/ppermute | solution.py:179
  221.4 8.3 %collective-permute-start.29 = (bf16[192,512]{1,0:T(8,128)(2,1)S(1)}, bf16[192,512]{1,0:T(8,128)(2,1)S(1)}, u32[]{:S(2)}, u32[]{:S(2)}) collective-permute-start(bf16[192,512]{1,0:T(8,128)(2,1)S(1)} %get-tuple-element.126), channel_id=1, source_target_pairs={{0,9},{1,25},{2,11},{3,27},{4,13},{5,29},{6,15},{7,31},{8,1},{9,17... | collective-permute-start | bytes 589832 | tf_op jit(solution)/shard_map/ppermute | solution.py:179
  247.5 27.3 %collective-permute-start.31 = (bf16[192,512]{1,0:T(8,128)(2,1)S(1)}, bf16[192,512]{1,0:T(8,128)(2,1)S(1)}, u32[]{:S(2)}, u32[]{:S(2)}) collective-permute-start(bf16[192,512]{1,0:T(8,128)(2,1)S(1)} %get-tuple-element.125), channel_id=1, source_target_pairs={{0,0},{1,16},{2,2},{3,18},{4,4},{5,20},{6,6},{7,22},{8,8},{9,24},{... | collective-permute-start | bytes 589832 | tf_op jit(solution)/shard_map/ppermute | solution.py:179
  254.6 22.0 %collective-permute-start.32 = (bf16[192,512]{1,0:T(8,128)(2,1)S(1)}, bf16[192,512]{1,0:T(8,128)(2,1)S(1)}, u32[]{:S(2)}, u32[]{:S(2)}) collective-permute-start(bf16[192,512]{1,0:T(8,128)(2,1)S(1)} %get-tuple-element.124), channel_id=1, source_target_pairs={{0,8},{1,24},{2,10},{3,26},{4,12},{5,28},{6,14},{7,30},{8,0},{9,16... | collective-permute-start | bytes 589832 | tf_op jit(solution)/shard_map/ppermute | solution.py:179
  256.4 22.0 %collective-permute-start.33 = (bf16[192,512]{1,0:T(8,128)(2,1)S(1)}, bf16[192,512]{1,0:T(8,128)(2,1)S(1)}, u32[]{:S(2)}, u32[]{:S(2)}) collective-permute-start(bf16[192,512]{1,0:T(8,128)(2,1)S(1)} %get-tuple-element.123), channel_id=1, source_target_pairs={{0,16},{1,0},{2,18},{3,2},{4,20},{5,4},{6,22},{7,6},{8,24},{9,8},{... | collective-permute-start | bytes 589832 | tf_op jit(solution)/shard_map/ppermute | solution.py:179
  256.4 23.9 %collective-permute-start.34 = (bf16[192,512]{1,0:T(8,128)(2,1)S(1)}, bf16[192,512]{1,0:T(8,128)(2,1)S(1)}, u32[]{:S(2)}, u32[]{:S(2)}) collective-permute-start(bf16[192,512]{1,0:T(8,128)(2,1)S(1)} %get-tuple-element.122), channel_id=1, source_target_pairs={{0,24},{1,8},{2,26},{3,10},{4,28},{5,12},{6,30},{7,14},{8,16},{9,0... | collective-permute-start | bytes 589832 | tf_op jit(solution)/shard_map/ppermute | solution.py:179
  272.8 25.6 %collective-permute-start.38 = (bf16[192,512]{1,0:T(8,128)(2,1)}, bf16[192,512]{1,0:T(8,128)(2,1)}, u32[]{:S(2)}, u32[]{:S(2)}) collective-permute-start(bf16[192,512]{1,0:T(8,128)(2,1)} %get-tuple-element.115), channel_id=1, source_target_pairs={{0,24},{1,8},{2,26},{3,10},{4,28},{5,12},{6,30},{7,14},{8,16},{9,0... | collective-permute-start | bytes 589832 | tf_op jit(solution)/shard_map/ppermute | solution.py:179
  274.8 24.8 %collective-permute-start.37 = (bf16[192,512]{1,0:T(8,128)(2,1)}, bf16[192,512]{1,0:T(8,128)(2,1)}, u32[]{:S(2)}, u32[]{:S(2)}) collective-permute-start(bf16[192,512]{1,0:T(8,128)(2,1)} %get-tuple-element.116), channel_id=1, source_target_pairs={{0,16},{1,0},{2,18},{3,2},{4,20},{5,4},{6,22},{7,6},{8,24},{9,8},{... | collective-permute-start | bytes 589832 | tf_op jit(solution)/shard_map/ppermute | solution.py:179
  276.6 24.2 %collective-permute-start.36 = (bf16[192,512]{1,0:T(8,128)(2,1)}, bf16[192,512]{1,0:T(8,128)(2,1)}, u32[]{:S(2)}, u32[]{:S(2)}) collective-permute-start(bf16[192,512]{1,0:T(8,128)(2,1)} %get-tuple-element.117), channel_id=1, source_target_pairs={{0,8},{1,24},{2,10},{3,26},{4,12},{5,28},{6,14},{7,30},{8,0},{9,16... | collective-permute-start | bytes 589832 | tf_op jit(solution)/shard_map/ppermute | solution.py:179
  278.4 23.7 %collective-permute-start.35 = (bf16[192,512]{1,0:T(8,128)(2,1)}, bf16[192,512]{1,0:T(8,128)(2,1)}, u32[]{:S(2)}, u32[]{:S(2)}) collective-permute-start(bf16[192,512]{1,0:T(8,128)(2,1)} %get-tuple-element.114), channel_id=1, source_target_pairs={{0,0},{1,16},{2,2},{3,18},{4,4},{5,20},{6,6},{7,22},{8,8},{9,24},{... | collective-permute-start | bytes 589832 | tf_op jit(solution)/shard_map/ppermute | solution.py:179
  280.4 47.9 %collective-permute-start.39 = (bf16[4,272,384]{2,1,0:T(8,128)(2,1)}, bf16[4,272,384]{2,1,0:T(8,128)(2,1)}, u32[]{:S(2)}, u32[]{:S(2)}) collective-permute-start(bf16[4,272,384]{2,1,0:T(8,128)(2,1)} %constant_dynamic-slice_fusion.9), channel_id=1, source_target_pairs={{0,4},{1,5},{2,6},{3,7},{4,0},{5,1},{6,2},{7,3},{8,12},{9,13},{10,... | collective-permute-start | bytes 2506760 | tf_op jit(solution)/shard_map/ppermute | solution.py:165
  298.4 8.9 %collective-permute-start.46 = (bf16[192,512]{1,0:T(8,128)(2,1)S(1)}, bf16[192,512]{1,0:T(8,128)(2,1)S(1)}, u32[]{:S(2)}, u32[]{:S(2)}) collective-permute-start(bf16[192,512]{1,0:T(8,128)(2,1)S(1)} %get-tuple-element.119), channel_id=1, source_target_pairs={{0,24},{1,8},{2,26},{3,10},{4,28},{5,12},{6,30},{7,14},{8,16},{9,0... | collective-permute-start | bytes 589832 | tf_op jit(solution)/shard_map/ppermute | solution.py:179
  299.6 18.6 %collective-permute-start.45 = (bf16[192,512]{1,0:T(8,128)(2,1)S(1)}, bf16[192,512]{1,0:T(8,128)(2,1)S(1)}, u32[]{:S(2)}, u32[]{:S(2)}) collective-permute-start(bf16[192,512]{1,0:T(8,128)(2,1)S(1)} %get-tuple-element.120), channel_id=1, source_target_pairs={{0,16},{1,0},{2,18},{3,2},{4,20},{5,4},{6,22},{7,6},{8,24},{9,8},{... | collective-permute-start | bytes 589832 | tf_op jit(solution)/shard_map/ppermute | solution.py:179
  300.8 18.6 %collective-permute-start.44 = (bf16[192,512]{1,0:T(8,128)(2,1)S(1)}, bf16[192,512]{1,0:T(8,128)(2,1)S(1)}, u32[]{:S(2)}, u32[]{:S(2)}) collective-permute-start(bf16[192,512]{1,0:T(8,128)(2,1)S(1)} %get-tuple-element.121), channel_id=1, source_target_pairs={{0,8},{1,24},{2,10},{3,26},{4,12},{5,28},{6,14},{7,30},{8,0},{9,16... | collective-permute-start | bytes 589832 | tf_op jit(solution)/shard_map/ppermute | solution.py:179
  302.1 17.3 %collective-permute-start.43 = (bf16[192,512]{1,0:T(8,128)(2,1)S(1)}, bf16[192,512]{1,0:T(8,128)(2,1)S(1)}, u32[]{:S(2)}, u32[]{:S(2)}) collective-permute-start(bf16[192,512]{1,0:T(8,128)(2,1)S(1)} %get-tuple-element.118), channel_id=1, source_target_pairs={{0,0},{1,16},{2,2},{3,18},{4,4},{5,20},{6,6},{7,22},{8,8},{9,24},{... | collective-permute-start | bytes 589832 | tf_op jit(solution)/shard_map/ppermute | solution.py:179
  307.3 23.7 %collective-permute-start.41 = (bf16[4,272,384]{2,1,0:T(8,128)(2,1)S(1)}, bf16[4,272,384]{2,1,0:T(8,128)(2,1)S(1)}, u32[]{:S(2)}, u32[]{:S(2)}) collective-permute-start(bf16[4,272,384]{2,1,0:T(8,128)(2,1)S(1)} %copy-done.48), channel_id=1, source_target_pairs={{0,2},{1,3},{2,0},{3,1},{4,6},{5,7},{6,4},{7,5},{8,10},{9,11},{10,... | collective-permute-start | bytes 2506760 | tf_op jit(solution)/shard_map/ppermute | solution.py:165
  318.2 9.5 %collective-permute-start.47 = (bf16[4,96,576]{2,1,0:T(8,128)(2,1)S(1)}, bf16[4,96,576]{2,1,0:T(8,128)(2,1)S(1)}, u32[]{:S(2)}, u32[]{:S(2)}) collective-permute-start(bf16[4,96,576]{2,1,0:T(8,128)(2,1)S(1)} %constant_dynamic-slice_fusion.1), channel_id=1, source_target_pairs={{0,4},{1,5},{2,6},{3,7},{4,0},{5,1},{6,2},{7,3},{8,12},{9,13},{10,... | collective-permute-start | bytes 1327112 | tf_op jit(solution)/shard_map/ppermute | solution.py:165
  327.9 8.1 %collective-permute-start.48 = (bf16[4,48,576]{2,1,0:T(8,128)(2,1)S(1)}, bf16[4,48,576]{2,1,0:T(8,128)(2,1)S(1)}, u32[]{:S(2)}, u32[]{:S(2)}) collective-permute-start(bf16[4,48,576]{2,1,0:T(8,128)(2,1)S(1)} %constant_dynamic-slice_fusion), channel_id=1, source_target_pairs={{0,2},{1,3},{2,0},{3,1},{4,6},{5,7},{6,4},{7,5},{8,10},{9,11},{10,... | collective-permute-start | bytes 663560 | tf_op jit(solution)/shard_map/ppermute | solution.py:165
  330.6 12.3 %collective-permute-start.40 = (bf16[4,136,384]{2,1,0:T(8,128)(2,1)S(1)}, bf16[4,136,384]{2,1,0:T(8,128)(2,1)S(1)}, u32[]{:S(2)}, u32[]{:S(2)}) collective-permute-start(bf16[4,136,384]{2,1,0:T(8,128)(2,1)S(1)} %constant_dynamic-slice_fusion.8), channel_id=1, source_target_pairs={{0,2},{1,3},{2,0},{3,1},{4,6},{5,7},{6,4},{7,5},{8,10},{9,11},{10,... | collective-permute-start | bytes 1253384 | tf_op jit(solution)/shard_map/ppermute | solution.py:165
  336.1 5.0 %collective-permute-start.51 = (bf16[48,576]{1,0:T(8,128)(2,1)S(1)}, bf16[48,576]{1,0:T(8,128)(2,1)S(1)}, u32[]{:S(2)}, u32[]{:S(2)}) collective-permute-start(bf16[48,576]{1,0:T(8,128)(2,1)S(1)} %get-tuple-element.163), channel_id=1, source_target_pairs={{0,24},{8,16},{16,8},{24,0},{1,25},{9,17},{17,9},{25,1},{2,26},{10... | collective-permute-start | bytes 165896 | tf_op jit(solution)/shard_map/ppermute | solution.py:165
  336.2 4.9 %collective-permute-start.50 = (bf16[48,576]{1,0:T(8,128)(2,1)S(1)}, bf16[48,576]{1,0:T(8,128)(2,1)S(1)}, u32[]{:S(2)}, u32[]{:S(2)}) collective-permute-start(bf16[48,576]{1,0:T(8,128)(2,1)S(1)} %get-tuple-element.164), channel_id=1, source_target_pairs={{0,8},{8,0},{16,24},{24,16},{1,9},{9,1},{17,25},{25,17},{2,10},{10... | collective-permute-start | bytes 165896 | tf_op jit(solution)/shard_map/ppermute | solution.py:165
  338.4 4.0 collective-permute-start.49
  339.8 7.0 %collective-permute-start.42 = (bf16[4,136,384]{2,1,0:T(8,128)(2,1)S(1)}, bf16[4,136,384]{2,1,0:T(8,128)(2,1)S(1)}, u32[]{:S(2)}, u32[]{:S(2)}) collective-permute-start(bf16[4,136,384]{2,1,0:T(8,128)(2,1)S(1)} %constant_dynamic-slice_fusion.6), channel_id=1, source_target_pairs={{0,4},{1,5},{2,6},{3,7},{4,0},{5,1},{6,2},{7,3},{8,12},{9,13},{10,... | collective-permute-start | bytes 1253384 | tf_op jit(solution)/shard_map/ppermute | solution.py:165
  342.5 8.1 %collective-permute-start.52 = (bf16[2,48,576]{2,1,0:T(8,128)(2,1)S(1)}, bf16[2,48,576]{2,1,0:T(8,128)(2,1)S(1)}, u32[]{:S(2)}, u32[]{:S(2)}) collective-permute-start(bf16[2,48,576]{2,1,0:T(8,128)(2,1)S(1)} %pad_maximum_fusion.27), channel_id=1, source_target_pairs={{0,2},{1,3},{2,0},{3,1},{4,6},{5,7},{6,4},{7,5},{8,10},{9,11},{10,... | collective-permute-start | bytes 331784 | tf_op jit(solution)/shard_map/ppermute | solution.py:165
  347.0 6.7 %collective-permute-start.57 = (bf16[136,768]{1,0:T(8,128)(2,1)S(1)}, bf16[136,768]{1,0:T(8,128)(2,1)S(1)}, u32[]{:S(2)}, u32[]{:S(2)}) collective-permute-start(bf16[136,768]{1,0:T(8,128)(2,1)S(1)} %get-tuple-element.105), channel_id=1, source_target_pairs={{0,24},{8,16},{16,8},{24,0},{1,25},{9,17},{17,9},{25,1},{2,26},{10... | collective-permute-start | bytes 626696 | tf_op jit(solution)/shard_map/ppermute | solution.py:165
  348.3 18.5 %collective-permute-start.56 = (bf16[136,768]{1,0:T(8,128)(2,1)S(1)}, bf16[136,768]{1,0:T(8,128)(2,1)S(1)}, u32[]{:S(2)}, u32[]{:S(2)}) collective-permute-start(bf16[136,768]{1,0:T(8,128)(2,1)S(1)} %get-tuple-element.104), channel_id=1, source_target_pairs={{0,16},{8,24},{16,0},{24,8},{1,17},{9,25},{17,1},{25,9},{2,18},{10... | collective-permute-start | bytes 626696 | tf_op jit(solution)/shard_map/ppermute | solution.py:165
  349.7 17.0 %collective-permute-start.55 = (bf16[136,768]{1,0:T(8,128)(2,1)S(1)}, bf16[136,768]{1,0:T(8,128)(2,1)S(1)}, u32[]{:S(2)}, u32[]{:S(2)}) collective-permute-start(bf16[136,768]{1,0:T(8,128)(2,1)S(1)} %get-tuple-element.103), channel_id=1, source_target_pairs={{0,8},{8,0},{16,24},{24,16},{1,9},{9,1},{17,25},{25,17},{2,10},{10... | collective-permute-start | bytes 626696 | tf_op jit(solution)/shard_map/ppermute | solution.py:165
  350.6 18.2 %collective-permute-start.53 = (bf16[2,96,576]{2,1,0:T(8,128)(2,1)S(1)}, bf16[2,96,576]{2,1,0:T(8,128)(2,1)S(1)}, u32[]{:S(2)}, u32[]{:S(2)}) collective-permute-start(bf16[2,96,576]{2,1,0:T(8,128)(2,1)S(1)} %pad_maximum_fusion.23), channel_id=1, source_target_pairs={{0,4},{1,5},{2,6},{3,7},{4,0},{5,1},{6,2},{7,3},{8,12},{9,13},{10,... | collective-permute-start | bytes 663560 | tf_op jit(solution)/shard_map/ppermute | solution.py:165
  366.9 3.6 collective-permute-start.58
  367.3 3.6 collective-permute-start.60
  371.0 7.1 %collective-permute-start.61 = (bf16[1,272,384]{2,1,0:T(8,128)(2,1)S(1)}, bf16[1,272,384]{2,1,0:T(8,128)(2,1)S(1)}, u32[]{:S(2)}, u32[]{:S(2)}) collective-permute-start(bf16[1,272,384]{2,1,0:T(8,128)(2,1)S(1)} %pad_maximum_fusion.26), channel_id=1, source_target_pairs={{0,2},{1,3},{2,0},{3,1},{4,6},{5,7},{6,4},{7,5},{8,10},{9,11},{10,... | collective-permute-start | bytes 626696 | tf_op jit(solution)/shard_map/ppermute | solution.py:165
  372.5 12.7 %collective-permute-start.54 = (bf16[2,192,576]{2,1,0:T(8,128)(2,1)S(1)}, bf16[2,192,576]{2,1,0:T(8,128)(2,1)S(1)}, u32[]{:S(2)}, u32[]{:S(2)}) collective-permute-start(bf16[2,192,576]{2,1,0:T(8,128)(2,1)S(1)} %pad_maximum_fusion.17), channel_id=1, source_target_pairs={{0,1},{1,0},{2,3},{3,2},{4,5},{5,4},{6,7},{7,6},{8,9},{9,8},{10,11... | collective-permute-start | bytes 1327112 | tf_op jit(solution)/shard_map/ppermute | solution.py:165
  376.5 6.8 %collective-permute-start.59 = (bf16[1,272,384]{2,1,0:T(8,128)(2,1)S(1)}, bf16[1,272,384]{2,1,0:T(8,128)(2,1)S(1)}, u32[]{:S(2)}, u32[]{:S(2)}) collective-permute-start(bf16[1,272,384]{2,1,0:T(8,128)(2,1)S(1)} %pad_maximum_fusion.25), channel_id=1, source_target_pairs={{0,4},{1,5},{2,6},{3,7},{4,0},{5,1},{6,2},{7,3},{8,12},{9,13},{10,... | collective-permute-start | bytes 626696 | tf_op jit(solution)/shard_map/ppermute | solution.py:165
  384.4 11.5 %collective-permute-start.62 = (bf16[1,544,768]{2,1,0:T(8,128)(2,1)}, bf16[1,544,768]{2,1,0:T(8,128)(2,1)}, u32[]{:S(2)}, u32[]{:S(2)}) collective-permute-start(bf16[1,544,768]{2,1,0:T(8,128)(2,1)} %maximum_maximum_fusion.2), channel_id=1, source_target_pairs={{0,1},{1,0},{2,3},{3,2},{4,5},{5,4},{6,7},{7,6},{8,9},{9,8},{10,11... | collective-permute-start | bytes 2506760 | tf_op jit(solution)/shard_map/ppermute | solution.py:165
  (63 other events, 525.1 us)

commit v3 on v2

--- a/solution.py
+++ b/solution.py
@@ -213,73 +213,133 @@
     return jnp.stack([pick(blocks, z ^ j) for j in range(size)])
 
 
-def orders(ranks):
-    far = []
+def far(ranks):
+    bits = []
     bit = 2
     while bit < ranks:
-        far.append(bit)
+        bits.append(bit)
         bit *= 2
-    return far, far[::-1]
-
-
-def place(r, bits):
-    total = 0
-    for k, bit in enumerate(bits):
-        total = total + jnp.where(r & bit != 0, 1 << k, 0)
+    return bits
+
+
+def stage_bit(core, ranks, stage):
+    bits = far(ranks)
+    return bits[stage] if core == 0 else bits[len(bits) - 1 - stage]
+
+
+def stage_swap(values, ranks, stage):
+    return lax.ppermute(values, "rep", [(i, i ^ stage_bit(i & 1, ranks, stage)) for i in range(ranks)])
+
+
+def stage_upper(r, ranks, stage):
+    bit = jnp.where(r & 1 == 0, stage_bit(0, ranks, stage), stage_bit(1, ranks, stage))
+    return r & bit != 0
+
+
+def place(r, ranks):
+    stages = len(far(ranks))
+    total = jnp.where(r & 1 != 0, 1 << stages, 0)
+    for stage in range(stages):
+        total = total + jnp.where(stage_upper(r, ranks, stage), 1 << stage, 0)
     return total
 
 
-def grow(values, r, ranks, bits):
-    for bit in bits:
-        other = swap(values, "rep", ranks, bit)
-        upper = r & bit != 0
-        values = jnp.concatenate(
-            [jnp.where(upper, other, values), jnp.where(upper, values, other)], axis=1
-        )
+def join(mine, other, upper):
+    return jnp.concatenate([jnp.where(upper, other, mine), jnp.where(upper, mine, other)], axis=1)
+
+
+def cut(values, upper):
+    half = values.shape[1] // 2
+    mine = jnp.where(upper, half, 0)
+    sent = lax.dynamic_slice_in_dim(values, half - mine, half, 1)
+    return sent, lax.dynamic_slice_in_dim(values, mine, half, 1)
+
+
+def add(one, two):
+    return (one.astype(F32) + two.astype(F32)).astype(BF16)
+
+
+def grow(values, r, ranks, stages):
+    for stage in stages:
+        values = join(values, stage_swap(values, ranks, stage), stage_upper(r, ranks, stage))
     return values
 
 
-def shrink(values, r, ranks, bits):
-    for bit in bits:
-        half = values.shape[1] // 2
-        mine = jnp.where(r & bit != 0, half, 0)
-        sent = lax.dynamic_slice_in_dim(values, half - mine, half, 1)
-        kept = lax.dynamic_slice_in_dim(values, mine, half, 1)
-        other = swap(sent, "rep", ranks, bit)
-        values = (kept.astype(F32) + other.astype(F32)).astype(BF16)
+def grow_core(values, r, ranks):
+    return join(values, swap(values, "rep", ranks, 1), r & 1 != 0)
+
+
+def shrink(values, r, ranks, stages):
+    for stage in stages:
+        sent, kept = cut(values, stage_upper(r, ranks, stage))
+        values = add(kept, stage_swap(sent, ranks, stage))
     return values
 
 
-def halves(values):
-    middle = values.shape[-1] // 2
-    return values[..., :middle], values[..., middle:]
+def shrink_core(values, r, ranks):
+    sent, kept = cut(values, r & 1 != 0)
+    return add(kept, swap(sent, "rep", ranks, 1))
 
 
 def split_rows(shard, r, ranks):
     rows = shard.shape[0] // ranks
-    one, two = orders(ranks)
-    left, right = halves(shard)
-    return jnp.concatenate(
-        [
-            lax.dynamic_slice_in_dim(left, place(r, one + [1]) * rows, rows, 0),
-            lax.dynamic_slice_in_dim(right, place(r, two + [1]) * rows, rows, 0),
+    return lax.dynamic_slice_in_dim(shard, place(r, ranks) * rows, rows, 0)
+
+
+def finish_into_kernel(low_ref, high_ref, weight_ref, gain_ref, sum_ref, gain_sum_ref):
+    part = sum_ref.shape[0]
+    total = jnp.zeros((part, 1), F32)
+    for t in range(3):
+        blocks = [ref[g, :, t * part : (t + 1) * part] for ref in (low_ref, high_ref) for g in range(2)]
+        row = jnp.concatenate([block.astype(F32) for block in blocks], axis=1)
+        width = row.shape[1]
+        sum_ref[:, t * width : (t + 1) * width] = row
+        weight = weight_ref[:, t * width : (t + 1) * width].astype(F32)
+        total = total + jnp.sum(row * weight, axis=1, keepdims=True)
+    gain_sum_ref[...] = total / gain_ref[...].astype(F32)
+
+
+def finish_into(low, high, weight, gain):
+    part = weight.shape[0]
+    return pl.pallas_call(
+        finish_into_kernel,
+        out_shape=[
+            jax.ShapeDtypeStruct(weight.shape, F32),
+            jax.ShapeDtypeStruct((part, 1), F32),
         ],
-        axis=1,
-    )
-
-
-def grow_both(values, r, ranks):
-    one, two = orders(ranks)
-    left, right = halves(values)
-    return jnp.concatenate([grow(left, r, ranks, one), grow(right, r, ranks, two)], axis=2)
-
-
-def shrink_both(values, r, ranks):
-    one, two = orders(ranks)
-    left, right = halves(values)
-    return jnp.concatenate(
-        [shrink(left, r, ranks, one[::-1]), shrink(right, r, ranks, two[::-1])], axis=2
-    )
+        compiler_params=pltpu.CompilerParams(vmem_limit_bytes=32 * 2**20),
+        name="finish_into",
+    )(low, high, weight, gain[:, None])
+
+
+def finish_rest_kernel(grads_ref, weight_ref, gain_ref, out_ref, expand_ref, contract_ref, gain_sum_ref):
+    part, width = out_ref.shape
+    hidden = contract_ref.shape[0]
+    total = jnp.zeros((part, 1), F32)
+    out_ref[...] = grads_ref[:part].astype(F32)
+    for t in range(3):
+        rows = grads_ref[(1 + t) * part : (2 + t) * part].astype(F32)
+        expand_ref[:, t * width : (t + 1) * width] = rows
+        weight = weight_ref[:, t * width : (t + 1) * width].astype(F32)
+        total = total + jnp.sum(rows * weight, axis=1, keepdims=True)
+    contract_ref[...] = grads_ref[4 * part : 4 * part + hidden].astype(F32)
+    gain_sum_ref[...] = total / gain_ref[...].astype(F32)
+
+
+def finish_rest(grads, weight, gain, hidden):
+    part = weight.shape[0]
+    width = grads.shape[1]
+    return pl.pallas_call(
+        finish_rest_kernel,
+        out_shape=[
+            jax.ShapeDtypeStruct((part, width), F32),
+            jax.ShapeDtypeStruct(weight.shape, F32),
+            jax.ShapeDtypeStruct((hidden, width), F32),
+            jax.ShapeDtypeStruct((part, 1), F32),
+        ],
+        compiler_params=pltpu.CompilerParams(vmem_limit_bytes=32 * 2**20),
+        name="finish_rest",
+    )(grads, weight, gain[:, None])
 
 
 def local(size, ranks, tokens, gain_a, projection_in, attention_out, gain_b, expansion, contraction, cotangent):
@@ -294,18 +354,19 @@
     hidden = contraction.shape[0]
     heads = HEADS // size
 
+    stages = list(range(len(far(ranks))))
     columns = [projection_in[:, t * width : (t + 1) * width] for t in range(3)]
     piece = split_rows(jnp.concatenate(columns, axis=0), r, ranks)
-    pieces = exchange([piece] * size, size)
-    gains = jnp.stack([gain_a, gain_b])
-    gains = exchange([gains] * size, size)
+    rows = piece.shape[0]
+    gains = jnp.pad(jnp.concatenate([gain_a, gain_b])[None], ((0, 7), (0, width - 2 * part)))
+    pieces = exchange([jnp.concatenate([piece, gains], axis=0)] * size, size)
     pair, other, second = collect(after(own, *pieces), home, size, ranks)
-    into = grow(grow_both(reorder(jnp.stack(pieces), z, size), r, ranks), r, ranks, [1])
+    pieces = reorder(jnp.stack(pieces), z, size)
+    into = grow_core(grow(pieces[:, :rows], r, ranks, stages), r, ranks)
     into = into.reshape(size, 3, part, width)
     into = [into[:, t].reshape(width, width) for t in range(3)]
-    gains = reorder(jnp.stack(gains), z, size)
-    gain_one = gains[:, 0].reshape(width).astype(F32)
-    gain_two = gains[:, 1].reshape(width).astype(F32)
+    gain_one = pieces[:, rows, :part].reshape(width).astype(F32)
+    gain_two = pieces[:, rows, part : 2 * part].reshape(width).astype(F32)
 
     freqs = THETA ** (-(jnp.arange(HALF, dtype=F32) * (2.0 / HEAD_DIM)))
     places = jnp.concatenate([(group ^ d) * count + jnp.arange(count, dtype=jnp.int32) for d in range(size)])
@@ -333,19 +394,20 @@
     stacked = jnp.concatenate([attention_out] + columns + [contraction], axis=0)
     pad = -stacked.shape[0] % (8 * ranks)
     stacked = jnp.concatenate([stacked, jnp.zeros((pad, width), BF16)], axis=0)
-    piece = split_rows(after(stacked, second), r, ranks)
+    piece = split_rows(after(stacked, queries), r, ranks)
     pieces = exchange([piece] * size, size)
+    rest = reorder(jnp.stack(pieces), z, size)
     merged = []
     logs = []
-    rest = reorder(jnp.stack(pieces), z, size)
+    ahead = []
     for head in range(heads):
-        tied = keys if head == 0 else after(keys, rest)
-        if head == 1:
-            rest = grow_both(rest, r, ranks)
-        out, log = attend(head, queries, tied, values_turned)
+        out, log = attend(head, queries, after(keys, *ahead), values_turned)
         merged.append(out)
         logs.append(log)
-    rest = grow(rest, r, ranks, [1])
+        if head < 2:
+            ahead = [rest]
+            rest = grow(after(rest, out), r, ranks, stages[:1] if head == 0 else stages[1:])
+    rest = grow_core(after(rest, merged[-1]), r, ranks)
     own_merged = jnp.concatenate(merged, axis=0)
 
     arrived = trade_out([own_merged[:, d * count : (d + 1) * count] for d in range(size)], size, ranks)
@@ -370,6 +432,7 @@
     state_back = upstream.astype(F32) + layer_norm_back(state, gain_two, normed_two_back)
     state_low = state_back.astype(BF16)
     merged_back = mul(out_weight, state_low, NT).astype(BF16)
+    upstream, active, inner_back, state_low = after((upstream, active, inner_back, state_low), merged_back)
     arrived = trade_back([merged_back[d * part : (d + 1) * part] for d in range(size)], size, ranks)
     own_upstream = jnp.concatenate(arrived, axis=1)
 
@@ -382,30 +445,36 @@
     grads = jnp.concatenate(
         [out_grad] + expansion_grad + [contraction_grad, jnp.zeros((size, pad, width), BF16)], axis=1
     )
-    grads = shrink(grads, r, ranks, [1])
+    grads = shrink_core(grads, r, ranks)
 
     turned_backs = []
     received = []
-    tied = after(own_upstream, grads)
+    ahead = [grads]
     for head in range(heads):
-        if head == 2:
-            grads = shrink_both(grads, r, ranks)
-            tied = after(own_upstream, grads, *received[0])
         grad = attend_back(
-            head, queries, keys_turned, keys, values, tied, own_merged, logs[head], cosine, sine
+            head, queries, keys_turned, keys, values, after(own_upstream, *ahead), own_merged, logs[head], cosine, sine
         )
         turned_backs.append(grad)
-        received.append(trade_out([grad[:, d * count : (d + 1) * count] for d in range(size)], size, ranks))
+        if head == 0:
+            received = trade_out([grad[:, d * count : (d + 1) * count] for d in range(size)], size, ranks)
+            grads = shrink(grads, r, ranks, stages[:0:-1])
+            ahead = [grads]
+        if head == 1:
+            grads = shrink(grads, r, ranks, stages[:1])
+            ahead = [grads] + received
+    later = jnp.concatenate(turned_backs[1:], axis=0)
+    later = trade_out([later[:, d * count : (d + 1) * count] for d in range(size)], size, ranks)
+    received = [jnp.concatenate(both, axis=0) for both in zip(received, later)]
 
     grads = exchange([pick(grads, z ^ d) for d in range(size)], size)
     grads = sum(part.astype(F32) for part in grads).astype(BF16)[None]
-    grads = grow(grow_both(grads, r, ranks), r, ranks, [1])[0].astype(F32)
-    attention_out_sum = grads[:part]
-    expansion_sum = jnp.concatenate([grads[(1 + t) * part : (2 + t) * part] for t in range(3)], axis=1)
-    contraction_sum = grads[4 * part : 4 * part + hidden]
-
-    projected_back = jnp.stack([jnp.stack(pieces) for pieces in received], axis=1)
-    projected_back = reorder(projected_back, z, size).reshape(size, heads, 3, HEAD_DIM, count)
+    owned = grads
+    grads = grow_core(grow(grads, r, ranks, stages), r, ranks)[0]
+    attention_out_sum, expansion_sum, contraction_sum, gain_two_sum = finish_rest(
+        grads, expansion, gain_b, hidden
+    )
+
+    projected_back = reorder(jnp.stack(received), z, size).reshape(size, heads, 3, HEAD_DIM, count)
     projected_back = projected_back.transpose(2, 0, 1, 3, 4).reshape(3, width, count)
     normed_back = sum(mul(projected_back[t], into[t], TT) for t in range(3))
     token_grad = (state_back + layer_norm_back(inputs, gain_one, normed_back))[None]
@@ -413,27 +482,25 @@
     all_backs = jnp.stack(turned_backs).reshape(heads, 3, HEAD_DIM, size * count)
     all_backs = all_backs.transpose(1, 0, 2, 3).reshape(3 * part, size * count)
     into_grad = mul(normed, all_backs, TT).astype(BF16).reshape(size, part, 3 * part)
-    into_grad = shrink(into_grad, r, ranks, orders(ranks)[1])
+    into_grad = after(shrink(into_grad, r, ranks, stages[::-1]), owned)
     arrived = exchange([pick(into_grad, z ^ d) for d in range(size)], size)
     even = (arrived[0].astype(F32) + arrived[2].astype(F32)).astype(BF16)
     odd = (arrived[1].astype(F32) + arrived[3].astype(F32)).astype(BF16)
     low = z & 1 == 0
     into_sum = jnp.stack([jnp.where(low, even, odd), jnp.where(low, odd, even)])
-    into_sum = grow(into_sum, r, ranks, orders(ranks)[0])
+    into_sum = grow(into_sum, r, ranks, stages)
     partner = swap(into_sum, "rep", ranks, 1)
     low = core == 0
-    into_sum = jnp.concatenate([jnp.where(low, into_sum, partner), jnp.where(low, partner, into_sum)], axis=0)
-    into_sum = into_sum.reshape(size, part, 3, part).transpose(1, 2, 0, 3).reshape(part, 3 * width).astype(F32)
-
-    gain_one_sum = jnp.sum(into_sum * projection_in.astype(F32), axis=1) / gain_a.astype(F32)
-    gain_two_sum = jnp.sum(expansion_sum * expansion.astype(F32), axis=1) / gain_b.astype(F32)
+    into_sum, gain_one_sum = finish_into(
+        jnp.where(low, into_sum, partner), jnp.where(low, partner, into_sum), projection_in, gain_a
+    )
     return (
         block_output,
         token_grad,
-        gain_one_sum,
+        gain_one_sum[:, 0],
         into_sum,
         attention_out_sum,
-        gain_two_sum,
+        gain_two_sum[:, 0],
         expansion_sum,
         contraction_sum,
     )

time: 409 us -> 377 us (0.922)
  local copies, waits for them, and re-layouts: 40.9 us -> 29 us
  starting transfers between devices: 91.7 us -> 80.9 us
  waiting for transfers between devices: 116 us -> 109 us
  other arithmetic: 53 us -> 47.3 us
    ppermute x41 -> x18, waiting for transfers between devices: 67.8 us -> 35.9 us  [swap(): return lax.ppermute(values, axis, [(i, i ^ offset) for i in range(size)])]
    ppermute x0 -> x12, waiting for transfers between devices: none -> 28.5 us  [stage_swap(): lax.ppermute(values, 'rep', [(i, i ^ stage_bit(i & 1, ranks, stage)) for...]
    ppermute x41 -> x18, starting transfers between devices: 47.6 us -> 26.1 us  [swap(): return lax.ppermute(values, axis, [(i, i ^ offset) for i in range(size)])]
    ppermute x0 -> x12, starting transfers between devices: none -> 8.66 us  [stage_swap(): lax.ppermute(values, 'rep', [(i, i ^ stage_bit(i & 1, ranks, stage)) for...]
    convert_element_type x5 -> x2, local copies, waits for them, and re-layouts: 7.98 us -> 0.15 us  [the longest x1 0.08 us: local(): gain_one = pieces[:, rows, :part].reshape(width).astype(F32)]
    unnamed x145 -> x105, local copies, waits for them, and re-layouts: 17 us -> 13.2 us
    ppermute x22 -> x18, waiting for transfers between devices: 48.7 us -> 44.9 us  [column(): return lax.ppermute(values, ('fsdp', 'rep'), full)]
    select_n x15 -> x12, other arithmetic: 11.2 us -> 8.3 us  [the longest x10 4.71 us: join(): jnp.where(upper, other, mine)]
  transfers between devices with their start and end apart: 63 -> 48, of which waited for: 24 -> 20; matrix products, arithmetic and copies ran while one was open for 18% -> 13% of each run, Pallas kernels for 14% -> 16%
where the time goes in v3:
time: 377 us; the launch traced here: 371 us
  waiting for transfers between devices  109 us (29%)
  starting transfers between devices  80.9 us (21%)
  Pallas kernels  72.9 us (19%)
  other arithmetic  47.3 us (13%)
  matrix products  29.2 us (8%)
  local copies, waits for them, and re-layouts  29 us (8%)
    ppermute x18, starting transfers between devices, column(): return lax.ppermute(values, ('fsdp', 'rep'), full)  46.2 us
    ppermute x18, waiting for transfers between devices, column(): return lax.ppermute(values, ('fsdp', 'rep'), full)  44.9 us
    pallas_call x3, Pallas kernels, attend_back(): pl.pallas_call(attend_back_kernel, grid=(count // step,), in_specs=[some,...  39.3 us
    ppermute x18, waiting for transfers between devices, swap(): return lax.ppermute(values, axis, [(i, i ^ offset) for i in range(size)])  35.9 us
    pallas_call x3, Pallas kernels, attend(): pl.pallas_call(attend_kernel, grid=(count // step,), in_specs=[pl.BlockSp...  30 us
    dot_general x22, matrix products, mul(): return lax.dot_general(a, b, dims, preferred_element_type=F32)  29.2 us
    ppermute x12, waiting for transfers between devices, stage_swap(): lax.ppermute(values, 'rep', [(i, i ^ stage_bit(i & 1, ranks, stage)) for...  28.5 us
    ppermute x18, starting transfers between devices, swap(): return lax.ppermute(values, axis, [(i, i ^ offset) for i in range(size)])  26.1 us
  transfers between devices with their start and end apart: 48, of which 20 were waited for; matrix products, arithmetic and copies ran while one was open for 13% of the time, Pallas kernels for 16%

profile of v3, /device:TPU:1, one launch (start us, length us, event | category | flops | bytes accessed | tf_op | source)
XLA Modules:
  0.0 370.8 jit_solution(3067793486458890445)
XLA Ops:
  2.8 4.2 %collective-permute-start.2 = (bf16[80,768]{1,0:T(8,128)(2,1)S(1)}, bf16[80,768]{1,0:T(8,128)(2,1)S(1)}, u32[]{:S(2)}, u32[]{:S(2)}) collective-permute-start(bf16[80,768]{1,0:T(8,128)(2,1)S(1)} %get-tuple-element.162), channel_id=1, source_target_pairs={{0,24},{8,16},{16,8},{24,0},{1,25},{9,17},{17,9},{25,1},{2,26},{10... | collective-permute-start | bytes 368648 | tf_op jit(solution)/shard_map/ppermute | solution.py:165
  7.3 2.7 collective-permute-done.2
  10.1 6.9 %collective-permute-done.1 = bf16[80,768]{1,0:T(8,128)(2,1)S(1)} collective-permute-done((bf16[80,768]{1,0:T(8,128)(2,1)S(1)}, bf16[80,768]{1,0:T(8,128)(2,1)S(1)}, u32[]{:S(2)}, u32[]{:S(2)}) %collective-permute-start.1) | collective-permute-done | bytes 122912 | tf_op jit(solution)/shard_map/ppermute | solution.py:165
  18.6 6.1 %collective-permute-done.3 = bf16[4,72,768]{2,1,0:T(8,128)(2,1)S(1)} collective-permute-done((bf16[4,72,768]{2,1,0:T(8,128)(2,1)S(1)}, bf16[4,72,768]{2,1,0:T(8,128)(2,1)S(1)}, u32[]{:S(2)}, u32[]{:S(2)}) %collective-permute-start.3) | collective-permute-done | bytes 442400 | tf_op jit(solution)/shard_map/ppermute | solution.py:231
  26.1 2.2 collective-permute-start.6
  28.5 18.5 %collective-permute-done.6 = bf16[512,768]{1,0:T(8,128)(2,1)} collective-permute-done((bf16[512,768]{1,0:T(8,128)(2,1)S(1)}, bf16[512,768]{1,0:T(8,128)(2,1)}, u32[]{:S(2)}, u32[]{:S(2)}) %collective-permute-start.6) | collective-permute-done | bytes 786464 | tf_op jit(solution)/shard_map/ppermute | solution.py:179
  47.0 2.4 collective-permute-start.7
  52.2 7.8 %collective-permute-done.7 = bf16[512,768]{1,0:T(8,128)(2,1)} collective-permute-done((bf16[512,768]{1,0:T(8,128)(2,1)}, bf16[512,768]{1,0:T(8,128)(2,1)}, u32[]{:S(2)}, u32[]{:S(2)}) %collective-permute-start.7) | collective-permute-done | bytes 786464 | tf_op jit(solution)/shard_map/ppermute | solution.py:179
  60.0 1.5 broadcast_select_fusion.13
  62.7 2.2 broadcast_select_fusion.3
  67.3 2.2 fusion.9
  69.5 1.5 fusion.48
  72.2 1.6 constant_dynamic-slice_fusion.21
  73.8 4.9 %collective-permute-start.11 = (bf16[136,768]{1,0:T(8,128)(2,1)}, bf16[136,768]{1,0:T(8,128)(2,1)S(1)}, u32[]{:S(2)}, u32[]{:S(2)}) collective-permute-start(bf16[136,768]{1,0:T(8,128)(2,1)} %constant_dynamic-slice_fusion.21), channel_id=1, source_target_pairs={{0,24},{8,16},{16,8},{24,0},{1,25},{9,17},{17,9},{25,1},{2,26},{10... | collective-permute-start | bytes 626696 | tf_op jit(solution)/shard_map/ppermute | solution.py:165
  79.1 1.5 fusion.46
  81.7 3.6 convolution_convert_fusion.2.v_ref
  85.3 10.0 %attend.3 = (bf16[64,2048]{1,0:T(8,128)(2,1)S(1)}, f32[1,2048]{1,0:T(1,128)S(1)}) custom-call(bf16[192,2048]{1,0:T(8,128)(2,1)S(1)} %bitcast.149, bf16[3,2048,64]{2,1,0:T(8,128)(2,1)S(1)} %bitcast.143, bf16[192,2048]{1,0:T(8,128)(2,1)S(1)} %convolution_convert_fusion.2.v_ref), custom_call_target="tpu_custom_call" | custom-call | flops 10737418240 | bytes 1048576 | tf_op jit(solution)/shard_map/attend/pallas_call | solution.py:66
  98.0 10.0 %attend.4 = (bf16[64,2048]{1,0:T(8,128)(2,1)S(1)}, f32[1,2048]{1,0:T(1,128)S(1)}) custom-call(bf16[192,2048]{1,0:T(8,128)(2,1)S(1)} %bitcast.150, bf16[3,2048,64]{2,1,0:T(8,128)(2,1)S(1)} %bitcast.144, bf16[192,2048]{1,0:T(8,128)(2,1)S(1)} %convolution_convert_fusion.2.v_ref), custom_call_target="tpu_custom_call" | custom-call | flops 10737418240 | bytes 1048576 | tf_op jit(solution)/shard_map/attend/pallas_call | solution.py:66
  111.0 10.0 %attend.5 = (bf16[64,2048]{1,0:T(8,128)(2,1)S(1)}, f32[1,2048]{1,0:T(1,128)S(1)}) custom-call(bf16[192,2048]{1,0:T(8,128)(2,1)S(1)} %bitcast.151, bf16[3,2048,64]{2,1,0:T(8,128)(2,1)S(1)} %bitcast.145, bf16[192,2048]{1,0:T(8,128)(2,1)S(1)} %convolution_convert_fusion.2.v_ref), custom_call_target="tpu_custom_call" | custom-call | flops 10737418240 | bytes 1048576 | tf_op jit(solution)/shard_map/attend/pallas_call | solution.py:66
  120.9 9.4 %collective-permute-done.17 = bf16[4,272,768]{2,1,0:T(8,128)(2,1)S(1)} collective-permute-done((bf16[4,272,768]{2,1,0:T(8,128)(2,1)S(1)}, bf16[4,272,768]{2,1,0:T(8,128)(2,1)S(1)}, u32[]{:S(2)}, u32[]{:S(2)}) %collective-permute-start.17) | collective-permute-done | bytes 1671200 | tf_op jit(solution)/shard_map/ppermute | solution.py:231
  130.6 1.9 pad_maximum_fusion.1
  132.5 2.3 collective-permute-start.18
  136.6 3.7 %collective-permute-start.13 = (bf16[192,512]{1,0:T(8,128)(2,1)}, bf16[192,512]{1,0:T(8,128)(2,1)}, u32[]{:S(2)}, u32[]{:S(2)}) collective-permute-start(bf16[192,512]{1,0:T(8,128)(2,1)} %get-tuple-element.143), channel_id=1, source_target_pairs={{0,0},{1,16},{2,2},{3,18},{4,4},{5,20},{6,6},{7,22},{8,8},{9,24},{... | collective-permute-start | bytes 589832 | tf_op jit(solution)/shard_map/ppermute | solution.py:179
  140.3 1.6 collective-permute-start.14
  142.0 2.7 collective-permute-start.16
  144.7 3.8 %collective-permute-done.13 = bf16[192,512]{1,0:T(8,128)(2,1)} collective-permute-done((bf16[192,512]{1,0:T(8,128)(2,1)}, bf16[192,512]{1,0:T(8,128)(2,1)}, u32[]{:S(2)}, u32[]{:S(2)}) %collective-permute-start.13) | collective-permute-done | bytes 196640 | tf_op jit(solution)/shard_map/ppermute | solution.py:179
  149.4 1.6 collective-permute-done.14
  152.0 4.7 %collective-permute-done.15 = bf16[192,512]{1,0:T(8,128)(2,1)S(1)} collective-permute-done((bf16[192,512]{1,0:T(8,128)(2,1)S(1)}, bf16[192,512]{1,0:T(8,128)(2,1)S(1)}, u32[]{:S(2)}, u32[]{:S(2)}) %collective-permute-start.15) | collective-permute-done | bytes 196640 | tf_op jit(solution)/shard_map/ppermute | solution.py:179
  156.7 3.4 broadcast_select_fusion
  168.3 5.2 %convert_multiply_fusion.1 = (f32[512,1152]{1,0:T(8,128)S(1)}, f32[512,1152]{1,0:T(8,128)S(1)}) fusion(bf16[512,1152]{1,0:T(8,128)(2,1)S(1)} %fusion.10, f32[512,768]{1,0:T(8,128)S(1)} %fusion.76, f32[512,768]{1,0:T(8,128)S(1)} %fusion.75), kind=kLoop, calls=%fused_computation.26 | loop fusion | flops 39518208 | bytes 9043968 | tf_op jit(solution)/shard_map/transpose(jvp())/mul | solution.py:47
  178.0 1.8 fusion.65
  179.7 1.7 convolution_convert_fusion.8
  186.4 2.2 constant_dynamic-slice_fusion.8
  188.7 1.4 copy-done.12
  191.6 1.5 fusion.26
  193.1 2.5 copy.28
  197.0 7.0 %collective-permute-start.19 = (bf16[192,512]{1,0:T(8,128)(2,1)S(1)}, bf16[192,512]{1,0:T(8,128)(2,1)S(1)}, u32[]{:S(2)}, u32[]{:S(2)}) collective-permute-start(bf16[192,512]{1,0:T(8,128)(2,1)S(1)} %get-tuple-element.139), channel_id=1, source_target_pairs={{0,0},{1,16},{2,2},{3,18},{4,4},{5,20},{6,6},{7,22},{8,8},{9,24},{... | collective-permute-start | bytes 589832 | tf_op jit(solution)/shard_map/ppermute | solution.py:179
  205.0 4.4 %fusion.27 = bf16[1,512,768]{2,1,0:T(8,128)(2,1)} fusion(f32[512,768]{1,0:T(8,128)} %copy-done.8, bf16[512,1152]{1,0:T(8,128)(2,1)} %copy-done.21, bf16[1152,768]{1,0:T(8,128)(2,1)} %bitcast.171), kind=kOutput, calls=%fused_computation.94 | convolution fusion | flops 906756096 | bytes 5308416 | tf_op jit(solution)/shard_map/dot_general | solution.py:26
  209.3 2.8 collective-permute-start.22
  213.5 2.8 add_convert_fusion
  217.8 13.1 %attend_back.3 = bf16[192,2048]{1,0:T(8,128)(2,1)S(1)} custom-call(bf16[192,2048]{1,0:T(8,128)(2,1)S(1)} %bitcast.152, bf16[192,2048]{1,0:T(8,128)(2,1)S(1)} %bitcast.140, bf16[3,2048,64]{2,1,0:T(8,128)(2,1)S(1)} %bitcast.146, bf16[3,2048,64]{2,1,0:T(8,128)(2,1)} %bitcast.173, bf16[192,2048]{1,0:T(8,128)(2,1)S(1)} %constant_dynamic-update-slice_fusion.10.up_ref, ...), custom_call_target="tpu_custom_call" | custom-call | flops 15032385536 | bytes 2097152 | tf_op jit(solution)/shard_map/attend_back/pallas_call | solution.py:133
  230.9 5.8 %collective-permute-start.24 = (bf16[192,512]{1,0:T(8,128)(2,1)S(1)}, bf16[192,512]{1,0:T(8,128)(2,1)S(1)}, u32[]{:S(2)}, u32[]{:S(2)}) collective-permute-start(bf16[192,512]{1,0:T(8,128)(2,1)S(1)} %get-tuple-element.135), channel_id=1, source_target_pairs={{0,0},{1,16},{2,2},{3,18},{4,4},{5,20},{6,6},{7,22},{8,8},{9,24},{... | collective-permute-start | bytes 589832 | tf_op jit(solution)/shard_map/ppermute | solution.py:179
  236.7 2.8 collective-permute-start.27
  242.0 13.1 %attend_back.4 = bf16[192,2048]{1,0:T(8,128)(2,1)S(1)} custom-call(bf16[192,2048]{1,0:T(8,128)(2,1)S(1)} %bitcast.153, bf16[192,2048]{1,0:T(8,128)(2,1)S(1)} %bitcast.141, bf16[3,2048,64]{2,1,0:T(8,128)(2,1)S(1)} %bitcast.147, bf16[3,2048,64]{2,1,0:T(8,128)(2,1)} %bitcast.174, bf16[192,2048]{1,0:T(8,128)(2,1)S(1)} %constant_dynamic-update-slice_fusion.10.up_ref, ...), custom_call_target="tpu_custom_call" | custom-call | flops 15032385536 | bytes 2097152 | tf_op jit(solution)/shard_map/attend_back/pallas_call | solution.py:133
  256.4 13.2 %attend_back.5 = bf16[192,2048]{1,0:T(8,128)(2,1)S(1)} custom-call(bf16[192,2048]{1,0:T(8,128)(2,1)S(1)} %bitcast.154, bf16[192,2048]{1,0:T(8,128)(2,1)S(1)} %bitcast.142, bf16[3,2048,64]{2,1,0:T(8,128)(2,1)S(1)} %bitcast.148, bf16[3,2048,64]{2,1,0:T(8,128)(2,1)} %bitcast.175, bf16[192,2048]{1,0:T(8,128)(2,1)S(1)} %constant_dynamic-update-slice_fusion.10.up_ref, ...), custom_call_target="tpu_custom_call" | custom-call | flops 15032385536 | bytes 2097152 | tf_op jit(solution)/shard_map/attend_back/pallas_call | solution.py:133
  270.6 2.9 collective-permute-start.33
  273.5 2.5 collective-permute-start.32
  276.0 3.4 collective-permute-start.38
  281.6 2.0 convolution_convert_fusion.7
  284.3 11.8 %collective-permute-done.38 = bf16[136,768]{1,0:T(8,128)(2,1)} collective-permute-done((bf16[136,768]{1,0:T(8,128)(2,1)}, bf16[136,768]{1,0:T(8,128)(2,1)}, u32[]{:S(2)}, u32[]{:S(2)}) %collective-permute-start.38) | collective-permute-done | bytes 208928 | tf_op jit(solution)/shard_map/ppermute | solution.py:165
  296.1 4.1 %collective-permute-start.31 = (bf16[384,512]{1,0:T(8,128)(2,1)}, bf16[384,512]{1,0:T(8,128)(2,1)S(1)}, u32[]{:S(2)}, u32[]{:S(2)}) collective-permute-start(bf16[384,512]{1,0:T(8,128)(2,1)} %get-tuple-element.105), channel_id=1, source_target_pairs={{0,8},{1,24},{2,10},{3,26},{4,12},{5,28},{6,14},{7,30},{8,0},{9,16... | collective-permute-start | bytes 1179656 | tf_op jit(solution)/shard_map/ppermute | solution.py:179
  300.2 11.9 %collective-permute-done.37 = bf16[136,768]{1,0:T(8,128)(2,1)} collective-permute-done((bf16[136,768]{1,0:T(8,128)(2,1)}, bf16[136,768]{1,0:T(8,128)(2,1)}, u32[]{:S(2)}, u32[]{:S(2)}) %collective-permute-start.37) | collective-permute-done | bytes 208928 | tf_op jit(solution)/shard_map/ppermute | solution.py:165
  312.1 3.3 collective-permute-start.30
  320.3 7.3 %collective-permute-done.30 = bf16[384,512]{1,0:T(8,128)(2,1)S(1)} collective-permute-done((bf16[384,512]{1,0:T(8,128)(2,1)S(1)}, bf16[384,512]{1,0:T(8,128)(2,1)S(1)}, u32[]{:S(2)}, u32[]{:S(2)}) %collective-permute-start.30) | collective-permute-done | bytes 393248 | tf_op jit(solution)/shard_map/ppermute | solution.py:179
  334.5 4.7 %collective-permute-done.35 = bf16[4,48,576]{2,1,0:T(8,128)(2,1)S(1)} collective-permute-done((bf16[4,48,576]{2,1,0:T(8,128)(2,1)S(1)}, bf16[4,48,576]{2,1,0:T(8,128)(2,1)S(1)}, u32[]{:S(2)}, u32[]{:S(2)}) %collective-permute-start.35) | collective-permute-done | bytes 221216 | tf_op jit(solution)/shard_map/ppermute | solution.py:231
  339.5 3.5 collective-permute-start.39
  346.1 5.1 %collective-permute-done.42 = bf16[2,48,576]{2,1,0:T(8,128)(2,1)S(1)} collective-permute-done((bf16[2,48,576]{2,1,0:T(8,128)(2,1)S(1)}, bf16[2,48,576]{2,1,0:T(8,128)(2,1)S(1)}, u32[]{:S(2)}, u32[]{:S(2)}) %collective-permute-start.42) | collective-permute-done | bytes 110624 | tf_op jit(solution)/shard_map/ppermute | solution.py:231
  351.8 2.9 collective-permute-start.47
  354.7 1.7 collective-permute-done.43
  356.5 3.7 %collective-permute-start.44 = (bf16[2,192,576]{2,1,0:T(8,128)(2,1)S(1)}, bf16[2,192,576]{2,1,0:T(8,128)(2,1)S(1)}, u32[]{:S(2)}, u32[]{:S(2)}) collective-permute-start(bf16[2,192,576]{2,1,0:T(8,128)(2,1)S(1)} %pad_maximum_fusion.19), channel_id=1, source_target_pairs={{0,1},{1,0},{2,3},{3,2},{4,5},{5,4},{6,7},{7,6},{8,9},{9,8},{10,11... | collective-permute-start | bytes 1327112 | tf_op jit(solution)/shard_map/ppermute | solution.py:165
  360.3 1.6 fusion.25
  363.1 1.7 finish_into.1
  365.4 1.5 broadcast_select_fusion.9
  368.1 1.9 finish_rest.1
  (291 shorter events, 75.0 us)
Async XLA Ops:
  2.8 7.3 %collective-permute-start.2 = (bf16[80,768]{1,0:T(8,128)(2,1)S(1)}, bf16[80,768]{1,0:T(8,128)(2,1)S(1)}, u32[]{:S(2)}, u32[]{:S(2)}) collective-permute-start(bf16[80,768]{1,0:T(8,128)(2,1)S(1)} %get-tuple-element.162), channel_id=1, source_target_pairs={{0,24},{8,16},{16,8},{24,0},{1,25},{9,17},{17,9},{25,1},{2,26},{10... | collective-permute-start | bytes 368648 | tf_op jit(solution)/shard_map/ppermute | solution.py:165
  7.0 10.0 %collective-permute-start.1 = (bf16[80,768]{1,0:T(8,128)(2,1)S(1)}, bf16[80,768]{1,0:T(8,128)(2,1)S(1)}, u32[]{:S(2)}, u32[]{:S(2)}) collective-permute-start(bf16[80,768]{1,0:T(8,128)(2,1)S(1)} %get-tuple-element.162), channel_id=1, source_target_pairs={{0,16},{8,24},{16,0},{24,8},{1,17},{9,25},{17,1},{25,9},{2,18},{10... | collective-permute-start | bytes 368648 | tf_op jit(solution)/shard_map/ppermute | solution.py:165
  7.0 10.0 %collective-permute-start = (bf16[80,768]{1,0:T(8,128)(2,1)S(1)}, bf16[80,768]{1,0:T(8,128)(2,1)S(1)}, u32[]{:S(2)}, u32[]{:S(2)}) collective-permute-start(bf16[80,768]{1,0:T(8,128)(2,1)S(1)} %get-tuple-element.162), channel_id=1, source_target_pairs={{0,8},{8,0},{16,24},{24,16},{1,9},{9,1},{17,25},{25,17},{2,10},{10... | collective-permute-start | bytes 368648 | tf_op jit(solution)/shard_map/ppermute | solution.py:165
  17.2 7.5 %collective-permute-start.3 = (bf16[4,72,768]{2,1,0:T(8,128)(2,1)S(1)}, bf16[4,72,768]{2,1,0:T(8,128)(2,1)S(1)}, u32[]{:S(2)}, u32[]{:S(2)}) collective-permute-start(bf16[4,72,768]{2,1,0:T(8,128)(2,1)S(1)} %slice.197), channel_id=1, source_target_pairs={{0,2},{1,5},{2,0},{3,7},{4,6},{5,1},{6,4},{7,3},{8,10},{9,13},{10,... | collective-permute-start | bytes 1327112 | tf_op jit(solution)/shard_map/ppermute | solution.py:231
  24.9 24.5 %collective-permute-start.4 = (bf16[4,144,768]{2,1,0:T(8,128)(2,1)S(1)}, bf16[4,144,768]{2,1,0:T(8,128)(2,1)S(1)}, u32[]{:S(2)}, u32[]{:S(2)}) collective-permute-start(bf16[4,144,768]{2,1,0:T(8,128)(2,1)S(1)} %pad_maximum_fusion.13), channel_id=1, source_target_pairs={{0,4},{1,3},{2,6},{3,1},{4,0},{5,7},{6,2},{7,5},{8,12},{9,11},{10,... | collective-permute-start | bytes 2654216 | tf_op jit(solution)/shard_map/ppermute | solution.py:231
  26.1 20.8 %collective-permute-start.6 = (bf16[512,768]{1,0:T(8,128)(2,1)S(1)}, bf16[512,768]{1,0:T(8,128)(2,1)}, u32[]{:S(2)}, u32[]{:S(2)}) collective-permute-start(bf16[512,768]{1,0:T(8,128)(2,1)S(1)} %bitcast.156), channel_id=1, source_target_pairs={{0,8},{1,16},{2,10},{3,18},{4,12},{5,20},{6,14},{7,22},{8,0},{9,24... | collective-permute-start | bytes 2359304 | tf_op jit(solution)/shard_map/ppermute | solution.py:179
  28.5 20.9 %copy-start.28 = (bf16[1088,768]{1,0:T(8,128)(2,1)}, bf16[1088,768]{1,0:T(8,128)(2,1)S(1)}, u32[]{:S(2)}) copy-start(bf16[1088,768]{1,0:T(8,128)(2,1)S(1)} %constant_dynamic-update-slice_fusion) | copy-start | bytes 5013508
  47.0 13.0 %collective-permute-start.7 = (bf16[512,768]{1,0:T(8,128)(2,1)}, bf16[512,768]{1,0:T(8,128)(2,1)}, u32[]{:S(2)}, u32[]{:S(2)}) collective-permute-start(bf16[512,768]{1,0:T(8,128)(2,1)} %collective-permute-done.6), channel_id=1, source_target_pairs={{1,9},{3,11},{5,13},{7,15},{9,1},{11,3},{13,5},{15,7},{16,24},{18,... | collective-permute-start | bytes 2359304 | tf_op jit(solution)/shard_map/ppermute | solution.py:179
  51.0 11.6 %collective-permute-start.5 = (bf16[4,288,768]{2,1,0:T(8,128)(2,1)}, bf16[4,288,768]{2,1,0:T(8,128)(2,1)}, u32[]{:S(2)}, u32[]{:S(2)}) collective-permute-start(bf16[4,288,768]{2,1,0:T(8,128)(2,1)} %pad_maximum_fusion.8), channel_id=1, source_target_pairs={{0,1},{1,0},{2,3},{3,2},{4,5},{5,4},{6,7},{7,6},{8,9},{9,8},{10,11... | collective-permute-start | bytes 5308424 | tf_op jit(solution)/shard_map/ppermute | solution.py:165
  52.2 15.0 %copy-start.38 = (f32[768]{0:T(1024)}, f32[768]{0:T(1024)S(1)}, u32[]{:S(2)}) copy-start(f32[768]{0:T(1024)S(1)} %reshape.275) | copy-start | bytes 9220
  61.6 4.7 %collective-permute-start.8 = (bf16[1024,768]{1,0:T(8,128)(2,1)S(1)}, bf16[1024,768]{1,0:T(8,128)(2,1)S(1)}, u32[]{:S(2)}, u32[]{:S(2)}) collective-permute-start(bf16[1024,768]{1,0:T(8,128)(2,1)S(1)} %pad_maximum_fusion.10), channel_id=1, source_target_pairs={{0,1},{1,0},{2,3},{3,2},{4,5},{5,4},{6,7},{7,6},{8,9},{9,8},{10,11... | collective-permute-start | bytes 4718600 | tf_op jit(solution)/shard_map/ppermute | solution.py:165
  66.3 12.7 %copy-start.22 = (bf16[4,1,192,768]{3,2,1,0:T(8,128)(2,1)}, bf16[4,1,192,768]{3,2,1,0:T(8,128)(2,1)S(1)}, u32[]{:S(2)}) copy-start(bf16[4,1,192,768]{3,2,1,0:T(8,128)(2,1)S(1)} %get-tuple-element.77) | copy-start | bytes 3538948
  69.5 9.6 %copy-start.17 = (bf16[1024,768]{1,0:T(8,128)(2,1)}, bf16[1024,768]{1,0:T(8,128)(2,1)S(1)}, u32[]{:S(2)}) copy-start(bf16[1024,768]{1,0:T(8,128)(2,1)S(1)} %get-tuple-element.165) | copy-start | bytes 4718596
  73.8 22.5 %collective-permute-start.11 = (bf16[136,768]{1,0:T(8,128)(2,1)}, bf16[136,768]{1,0:T(8,128)(2,1)S(1)}, u32[]{:S(2)}, u32[]{:S(2)}) collective-permute-start(bf16[136,768]{1,0:T(8,128)(2,1)} %constant_dynamic-slice_fusion.21), channel_id=1, source_target_pairs={{0,24},{8,16},{16,8},{24,0},{1,25},{9,17},{17,9},{25,1},{2,26},{10... | collective-permute-start | bytes 626696 | tf_op jit(solution)/shard_map/ppermute | solution.py:165
  78.8 17.7 %collective-permute-start.10 = (bf16[136,768]{1,0:T(8,128)(2,1)}, bf16[136,768]{1,0:T(8,128)(2,1)S(1)}, u32[]{:S(2)}, u32[]{:S(2)}) collective-permute-start(bf16[136,768]{1,0:T(8,128)(2,1)} %constant_dynamic-slice_fusion.21), channel_id=1, source_target_pairs={{0,16},{8,24},{16,0},{24,8},{1,17},{9,25},{17,1},{25,9},{2,18},{10... | collective-permute-start | bytes 626696 | tf_op jit(solution)/shard_map/ppermute | solution.py:165
  78.8 17.7 %collective-permute-start.9 = (bf16[136,768]{1,0:T(8,128)(2,1)}, bf16[136,768]{1,0:T(8,128)(2,1)}, u32[]{:S(2)}, u32[]{:S(2)}) collective-permute-start(bf16[136,768]{1,0:T(8,128)(2,1)} %constant_dynamic-slice_fusion.21), channel_id=1, source_target_pairs={{0,8},{8,0},{16,24},{24,16},{1,9},{9,1},{17,25},{25,17},{2,10},{10... | collective-permute-start | bytes 626696 | tf_op jit(solution)/shard_map/ppermute | solution.py:165
  85.3 25.6 %copy-start.7 = (bf16[192,2048]{1,0:T(8,128)(2,1)}, bf16[192,2048]{1,0:T(8,128)(2,1)S(1)}, u32[]{:S(2)}) copy-start(bf16[192,2048]{1,0:T(8,128)(2,1)S(1)} %convolution_convert_fusion.2.v_ref) | copy-start | bytes 2359300
  97.7 11.7 %collective-permute-start.12 = (bf16[4,136,768]{2,1,0:T(8,128)(2,1)S(1)}, bf16[4,136,768]{2,1,0:T(8,128)(2,1)S(1)}, u32[]{:S(2)}, u32[]{:S(2)}) collective-permute-start(bf16[4,136,768]{2,1,0:T(8,128)(2,1)S(1)} %pad_maximum_fusion.15), channel_id=1, source_target_pairs={{0,2},{1,5},{2,0},{3,7},{4,6},{5,1},{6,4},{7,3},{8,10},{9,13},{10,... | collective-permute-start | bytes 2506760 | tf_op jit(solution)/shard_map/ppermute | solution.py:231
  109.7 20.7 %collective-permute-start.17 = (bf16[4,272,768]{2,1,0:T(8,128)(2,1)S(1)}, bf16[4,272,768]{2,1,0:T(8,128)(2,1)S(1)}, u32[]{:S(2)}, u32[]{:S(2)}) collective-permute-start(bf16[4,272,768]{2,1,0:T(8,128)(2,1)S(1)} %pad_maximum_fusion.9), channel_id=1, source_target_pairs={{0,4},{1,3},{2,6},{3,1},{4,0},{5,7},{6,2},{7,5},{8,12},{9,11},{10,... | collective-permute-start | bytes 5013512 | tf_op jit(solution)/shard_map/ppermute | solution.py:231
  132.5 24.2 %collective-permute-start.18 = (bf16[4,544,768]{2,1,0:T(8,128)(2,1)}, bf16[4,544,768]{2,1,0:T(8,128)(2,1)}, u32[]{:S(2)}, u32[]{:S(2)}) collective-permute-start(bf16[4,544,768]{2,1,0:T(8,128)(2,1)} %pad_maximum_fusion.1), channel_id=1, source_target_pairs={{0,1},{1,0},{2,3},{3,2},{4,5},{5,4},{6,7},{7,6},{8,9},{9,8},{10,11... | collective-permute-start | bytes 10027016 | tf_op jit(solution)/shard_map/ppermute | solution.py:165
  136.6 11.9 %collective-permute-start.13 = (bf16[192,512]{1,0:T(8,128)(2,1)}, bf16[192,512]{1,0:T(8,128)(2,1)}, u32[]{:S(2)}, u32[]{:S(2)}) collective-permute-start(bf16[192,512]{1,0:T(8,128)(2,1)} %get-tuple-element.143), channel_id=1, source_target_pairs={{0,0},{1,16},{2,2},{3,18},{4,4},{5,20},{6,6},{7,22},{8,8},{9,24},{... | collective-permute-start | bytes 589832 | tf_op jit(solution)/shard_map/ppermute | solution.py:179
  140.3 10.7 %collective-permute-start.14 = (bf16[192,512]{1,0:T(8,128)(2,1)}, bf16[192,512]{1,0:T(8,128)(2,1)}, u32[]{:S(2)}, u32[]{:S(2)}) collective-permute-start(bf16[192,512]{1,0:T(8,128)(2,1)} %get-tuple-element.142), channel_id=1, source_target_pairs={{0,8},{1,24},{2,10},{3,26},{4,12},{5,28},{6,14},{7,30},{8,0},{9,16... | collective-permute-start | bytes 589832 | tf_op jit(solution)/shard_map/ppermute | solution.py:179
  142.0 14.7 %collective-permute-start.15 = (bf16[192,512]{1,0:T(8,128)(2,1)S(1)}, bf16[192,512]{1,0:T(8,128)(2,1)S(1)}, u32[]{:S(2)}, u32[]{:S(2)}) collective-permute-start(bf16[192,512]{1,0:T(8,128)(2,1)S(1)} %get-tuple-element.141), channel_id=1, source_target_pairs={{0,16},{1,0},{2,18},{3,2},{4,20},{5,4},{6,22},{7,6},{8,24},{9,8},{... | collective-permute-start | bytes 589832 | tf_op jit(solution)/shard_map/ppermute | solution.py:179
  142.0 14.7 %collective-permute-start.16 = (bf16[192,512]{1,0:T(8,128)(2,1)S(1)}, bf16[192,512]{1,0:T(8,128)(2,1)S(1)}, u32[]{:S(2)}, u32[]{:S(2)}) collective-permute-start(bf16[192,512]{1,0:T(8,128)(2,1)S(1)} %get-tuple-element.140), channel_id=1, source_target_pairs={{0,24},{1,8},{2,26},{3,10},{4,28},{5,12},{6,30},{7,14},{8,16},{9,0... | collective-permute-start | bytes 589832 | tf_op jit(solution)/shard_map/ppermute | solution.py:179
  165.3 12.7 %copy-start.8 = (f32[512,768]{1,0:T(8,128)}, f32[512,768]{1,0:T(8,128)S(1)}, u32[]{:S(2)}) copy-start(f32[512,768]{1,0:T(8,128)S(1)} %get-tuple-element.168) | copy-start | bytes 4718596
  174.8 10.3 %copy-start.21 = (bf16[512,1152]{1,0:T(8,128)(2,1)}, bf16[512,1152]{1,0:T(8,128)(2,1)S(1)}, u32[]{:S(2)}) copy-start(bf16[512,1152]{1,0:T(8,128)(2,1)S(1)} %get-tuple-element.47) | copy-start | bytes 3538948
  190.1 23.3 %collective-permute-start.23 = (bf16[4,544,768]{2,1,0:T(8,128)(2,1)}, bf16[4,544,768]{2,1,0:T(8,128)(2,1)}, u32[]{:S(2)}, u32[]{:S(2)}) collective-permute-start(bf16[4,544,768]{2,1,0:T(8,128)(2,1)} %constant_dynamic-slice_fusion.8), channel_id=1, source_target_pairs={{0,1},{1,0},{2,3},{3,2},{4,5},{5,4},{6,7},{7,6},{8,9},{9,8},{10,11... | collective-permute-start | bytes 10027016 | tf_op jit(solution)/shard_map/ppermute | solution.py:165
  195.6 17.8 %slice-start = ((s8[6684672]{0:T(1024)(128)(4,1)}), s8[4194304]{0:T(1024)(128)(4,1)S(1)}, s32[]{:S(2)}) async-start(s8[6684672]{0:T(1024)(128)(4,1)} %bitcast.160), calls=%async_computation | async-start | bytes 8388608
  197.0 15.1 %collective-permute-start.19 = (bf16[192,512]{1,0:T(8,128)(2,1)S(1)}, bf16[192,512]{1,0:T(8,128)(2,1)S(1)}, u32[]{:S(2)}, u32[]{:S(2)}) collective-permute-start(bf16[192,512]{1,0:T(8,128)(2,1)S(1)} %get-tuple-element.139), channel_id=1, source_target_pairs={{0,0},{1,16},{2,2},{3,18},{4,4},{5,20},{6,6},{7,22},{8,8},{9,24},{... | collective-permute-start | bytes 589832 | tf_op jit(solution)/shard_map/ppermute | solution.py:179
  204.1 8.1 %collective-permute-start.20 = (bf16[192,512]{1,0:T(8,128)(2,1)S(1)}, bf16[192,512]{1,0:T(8,128)(2,1)S(1)}, u32[]{:S(2)}, u32[]{:S(2)}) collective-permute-start(bf16[192,512]{1,0:T(8,128)(2,1)S(1)} %get-tuple-element.138), channel_id=1, source_target_pairs={{0,8},{1,24},{2,10},{3,26},{4,12},{5,28},{6,14},{7,30},{8,0},{9,16... | collective-permute-start | bytes 589832 | tf_op jit(solution)/shard_map/ppermute | solution.py:179
  209.3 4.1 %collective-permute-start.21 = (bf16[192,512]{1,0:T(8,128)(2,1)S(1)}, bf16[192,512]{1,0:T(8,128)(2,1)S(1)}, u32[]{:S(2)}, u32[]{:S(2)}) collective-permute-start(bf16[192,512]{1,0:T(8,128)(2,1)S(1)} %get-tuple-element.137), channel_id=1, source_target_pairs={{0,1},{1,17},{2,3},{3,19},{4,5},{5,21},{6,7},{7,23},{8,9},{9,25},{... | collective-permute-start | bytes 589832 | tf_op jit(solution)/shard_map/ppermute | solution.py:179
  209.3 8.4 %collective-permute-start.22 = (bf16[192,512]{1,0:T(8,128)(2,1)S(1)}, bf16[192,512]{1,0:T(8,128)(2,1)S(1)}, u32[]{:S(2)}, u32[]{:S(2)}) collective-permute-start(bf16[192,512]{1,0:T(8,128)(2,1)S(1)} %get-tuple-element.136), channel_id=1, source_target_pairs={{0,9},{1,25},{2,11},{3,27},{4,13},{5,29},{6,15},{7,31},{8,1},{9,17... | collective-permute-start | bytes 589832 | tf_op jit(solution)/shard_map/ppermute | solution.py:179
  216.5 24.4 %collective-permute-start.25 = (bf16[4,272,768]{2,1,0:T(8,128)(2,1)S(1)}, bf16[4,272,768]{2,1,0:T(8,128)(2,1)S(1)}, u32[]{:S(2)}, u32[]{:S(2)}) collective-permute-start(bf16[4,272,768]{2,1,0:T(8,128)(2,1)S(1)} %constant_dynamic-slice_fusion.7), channel_id=1, source_target_pairs={{0,4},{1,3},{2,6},{3,1},{4,0},{5,7},{6,2},{7,5},{8,12},{9,11},{10,... | collective-permute-start | bytes 5013512 | tf_op jit(solution)/shard_map/ppermute | solution.py:231
  230.9 25.2 %collective-permute-start.24 = (bf16[192,512]{1,0:T(8,128)(2,1)S(1)}, bf16[192,512]{1,0:T(8,128)(2,1)S(1)}, u32[]{:S(2)}, u32[]{:S(2)}) collective-permute-start(bf16[192,512]{1,0:T(8,128)(2,1)S(1)} %get-tuple-element.135), channel_id=1, source_target_pairs={{0,0},{1,16},{2,2},{3,18},{4,4},{5,20},{6,6},{7,22},{8,8},{9,24},{... | collective-permute-start | bytes 589832 | tf_op jit(solution)/shard_map/ppermute | solution.py:179
  236.7 19.5 %collective-permute-start.27 = (bf16[192,512]{1,0:T(8,128)(2,1)S(1)}, bf16[192,512]{1,0:T(8,128)(2,1)S(1)}, u32[]{:S(2)}, u32[]{:S(2)}) collective-permute-start(bf16[192,512]{1,0:T(8,128)(2,1)S(1)} %get-tuple-element.134), channel_id=1, source_target_pairs={{0,8},{1,24},{2,10},{3,26},{4,12},{5,28},{6,14},{7,30},{8,0},{9,16... | collective-permute-start | bytes 589832 | tf_op jit(solution)/shard_map/ppermute | solution.py:179
  239.5 16.7 %collective-permute-start.28 = (bf16[192,512]{1,0:T(8,128)(2,1)S(1)}, bf16[192,512]{1,0:T(8,128)(2,1)S(1)}, u32[]{:S(2)}, u32[]{:S(2)}) collective-permute-start(bf16[192,512]{1,0:T(8,128)(2,1)S(1)} %get-tuple-element.133), channel_id=1, source_target_pairs={{0,16},{1,0},{2,18},{3,2},{4,20},{5,4},{6,22},{7,6},{8,24},{9,8},{... | collective-permute-start | bytes 589832 | tf_op jit(solution)/shard_map/ppermute | solution.py:179
  239.5 16.7 %collective-permute-start.29 = (bf16[192,512]{1,0:T(8,128)(2,1)S(1)}, bf16[192,512]{1,0:T(8,128)(2,1)S(1)}, u32[]{:S(2)}, u32[]{:S(2)}) collective-permute-start(bf16[192,512]{1,0:T(8,128)(2,1)S(1)} %get-tuple-element.132), channel_id=1, source_target_pairs={{0,24},{1,8},{2,26},{3,10},{4,28},{5,12},{6,30},{7,14},{8,16},{9,0... | collective-permute-start | bytes 589832 | tf_op jit(solution)/shard_map/ppermute | solution.py:179
  241.4 13.7 %collective-permute-start.26 = (bf16[4,136,768]{2,1,0:T(8,128)(2,1)S(1)}, bf16[4,136,768]{2,1,0:T(8,128)(2,1)S(1)}, u32[]{:S(2)}, u32[]{:S(2)}) collective-permute-start(bf16[4,136,768]{2,1,0:T(8,128)(2,1)S(1)} %constant_dynamic-slice_fusion.6), channel_id=1, source_target_pairs={{0,2},{1,5},{2,0},{3,7},{4,6},{5,1},{6,4},{7,3},{8,10},{9,13},{10,... | collective-permute-start | bytes 2506760 | tf_op jit(solution)/shard_map/ppermute | solution.py:231
  256.2 13.3 %copy-start.30 = (bf16[192,512]{1,0:T(8,128)(2,1)}, bf16[192,512]{1,0:T(8,128)(2,1)S(1)}, u32[]{:S(2)}) copy-start(bf16[192,512]{1,0:T(8,128)(2,1)S(1)} %collective-permute-done.24) | copy-start | bytes 589828
  256.2 13.3 %copy-start.32 = (bf16[192,512]{1,0:T(8,128)(2,1)}, bf16[192,512]{1,0:T(8,128)(2,1)S(1)}, u32[]{:S(2)}) copy-start(bf16[192,512]{1,0:T(8,128)(2,1)S(1)} %collective-permute-done.27) | copy-start | bytes 589828
  256.2 13.3 %copy-start.34 = (bf16[192,512]{1,0:T(8,128)(2,1)}, bf16[192,512]{1,0:T(8,128)(2,1)S(1)}, u32[]{:S(2)}) copy-start(bf16[192,512]{1,0:T(8,128)(2,1)S(1)} %collective-permute-done.28) | copy-start | bytes 589828
  256.3 13.2 %copy-start.36 = (bf16[192,512]{1,0:T(8,128)(2,1)}, bf16[192,512]{1,0:T(8,128)(2,1)S(1)}, u32[]{:S(2)}) copy-start(bf16[192,512]{1,0:T(8,128)(2,1)S(1)} %collective-permute-done.29) | copy-start | bytes 589828
  270.6 46.6 %collective-permute-start.33 = (bf16[384,512]{1,0:T(8,128)(2,1)}, bf16[384,512]{1,0:T(8,128)(2,1)}, u32[]{:S(2)}, u32[]{:S(2)}) collective-permute-start(bf16[384,512]{1,0:T(8,128)(2,1)} %get-tuple-element.106), channel_id=1, source_target_pairs={{0,24},{1,8},{2,26},{3,10},{4,28},{5,12},{6,30},{7,14},{8,16},{9,0... | collective-permute-start | bytes 1179656 | tf_op jit(solution)/shard_map/ppermute | solution.py:179
  273.5 45.7 %collective-permute-start.32 = (bf16[384,512]{1,0:T(8,128)(2,1)S(1)}, bf16[384,512]{1,0:T(8,128)(2,1)}, u32[]{:S(2)}, u32[]{:S(2)}) collective-permute-start(bf16[384,512]{1,0:T(8,128)(2,1)S(1)} %get-tuple-element.107), channel_id=1, source_target_pairs={{0,16},{1,0},{2,18},{3,2},{4,20},{5,4},{6,22},{7,6},{8,24},{9,8},{... | collective-permute-start | bytes 1179656 | tf_op jit(solution)/shard_map/ppermute | solution.py:179
  276.0 20.1 %collective-permute-start.38 = (bf16[136,768]{1,0:T(8,128)(2,1)}, bf16[136,768]{1,0:T(8,128)(2,1)}, u32[]{:S(2)}, u32[]{:S(2)}) collective-permute-start(bf16[136,768]{1,0:T(8,128)(2,1)} %get-tuple-element.126), channel_id=1, source_target_pairs={{0,24},{8,16},{16,8},{24,0},{1,25},{9,17},{17,9},{25,1},{2,26},{10... | collective-permute-start | bytes 626696 | tf_op jit(solution)/shard_map/ppermute | solution.py:165
  279.4 32.7 %collective-permute-start.37 = (bf16[136,768]{1,0:T(8,128)(2,1)}, bf16[136,768]{1,0:T(8,128)(2,1)}, u32[]{:S(2)}, u32[]{:S(2)}) collective-permute-start(bf16[136,768]{1,0:T(8,128)(2,1)} %get-tuple-element.127), channel_id=1, source_target_pairs={{0,16},{8,24},{16,0},{24,8},{1,17},{9,25},{17,1},{25,9},{2,18},{10... | collective-permute-start | bytes 626696 | tf_op jit(solution)/shard_map/ppermute | solution.py:165
  279.4 36.0 %collective-permute-start.36 = (bf16[136,768]{1,0:T(8,128)(2,1)}, bf16[136,768]{1,0:T(8,128)(2,1)}, u32[]{:S(2)}, u32[]{:S(2)}) collective-permute-start(bf16[136,768]{1,0:T(8,128)(2,1)} %get-tuple-element.125), channel_id=1, source_target_pairs={{0,8},{8,0},{16,24},{24,16},{1,9},{9,1},{17,25},{25,17},{2,10},{10... | collective-permute-start | bytes 626696 | tf_op jit(solution)/shard_map/ppermute | solution.py:165
  284.2 33.9 %copy-start.37 = (bf16[192,512]{1,0:T(8,128)(2,1)S(1)}, bf16[192,512]{1,0:T(8,128)(2,1)}, u32[]{:S(2)}) copy-start(bf16[192,512]{1,0:T(8,128)(2,1)} %copy-done.36) | copy-start | bytes 589828
  284.2 35.0 %copy-start.35 = (bf16[192,512]{1,0:T(8,128)(2,1)S(1)}, bf16[192,512]{1,0:T(8,128)(2,1)}, u32[]{:S(2)}) copy-start(bf16[192,512]{1,0:T(8,128)(2,1)} %copy-done.34) | copy-start | bytes 589828
  284.3 36.0 %copy-start.33 = (bf16[192,512]{1,0:T(8,128)(2,1)S(1)}, bf16[192,512]{1,0:T(8,128)(2,1)}, u32[]{:S(2)}) copy-start(bf16[192,512]{1,0:T(8,128)(2,1)} %copy-done.32) | copy-start | bytes 589828
  296.1 24.2 %collective-permute-start.31 = (bf16[384,512]{1,0:T(8,128)(2,1)}, bf16[384,512]{1,0:T(8,128)(2,1)S(1)}, u32[]{:S(2)}, u32[]{:S(2)}) collective-permute-start(bf16[384,512]{1,0:T(8,128)(2,1)} %get-tuple-element.105), channel_id=1, source_target_pairs={{0,8},{1,24},{2,10},{3,26},{4,12},{5,28},{6,14},{7,30},{8,0},{9,16... | collective-permute-start | bytes 1179656 | tf_op jit(solution)/shard_map/ppermute | solution.py:179
  312.1 15.5 %collective-permute-start.30 = (bf16[384,512]{1,0:T(8,128)(2,1)S(1)}, bf16[384,512]{1,0:T(8,128)(2,1)S(1)}, u32[]{:S(2)}, u32[]{:S(2)}) collective-permute-start(bf16[384,512]{1,0:T(8,128)(2,1)S(1)} %get-tuple-element.104), channel_id=1, source_target_pairs={{0,0},{1,16},{2,2},{3,18},{4,4},{5,20},{6,6},{7,22},{8,8},{9,24},{... | collective-permute-start | bytes 1179656 | tf_op jit(solution)/shard_map/ppermute | solution.py:179
  315.5 18.4 %collective-permute-start.34 = (bf16[4,96,576]{2,1,0:T(8,128)(2,1)S(1)}, bf16[4,96,576]{2,1,0:T(8,128)(2,1)S(1)}, u32[]{:S(2)}, u32[]{:S(2)}) collective-permute-start(bf16[4,96,576]{2,1,0:T(8,128)(2,1)S(1)} %constant_dynamic-slice_fusion.1), channel_id=1, source_target_pairs={{0,4},{1,3},{2,6},{3,1},{4,0},{5,7},{6,2},{7,5},{8,12},{9,11},{10,... | collective-permute-start | bytes 1327112 | tf_op jit(solution)/shard_map/ppermute | solution.py:231
  317.1 10.5 %copy-start.31 = (bf16[192,512]{1,0:T(8,128)(2,1)S(1)}, bf16[192,512]{1,0:T(8,128)(2,1)}, u32[]{:S(2)}) copy-start(bf16[192,512]{1,0:T(8,128)(2,1)} %copy-done.30) | copy-start | bytes 589828
  317.2 17.3 %collective-permute-start.45 = (bf16[1,136,768]{2,1,0:T(8,128)(2,1)S(1)}, bf16[1,136,768]{2,1,0:T(8,128)(2,1)S(1)}, u32[]{:S(2)}, u32[]{:S(2)}) collective-permute-start(bf16[1,136,768]{2,1,0:T(8,128)(2,1)S(1)} %fusion.51), channel_id=1, source_target_pairs={{0,2},{1,5},{2,0},{3,7},{4,6},{5,1},{6,4},{7,3},{8,10},{9,13},{10,... | collective-permute-start | bytes 626696 | tf_op jit(solution)/shard_map/ppermute | solution.py:231
  334.1 5.1 %collective-permute-start.35 = (bf16[4,48,576]{2,1,0:T(8,128)(2,1)S(1)}, bf16[4,48,576]{2,1,0:T(8,128)(2,1)S(1)}, u32[]{:S(2)}, u32[]{:S(2)}) collective-permute-start(bf16[4,48,576]{2,1,0:T(8,128)(2,1)S(1)} %constant_dynamic-slice_fusion), channel_id=1, source_target_pairs={{0,2},{1,5},{2,0},{3,7},{4,6},{5,1},{6,4},{7,3},{8,10},{9,13},{10,... | collective-permute-start | bytes 663560 | tf_op jit(solution)/shard_map/ppermute | solution.py:231
  339.3 5.0 %collective-permute-start.41 = (bf16[48,576]{1,0:T(8,128)(2,1)S(1)}, bf16[48,576]{1,0:T(8,128)(2,1)S(1)}, u32[]{:S(2)}, u32[]{:S(2)}) collective-permute-start(bf16[48,576]{1,0:T(8,128)(2,1)S(1)} %get-tuple-element.159), channel_id=1, source_target_pairs={{0,24},{8,16},{16,8},{24,0},{1,25},{9,17},{17,9},{25,1},{2,26},{10... | collective-permute-start | bytes 165896 | tf_op jit(solution)/shard_map/ppermute | solution.py:165
  339.4 4.9 %collective-permute-start.40 = (bf16[48,576]{1,0:T(8,128)(2,1)S(1)}, bf16[48,576]{1,0:T(8,128)(2,1)S(1)}, u32[]{:S(2)}, u32[]{:S(2)}) collective-permute-start(bf16[48,576]{1,0:T(8,128)(2,1)S(1)} %get-tuple-element.160), channel_id=1, source_target_pairs={{0,8},{8,0},{16,24},{24,16},{1,9},{9,1},{17,25},{25,17},{2,10},{10... | collective-permute-start | bytes 165896 | tf_op jit(solution)/shard_map/ppermute | solution.py:165
  339.5 6.2 %collective-permute-start.39 = (bf16[48,576]{1,0:T(8,128)(2,1)S(1)}, bf16[48,576]{1,0:T(8,128)(2,1)S(1)}, u32[]{:S(2)}, u32[]{:S(2)}) collective-permute-start(bf16[48,576]{1,0:T(8,128)(2,1)S(1)} %get-tuple-element.158), channel_id=1, source_target_pairs={{0,16},{8,24},{16,0},{24,8},{1,17},{9,25},{17,1},{25,9},{2,18},{10... | collective-permute-start | bytes 165896 | tf_op jit(solution)/shard_map/ppermute | solution.py:165
  342.9 8.7 %collective-permute-start.46 = (bf16[1,272,768]{2,1,0:T(8,128)(2,1)S(1)}, bf16[1,272,768]{2,1,0:T(8,128)(2,1)S(1)}, u32[]{:S(2)}, u32[]{:S(2)}) collective-permute-start(bf16[1,272,768]{2,1,0:T(8,128)(2,1)S(1)} %pad_maximum_fusion.20), channel_id=1, source_target_pairs={{0,4},{1,3},{2,6},{3,1},{4,0},{5,7},{6,2},{7,5},{8,12},{9,11},{10,... | collective-permute-start | bytes 1253384 | tf_op jit(solution)/shard_map/ppermute | solution.py:231
  345.8 5.4 %collective-permute-start.42 = (bf16[2,48,576]{2,1,0:T(8,128)(2,1)S(1)}, bf16[2,48,576]{2,1,0:T(8,128)(2,1)S(1)}, u32[]{:S(2)}, u32[]{:S(2)}) collective-permute-start(bf16[2,48,576]{2,1,0:T(8,128)(2,1)S(1)} %pad_maximum_fusion.23), channel_id=1, source_target_pairs={{0,2},{1,5},{2,0},{3,7},{4,6},{5,1},{6,4},{7,3},{8,10},{9,13},{10,... | collective-permute-start | bytes 331784 | tf_op jit(solution)/shard_map/ppermute | solution.py:231
  351.3 5.1 %collective-permute-start.43 = (bf16[2,96,576]{2,1,0:T(8,128)(2,1)S(1)}, bf16[2,96,576]{2,1,0:T(8,128)(2,1)S(1)}, u32[]{:S(2)}, u32[]{:S(2)}) collective-permute-start(bf16[2,96,576]{2,1,0:T(8,128)(2,1)S(1)} %pad_maximum_fusion.22), channel_id=1, source_target_pairs={{0,4},{1,3},{2,6},{3,1},{4,0},{5,7},{6,2},{7,5},{8,12},{9,11},{10,... | collective-permute-start | bytes 663560 | tf_op jit(solution)/shard_map/ppermute | solution.py:231
  351.8 13.6 %collective-permute-start.47 = (bf16[1,544,768]{2,1,0:T(8,128)(2,1)S(1)}, bf16[1,544,768]{2,1,0:T(8,128)(2,1)}, u32[]{:S(2)}, u32[]{:S(2)}) collective-permute-start(bf16[1,544,768]{2,1,0:T(8,128)(2,1)S(1)} %pad_maximum_fusion.16), channel_id=1, source_target_pairs={{0,1},{1,0},{2,3},{3,2},{4,5},{5,4},{6,7},{7,6},{8,9},{9,8},{10,11... | collective-permute-start | bytes 2506760 | tf_op jit(solution)/shard_map/ppermute | solution.py:165
  356.5 5.4 %collective-permute-start.44 = (bf16[2,192,576]{2,1,0:T(8,128)(2,1)S(1)}, bf16[2,192,576]{2,1,0:T(8,128)(2,1)S(1)}, u32[]{:S(2)}, u32[]{:S(2)}) collective-permute-start(bf16[2,192,576]{2,1,0:T(8,128)(2,1)S(1)} %pad_maximum_fusion.19), channel_id=1, source_target_pairs={{0,1},{1,0},{2,3},{3,2},{4,5},{5,4},{6,7},{7,6},{8,9},{9,8},{10,11... | collective-permute-start | bytes 1327112 | tf_op jit(solution)/shard_map/ppermute | solution.py:165
  (28 other events, 80.7 us)
